TPU v7x, 512 devices: a whole 4x4x16 slice. The times are simulated.
512 devices in a mesh: slab: 8 (over y_hi, x), tile: 64 (over z, y_lo, core).
Axes of the slice: x: 4, y: 4 (y_hi: 2, y_lo: 2; y = y_hi * 2 + y_lo), z: 16, core: 2. Of those that a mesh axis runs over, the one named last changes fastest.
Arguments:
- source: float32 [16, 2, 3, 128, 64, 128], P(None, None, None, 'tile', 'slab'), may hold values from -48 to 48
- soil_index: int32 [128, 64, 128], P('tile', 'slab'), may hold values from 0 to 7
- soil_table: float32 [3, 8], replicated, may hold values from 0.5 to 2
- pml_width: int32 [8, 2], P('slab'), may hold values from 1 to 4
- interface_blocks: float32 [128, 8, 2, 384, 384], P('tile', 'slab'), may hold values from -0.25 to 0.25
- inflow: float32 [128, 2, 16, 384], P('tile'), may hold values from -6 to 6
Outputs:
- solution: float32 [16, 2, 3, 128, 64, 128], P(None, None, None, 'tile', 'slab')
- traces: float32 [128, 8, 2, 16, 384], P('tile', 'slab')
All inputs are finite; a program needn't handle non-finite values.
Results may differ from a plain program's by a relative error of at most 0.0001.
Values sent between devices are 32-bit elements; how exact they have to be, the bound alone decides.
No kernel may reach another device: no remote copies, remote signals or barrier semaphores. Data moves between devices by JAX's collectives and lax.ppermute only.
A program may use at most 128 MiB of HBM per device.

v0:
```python
import jax
import jax.numpy as jnp
from jax import lax
from jax.sharding import PartitionSpec as P

ITERS = 3
PATCH = 64


RELAX_WEIGHT = 0.8
SIGMA_PEAK = 3.0
UNIT_STEPS = ((1, 0, 0), (0, 0, 1), (0, 1, 0))


def extended(x, sides, width):
    for axis, dim in sides:
        size, length = (lax.axis_size(axis), x.shape[dim])
        up = [(i, (i + 1) % size) for i in range(size - 1)]
        down = [(j, i) for i, j in up]
        last = lax.slice_in_dim(x, length - width, length, axis=dim)
        first = lax.slice_in_dim(x, 0, width, axis=dim)
        before = lax.ppermute(last, axis, up)
        after = lax.ppermute(first, axis, down)
        x = jnp.concatenate([before, x, after], axis=dim)
    return x


def from_behind(block, axis, distance):
    devices = range(lax.axis_size(axis))
    route = [(i - distance, i) for i in devices if i - distance in devices]
    return lax.ppermute(block, axis, route)


def neighbour(padded, offset, component):
    width_cells = padded.shape[3] - 2
    depth_cells = padded.shape[4] - 2
    length_cells = padded.shape[5] - 2
    return padded[
        :,
        :,
        component,
        1 + offset[0] : 1 + offset[0] + width_cells,
        1 + offset[1] : 1 + offset[1] + depth_cells,
        1 + offset[2] : 1 + offset[2] + length_cells,
    ]


def negate(offset):
    return tuple((-entry for entry in offset))


def joined(first_off, second_off, sign_factor):
    return tuple(
        (
            first_entry + sign_factor * second_entry
            for first_entry, second_entry in zip(first_off, second_off)
        )
    )


def stiffness(padded, shear_mod, lame_first):
    every_comp = slice(None)
    centre = neighbour(padded, (0, 0, 0), every_comp)
    face_sum = neighbour(padded, (1, 0, 0), every_comp) + neighbour(padded, (-1, 0, 0), every_comp)
    face_sum = (
        face_sum
        + neighbour(padded, (0, 1, 0), every_comp)
        + neighbour(padded, (0, -1, 0), every_comp)
    )
    face_sum = (
        face_sum
        + neighbour(padded, (0, 0, 1), every_comp)
        + neighbour(padded, (0, 0, -1), every_comp)
    )
    laplace_term = 6.0 * centre - face_sum
    term_list = []
    for component in range(3):
        own_step = UNIT_STEPS[component]
        own_term = (
            2.0 * centre[:, :, component]
            - neighbour(padded, own_step, component)
            - neighbour(padded, negate(own_step), component)
        )
        for other_dir in range(3):
            if other_dir != component:
                plus_step = joined(own_step, UNIT_STEPS[other_dir], 1)
                minus_step = joined(own_step, UNIT_STEPS[other_dir], -1)
                cross_term = neighbour(padded, plus_step, other_dir) + neighbour(
                    padded, negate(plus_step), other_dir
                )
                cross_term = (
                    cross_term
                    - neighbour(padded, minus_step, other_dir)
                    - neighbour(padded, negate(minus_step), other_dir)
                )
                own_term = own_term - 0.25 * cross_term
        term_list.append(own_term)
    grad_term = jnp.stack(term_list, axis=2)
    return shear_mod * laplace_term + (lame_first + shear_mod) * grad_term


def relax_step(field_now, padded, source_field, coeffs):
    shear_mod, lame_first, mass_term, damp_rate = coeffs
    stiff_part = stiffness(padded, shear_mod, lame_first)
    real_part = field_now[:, 0]
    imag_part = field_now[:, 1]
    res_real = (
        source_field[:, 0] - stiff_part[:, 0] - mass_term * (real_part - damp_rate * imag_part)
    )
    res_imag = (
        source_field[:, 1] - stiff_part[:, 1] - mass_term * (imag_part + damp_rate * real_part)
    )
    diag_real = 6.0 * shear_mod + 2.0 * (lame_first + shear_mod) + mass_term
    diag_imag = mass_term * damp_rate
    step_scale = RELAX_WEIGHT / (diag_real * diag_real + diag_imag * diag_imag)
    new_real = real_part + step_scale * (diag_real * res_real + diag_imag * res_imag)
    new_imag = imag_part + step_scale * (diag_real * res_imag - diag_imag * res_real)
    return jnp.stack([new_real, new_imag], axis=1)


def first_step(source_field, coeffs):
    shear_mod, lame_first, mass_term, damp_rate = coeffs
    diag_real = 6.0 * shear_mod + 2.0 * (lame_first + shear_mod) + mass_term
    diag_imag = mass_term * damp_rate
    step_scale = RELAX_WEIGHT / (diag_real * diag_real + diag_imag * diag_imag)
    real_part = source_field[:, 0]
    imag_part = source_field[:, 1]
    new_real = step_scale * (diag_real * real_part + diag_imag * imag_part)
    new_imag = step_scale * (diag_real * imag_part - diag_imag * real_part)
    return jnp.stack([new_real, new_imag], axis=1)


def soil_lookup(soil_index, soil_table):
    picked_list = []
    for table_row in range(3):
        picked = jnp.zeros(soil_index.shape, jnp.float32)
        for layer_id in range(soil_table.shape[1]):
            picked = picked + jnp.where(
                soil_index == layer_id, soil_table[table_row, layer_id], 0.0
            )
        picked_list.append(picked)
    return (picked_list[0], picked_list[1], picked_list[2])


def damping(widths, depth_cells):
    depth_level = jnp.arange(depth_cells, dtype=jnp.int32)
    upper_damp = jnp.maximum(widths[0] - depth_level, 0).astype(jnp.float32) / widths[0].astype(
        jnp.float32
    )
    lower_damp = jnp.maximum(widths[1] - (depth_cells - 1 - depth_level), 0).astype(
        jnp.float32
    ) / widths[1].astype(jnp.float32)
    return (SIGMA_PEAK * upper_damp * upper_damp + SIGMA_PEAK * lower_damp * lower_damp).reshape(
        1, depth_cells, 1
    )


def pack_plane(plane_field, patch_cells):
    shot_count, _, _, width_cells, length_cells = plane_field.shape
    block_count = length_cells // patch_cells
    grouped = plane_field.reshape(shot_count, 2, 3, width_cells, block_count, patch_cells)
    return grouped.transpose(3, 4, 0, 1, 2, 5).reshape(
        width_cells, block_count, shot_count, 6 * patch_cells
    )


def unpack_plane(vectors, patch_cells):
    width_cells, block_count, shot_count, _ = vectors.shape
    grouped = vectors.reshape(width_cells, block_count, shot_count, 2, 3, patch_cells)
    return grouped.transpose(2, 3, 4, 0, 1, 5).reshape(
        shot_count, 2, 3, width_cells, block_count * patch_cells
    )


def apply_blocks(vectors, blocks):
    return jnp.einsum("xpri,xpio->xpro", vectors, blocks, precision=lax.Precision.HIGHEST)


def per_device(source, soil_index, soil_table, pml_width, interface_blocks, inflow):
    depth_cells = source.shape[4]
    shear_mod, lame_first, mass_term = soil_lookup(soil_index, soil_table)
    damp_rate = damping(pml_width[0], depth_cells)
    blocks = interface_blocks[:, 0]
    coeffs_used = (shear_mod, lame_first, mass_term, damp_rate)

    def solve_local(source_field, coeffs):
        field_now = first_step(source_field, coeffs)
        for sweep_step in range(ITERS - 1):
            rimmed = extended(field_now, (("tile", 3),), 1)
            padded = jnp.pad(rimmed, ((0, 0), (0, 0), (0, 0), (0, 0), (1, 1), (1, 1)))
            field_now = relax_step(field_now, padded, source_field, coeffs)
        return field_now

    local_field = solve_local(source, coeffs_used)
    bottom = pack_plane(local_field[:, :, :, :, depth_cells - 1, :], PATCH)

    def hop(hop_index, state_pair):
        trace_now, incoming = state_pair
        arrived = from_behind(trace_now, "slab", 1)
        incoming = jnp.where(lax.axis_index("slab") == 0, inflow, arrived)
        trace_now = apply_blocks(incoming, blocks) + bottom
        return (trace_now, incoming)

    zero_trace = jnp.zeros_like(bottom)
    trace_now, incoming = lax.fori_loop(0, lax.axis_size("slab"), hop, (zero_trace, zero_trace))
    injection = shear_mod[:, 0, :] * unpack_plane(incoming, PATCH)
    injected = source.at[:, :, :, :, 0, :].add(injection)
    solution = solve_local(injected, coeffs_used)
    return (solution, trace_now[:, None])


def solution(mesh):
    in_specs = (
        P(None, None, None, "tile", "slab", None),
        P("tile", "slab", None),
        P(),
        P("slab", None),
        P("tile", "slab", None, None, None),
        P("tile", None, None, None),
    )
    out_specs = (P(None, None, None, "tile", "slab", None), P("tile", "slab", None, None, None))
    return jax.shard_map(
        per_device, mesh=mesh, in_specs=in_specs, out_specs=out_specs, check_vma=False
    )
```

profile of v0, /device:TPU:248, one launch (start us, length us, event | category | flops | bytes accessed | tf_op | source)
XLA Modules:
  0.0 219.7 jit_solution(8347773294878200227)
XLA Ops:
  1.8 2.1 fusion.132
  9.8 15.1 %add_divide_fusion = (f32[2,8,128]{2,1,0:T(8,128)S(1)}, f32[2,8,128]{2,1,0:T(8,128)S(1)}, f32[2,8,128]{2,1,0:T(8,128)S(1)}, f32[2,8,128]{2,1,0:T(8,128)S(1)}, f3...) fusion(pred[2,8,128]{2,1,0:T(8,128)(4,1)S(1)} %get-tuple-element.120, f32[]{:T(128)} %bitcast.15, ...), kind=kLoop, calls=%fused_computation.321 | loop fusion | flops 112640 | bytes 65664 | tf_op jit(solution)/shard_map/div | solution.py:125
  25.1 2.1 collective-permute-start.1
  27.2 2.2 %collective-permute-start.2 = (f32[16,2,3,1,8,128]{5,4,3,2,1,0:T(8,128)S(1)}, f32[16,2,3,1,8,128]{5,4,3,2,1,0:T(8,128)S(1)}, u32[]{:S(2)}, u32[]{:S(2)}) collective-permute-start(f32[16,2,3,1,8,128]{5,4,3,2,1,0:T(8,128)S(1)} %get-tuple-element.112), channel_id=1, source_target_pairs={{0,1},{1,2},{2,3},{3,4},{4,5},{5,6},{6,7},{7,8},{8,9},{9,10},{10,1... | collective-permute-start | bytes 1179656 | tf_op jit(solution)/shard_map/ppermute | solution.py:22
  29.4 7.2 %collective-permute-done.1 = f32[16,2,3,1,8,128]{5,4,3,2,1,0:T(8,128)S(1)} collective-permute-done((f32[16,2,3,1,8,128]{5,4,3,2,1,0:T(8,128)S(1)}, f32[16,2,3,1,8,128]{5,4,3,2,1,0:T(8,128)S(1)}, u32[]{:S(2)}, u32[]{:S(2)}) %collective-permute-start.1) | collective-permute-done | bytes 393248 | tf_op jit(solution)/shard_map/ppermute | solution.py:23
  36.7 3.8 %collective-permute-done.2 = f32[16,2,3,1,8,128]{5,4,3,2,1,0:T(8,128)S(1)} collective-permute-done((f32[16,2,3,1,8,128]{5,4,3,2,1,0:T(8,128)S(1)}, f32[16,2,3,1,8,128]{5,4,3,2,1,0:T(8,128)S(1)}, u32[]{:S(2)}, u32[]{:S(2)}) %collective-permute-start.2) | collective-permute-done | bytes 393248 | tf_op jit(solution)/shard_map/ppermute | solution.py:22
  40.5 3.1 %select_maximum_fusion.9 = f32[16,2,3,4,10,130]{5,4,3,2,1,0:T(8,128)S(1)} fusion(f32[16,2,3,1,8,128]{5,4,3,2,1,0:T(8,128)S(1)} %collective-permute-done.1, f32[16,2,3,1,8,128]{5,4,3,2,1,0:T(8,128)S(1)} %collective-permute-done.2, f32[16,1,3,2,8,128]{5,4,3,2,1,0:T(8,128)S(1)} %get-tuple-element.97, f32[16,1,3,2,8,128]{5,4,3,2,1,0:T(8,128)S(1)} %get-tuple-element.96), kind=kLoop, calls=%fused_computation.16 | loop fusion | flops 8985600 | bytes 3569664 | tf_op jit(solution)/shard_map/concatenate | solution.py:24
  48.4 2.4 %collective-permute-start.4 = (f32[16,2,3,1,8,128]{5,4,3,2,1,0:T(8,128)S(1)}, f32[16,2,3,1,8,128]{5,4,3,2,1,0:T(8,128)S(1)}, u32[]{:S(2)}, u32[]{:S(2)}) collective-permute-start(f32[16,2,3,1,8,128]{5,4,3,2,1,0:T(8,128)S(1)} %get-tuple-element.108), channel_id=1, source_target_pairs={{0,1},{1,2},{2,3},{3,4},{4,5},{5,6},{6,7},{7,8},{8,9},{9,10},{10,1... | collective-permute-start | bytes 1179656 | tf_op jit(solution)/shard_map/ppermute | solution.py:22
  51.5 6.5 %collective-permute-done.3 = f32[16,2,3,1,8,128]{5,4,3,2,1,0:T(8,128)S(1)} collective-permute-done((f32[16,2,3,1,8,128]{5,4,3,2,1,0:T(8,128)S(1)}, f32[16,2,3,1,8,128]{5,4,3,2,1,0:T(8,128)S(1)}, u32[]{:S(2)}, u32[]{:S(2)}) %collective-permute-start.3) | collective-permute-done | bytes 393248 | tf_op jit(solution)/shard_map/ppermute | solution.py:23
  59.7 3.1 %select_maximum_fusion.6 = f32[16,2,3,4,10,130]{5,4,3,2,1,0:T(8,128)S(1)} fusion(f32[16,2,3,1,8,128]{5,4,3,2,1,0:T(8,128)S(1)} %collective-permute-done.3, f32[16,2,3,1,8,128]{5,4,3,2,1,0:T(8,128)S(1)} %collective-permute-done.4, f32[16,1,3,2,8,128]{5,4,3,2,1,0:T(8,128)S(1)} %get-tuple-element.93, f32[16,1,3,2,8,128]{5,4,3,2,1,0:T(8,128)S(1)} %get-tuple-element.92), kind=kLoop, calls=%fused_computation.13 | loop fusion | flops 8985600 | bytes 3569664 | tf_op jit(solution)/shard_map/concatenate | solution.py:24
  67.5 104.8 %while.14 = (s32[]{:T(128)}, f32[2,2,16,384]{3,2,1,0:T(8,128)}, f32[2,2,16,384]{3,2,1,0:T(8,128)}, f32[2,2,16,384]{3,2,1,0:T(8,128)}, f32[2,2,384,384]{3,2,1,0:T...) while((s32[]{:T(128)}, f32[2,2,16,384]{3,2,1,0:T(8,128)}, ...), condition=%wide.region_1.2_spmd.clone, body=%wide.region_0.1_spmd.clone.sunk | while | flops 113319944 | bytes 3932381 | solution.py:205
  67.5 3.5 %collective-permute-start = (f32[2,2,16,384]{3,2,1,0:T(8,128)S(1)}, f32[2,2,16,384]{3,2,1,0:T(8,128)S(1)}, u32[]{:S(2)}, u32[]{:S(2)}) collective-permute-start(f32[2,2,16,384]{3,2,1,0:T(8,128)S(1)} %broadcast_select_fusion.4), channel_id=1, source_target_pairs={{0,64},{64,128},{128,192},{192,256},{256,320},{320,384},{384,448},... | collective-permute-start | bytes 294920 | tf_op jit(solution)/shard_map/while/body/eval_jaxpr/ppermute | solution.py:31
  71.0 6.7 %collective-permute-done = f32[2,2,16,384]{3,2,1,0:T(8,128)S(1)} collective-permute-done((f32[2,2,16,384]{3,2,1,0:T(8,128)S(1)}, f32[2,2,16,384]{3,2,1,0:T(8,128)S(1)}, u32[]{:S(2)}, u32[]{:S(2)}) %collective-permute-start) | collective-permute-done | bytes 98336 | tf_op jit(solution)/shard_map/while/body/eval_jaxpr/ppermute | solution.py:31
  82.6 8.2 %collective-permute-done = f32[2,2,16,384]{3,2,1,0:T(8,128)S(1)} collective-permute-done((f32[2,2,16,384]{3,2,1,0:T(8,128)S(1)}, f32[2,2,16,384]{3,2,1,0:T(8,128)S(1)}, u32[]{:S(2)}, u32[]{:S(2)}) %collective-permute-start) | collective-permute-done | bytes 98336 | tf_op jit(solution)/shard_map/while/body/eval_jaxpr/ppermute | solution.py:31
  90.8 2.0 convolution_add_fusion.2
  95.6 8.2 %collective-permute-done = f32[2,2,16,384]{3,2,1,0:T(8,128)S(1)} collective-permute-done((f32[2,2,16,384]{3,2,1,0:T(8,128)S(1)}, f32[2,2,16,384]{3,2,1,0:T(8,128)S(1)}, u32[]{:S(2)}, u32[]{:S(2)}) %collective-permute-start) | collective-permute-done | bytes 98336 | tf_op jit(solution)/shard_map/while/body/eval_jaxpr/ppermute | solution.py:31
  103.8 2.0 convolution_add_fusion.2
  108.7 8.2 %collective-permute-done = f32[2,2,16,384]{3,2,1,0:T(8,128)S(1)} collective-permute-done((f32[2,2,16,384]{3,2,1,0:T(8,128)S(1)}, f32[2,2,16,384]{3,2,1,0:T(8,128)S(1)}, u32[]{:S(2)}, u32[]{:S(2)}) %collective-permute-start) | collective-permute-done | bytes 98336 | tf_op jit(solution)/shard_map/while/body/eval_jaxpr/ppermute | solution.py:31
  121.7 8.2 %collective-permute-done = f32[2,2,16,384]{3,2,1,0:T(8,128)S(1)} collective-permute-done((f32[2,2,16,384]{3,2,1,0:T(8,128)S(1)}, f32[2,2,16,384]{3,2,1,0:T(8,128)S(1)}, u32[]{:S(2)}, u32[]{:S(2)}) %collective-permute-start) | collective-permute-done | bytes 98336 | tf_op jit(solution)/shard_map/while/body/eval_jaxpr/ppermute | solution.py:31
  129.9 2.0 convolution_add_fusion.2
  134.7 8.2 %collective-permute-done = f32[2,2,16,384]{3,2,1,0:T(8,128)S(1)} collective-permute-done((f32[2,2,16,384]{3,2,1,0:T(8,128)S(1)}, f32[2,2,16,384]{3,2,1,0:T(8,128)S(1)}, u32[]{:S(2)}, u32[]{:S(2)}) %collective-permute-start) | collective-permute-done | bytes 98336 | tf_op jit(solution)/shard_map/while/body/eval_jaxpr/ppermute | solution.py:31
  147.7 8.4 %collective-permute-done = f32[2,2,16,384]{3,2,1,0:T(8,128)S(1)} collective-permute-done((f32[2,2,16,384]{3,2,1,0:T(8,128)S(1)}, f32[2,2,16,384]{3,2,1,0:T(8,128)S(1)}, u32[]{:S(2)}, u32[]{:S(2)}) %collective-permute-start) | collective-permute-done | bytes 98336 | tf_op jit(solution)/shard_map/while/body/eval_jaxpr/ppermute | solution.py:31
  161.0 9.3 %collective-permute-done = f32[2,2,16,384]{3,2,1,0:T(8,128)S(1)} collective-permute-done((f32[2,2,16,384]{3,2,1,0:T(8,128)S(1)}, f32[2,2,16,384]{3,2,1,0:T(8,128)S(1)}, u32[]{:S(2)}, u32[]{:S(2)}) %collective-permute-start) | collective-permute-done | bytes 98336 | tf_op jit(solution)/shard_map/while/body/eval_jaxpr/ppermute | solution.py:31
  174.5 4.8 %scatter-add.4 = f32[16,2,3,2,8,128]{5,4,3,2,1,0:T(8,128)S(1)} dynamic-update-slice(f32[16,2,3,2,8,128]{5,4,3,2,1,0:T(8,128)S(1)} %copy-done.2, f32[16,2,3,2,1,128]{5,4,3,2,1,0:T(1,128)S(1)} %copy.14, s32[]{:T(128)} %constant.60.clone.1, s32[]{:T(128)} %constant.60.clone.1, s32[]{:T(128)} %constant.60.clone.1, s32[]{:T(128)} %constant.60.clone.1, s32[]{:T(128)} %constant.60.clone.1, ...) | dynamic-update-slice | bytes 196612 | tf_op jit(solution)/shard_map/scatter-add | solution.py:207
  182.1 2.6 %collective-permute-start.6 = (f32[16,2,3,1,8,128]{5,4,3,2,1,0:T(8,128)S(1)}, f32[16,2,3,1,8,128]{5,4,3,2,1,0:T(8,128)S(1)}, u32[]{:S(2)}, u32[]{:S(2)}) collective-permute-start(f32[16,2,3,1,8,128]{5,4,3,2,1,0:T(8,128)S(1)} %get-tuple-element.104), channel_id=1, source_target_pairs={{0,1},{1,2},{2,3},{3,4},{4,5},{5,6},{6,7},{7,8},{8,9},{9,10},{10,1... | collective-permute-start | bytes 1179656 | tf_op jit(solution)/shard_map/ppermute | solution.py:22
  184.7 5.5 %collective-permute-done.5 = f32[16,2,3,1,8,128]{5,4,3,2,1,0:T(8,128)S(1)} collective-permute-done((f32[16,2,3,1,8,128]{5,4,3,2,1,0:T(8,128)S(1)}, f32[16,2,3,1,8,128]{5,4,3,2,1,0:T(8,128)S(1)}, u32[]{:S(2)}, u32[]{:S(2)}) %collective-permute-start.5) | collective-permute-done | bytes 393248 | tf_op jit(solution)/shard_map/ppermute | solution.py:23
  190.2 3.7 %collective-permute-done.6 = f32[16,2,3,1,8,128]{5,4,3,2,1,0:T(8,128)S(1)} collective-permute-done((f32[16,2,3,1,8,128]{5,4,3,2,1,0:T(8,128)S(1)}, f32[16,2,3,1,8,128]{5,4,3,2,1,0:T(8,128)S(1)}, u32[]{:S(2)}, u32[]{:S(2)}) %collective-permute-start.6) | collective-permute-done | bytes 393248 | tf_op jit(solution)/shard_map/ppermute | solution.py:22
  193.9 3.1 %select_maximum_fusion.3 = f32[16,2,3,4,10,130]{5,4,3,2,1,0:T(8,128)S(1)} fusion(f32[16,2,3,1,8,128]{5,4,3,2,1,0:T(8,128)S(1)} %collective-permute-done.5, f32[16,2,3,1,8,128]{5,4,3,2,1,0:T(8,128)S(1)} %collective-permute-done.6, f32[16,1,3,2,8,128]{5,4,3,2,1,0:T(8,128)S(1)} %get-tuple-element.95, f32[16,1,3,2,8,128]{5,4,3,2,1,0:T(8,128)S(1)} %get-tuple-element.94), kind=kLoop, calls=%fused_computation.10 | loop fusion | flops 8985600 | bytes 3569664 | tf_op jit(solution)/shard_map/concatenate | solution.py:24
  201.7 2.4 %collective-permute-start.8 = (f32[16,2,3,1,8,128]{5,4,3,2,1,0:T(8,128)S(1)}, f32[16,2,3,1,8,128]{5,4,3,2,1,0:T(8,128)S(1)}, u32[]{:S(2)}, u32[]{:S(2)}) collective-permute-start(f32[16,2,3,1,8,128]{5,4,3,2,1,0:T(8,128)S(1)} %get-tuple-element.100), channel_id=1, source_target_pairs={{0,1},{1,2},{2,3},{3,4},{4,5},{5,6},{6,7},{7,8},{8,9},{9,10},{10,1... | collective-permute-start | bytes 1179656 | tf_op jit(solution)/shard_map/ppermute | solution.py:22
  204.1 4.2 %collective-permute-done.7 = f32[16,2,3,1,8,128]{5,4,3,2,1,0:T(8,128)S(1)} collective-permute-done((f32[16,2,3,1,8,128]{5,4,3,2,1,0:T(8,128)S(1)}, f32[16,2,3,1,8,128]{5,4,3,2,1,0:T(8,128)S(1)}, u32[]{:S(2)}, u32[]{:S(2)}) %collective-permute-start.7) | collective-permute-done | bytes 393248 | tf_op jit(solution)/shard_map/ppermute | solution.py:23
  208.4 4.6 %collective-permute-done.8 = f32[16,2,3,1,8,128]{5,4,3,2,1,0:T(8,128)S(1)} collective-permute-done((f32[16,2,3,1,8,128]{5,4,3,2,1,0:T(8,128)S(1)}, f32[16,2,3,1,8,128]{5,4,3,2,1,0:T(8,128)S(1)}, u32[]{:S(2)}, u32[]{:S(2)}) %collective-permute-start.8) | collective-permute-done | bytes 393248 | tf_op jit(solution)/shard_map/ppermute | solution.py:22
  212.9 3.1 %select_maximum_fusion = f32[16,2,3,4,10,130]{5,4,3,2,1,0:T(8,128)S(1)} fusion(f32[16,2,3,1,8,128]{5,4,3,2,1,0:T(8,128)S(1)} %collective-permute-done.7, f32[16,2,3,1,8,128]{5,4,3,2,1,0:T(8,128)S(1)} %collective-permute-done.8, f32[16,1,3,2,8,128]{5,4,3,2,1,0:T(8,128)S(1)} %get-tuple-element.89, f32[16,1,3,2,8,128]{5,4,3,2,1,0:T(8,128)S(1)} %get-tuple-element.88), kind=kLoop, calls=%fused_computation.7 | loop fusion | flops 8985600 | bytes 3569664 | tf_op jit(solution)/shard_map/concatenate | solution.py:24
  (139 shorter events, 60.7 us)
Async XLA Ops:
  1.8 64.7 %copy-start.1 = (f32[16,2,3,2,8,128]{5,4,3,2,1,0:T(8,128)}, f32[16,2,3,2,8,128]{5,4,3,2,1,0:T(8,128)S(1)}, u32[]{:S(2)}) copy-start(f32[16,2,3,2,8,128]{5,4,3,2,1,0:T(8,128)S(1)} %copy.28) | copy-start | bytes 2359300
  9.8 36.2 %copy-start.18 = (f32[8]{0:T(128)}, f32[8]{0:T(128)S(1)}, u32[]{:S(2)}) copy-start(f32[8]{0:T(128)S(1)} %fusion.131) | copy-start | bytes 100
  24.9 20.4 %copy-start.15 = (f32[2,8,128]{2,1,0:T(8,128)}, f32[2,8,128]{2,1,0:T(8,128)S(1)}, u32[]{:S(2)}) copy-start(f32[2,8,128]{2,1,0:T(8,128)S(1)} %get-tuple-element.82) | copy-start | bytes 24580
  24.9 21.2 %copy-start.6 = (f32[2,8,128]{2,1,0:T(8,128)}, f32[2,8,128]{2,1,0:T(8,128)S(1)}, u32[]{:S(2)}) copy-start(f32[2,8,128]{2,1,0:T(8,128)S(1)} %get-tuple-element.84) | copy-start | bytes 24580
  24.9 21.2 %copy-start.12 = (f32[2,8,128]{2,1,0:T(8,128)}, f32[2,8,128]{2,1,0:T(8,128)S(1)}, u32[]{:S(2)}) copy-start(f32[2,8,128]{2,1,0:T(8,128)S(1)} %get-tuple-element.85) | copy-start | bytes 24580
  24.9 26.0 %copy-start.9 = (f32[2,8,128]{2,1,0:T(8,128)}, f32[2,8,128]{2,1,0:T(8,128)S(1)}, u32[]{:S(2)}) copy-start(f32[2,8,128]{2,1,0:T(8,128)S(1)} %get-tuple-element.83) | copy-start | bytes 24580
  25.1 11.6 %collective-permute-start.1 = (f32[16,2,3,1,8,128]{5,4,3,2,1,0:T(8,128)S(1)}, f32[16,2,3,1,8,128]{5,4,3,2,1,0:T(8,128)S(1)}, u32[]{:S(2)}, u32[]{:S(2)}) collective-permute-start(f32[16,2,3,1,8,128]{5,4,3,2,1,0:T(8,128)S(1)} %get-tuple-element.113), channel_id=1, source_target_pairs={{1,0},{2,1},{3,2},{4,3},{5,4},{6,5},{7,6},{8,7},{9,8},{10,9},{11,1... | collective-permute-start | bytes 1179656 | tf_op jit(solution)/shard_map/ppermute | solution.py:23
  27.2 13.3 %collective-permute-start.2 = (f32[16,2,3,1,8,128]{5,4,3,2,1,0:T(8,128)S(1)}, f32[16,2,3,1,8,128]{5,4,3,2,1,0:T(8,128)S(1)}, u32[]{:S(2)}, u32[]{:S(2)}) collective-permute-start(f32[16,2,3,1,8,128]{5,4,3,2,1,0:T(8,128)S(1)} %get-tuple-element.112), channel_id=1, source_target_pairs={{0,1},{1,2},{2,3},{3,4},{4,5},{5,6},{6,7},{7,8},{8,9},{9,10},{10,1... | collective-permute-start | bytes 1179656 | tf_op jit(solution)/shard_map/ppermute | solution.py:22
  46.4 17.9 %copy-start.3 = (f32[16,1,3,2,8,128]{5,4,3,2,1,0:T(8,128)}, f32[16,1,3,2,8,128]{5,4,3,2,1,0:T(8,128)S(1)}, u32[]{:S(2)}) copy-start(f32[16,1,3,2,8,128]{5,4,3,2,1,0:T(8,128)S(1)} %get-tuple-element.93) | copy-start | bytes 1179652
  46.5 11.4 %collective-permute-start.3 = (f32[16,2,3,1,8,128]{5,4,3,2,1,0:T(8,128)S(1)}, f32[16,2,3,1,8,128]{5,4,3,2,1,0:T(8,128)S(1)}, u32[]{:S(2)}, u32[]{:S(2)}) collective-permute-start(f32[16,2,3,1,8,128]{5,4,3,2,1,0:T(8,128)S(1)} %get-tuple-element.109), channel_id=1, source_target_pairs={{1,0},{2,1},{3,2},{4,3},{5,4},{6,5},{7,6},{8,7},{9,8},{10,9},{11,1... | collective-permute-start | bytes 1179656 | tf_op jit(solution)/shard_map/ppermute | solution.py:23
  48.4 11.2 %collective-permute-start.4 = (f32[16,2,3,1,8,128]{5,4,3,2,1,0:T(8,128)S(1)}, f32[16,2,3,1,8,128]{5,4,3,2,1,0:T(8,128)S(1)}, u32[]{:S(2)}, u32[]{:S(2)}) collective-permute-start(f32[16,2,3,1,8,128]{5,4,3,2,1,0:T(8,128)S(1)} %get-tuple-element.108), channel_id=1, source_target_pairs={{0,1},{1,2},{2,3},{3,4},{4,5},{5,6},{6,7},{7,8},{8,9},{9,10},{10,1... | collective-permute-start | bytes 1179656 | tf_op jit(solution)/shard_map/ppermute | solution.py:22
  64.4 2.1 copy-start.7
  64.4 2.1 copy-start.13
  64.4 2.1 copy-start.19
  64.6 2.9 %copy-start = (f32[2,1,2,384,384]{4,3,2,1,0:T(8,128)S(1)}, f32[2,1,2,384,384]{4,3,2,1,0:T(8,128)}, u32[]{:S(2)}) copy-start(f32[2,1,2,384,384]{4,3,2,1,0:T(8,128)} %param.14) | copy-start | bytes 7077892
  67.4 106.2 %slice-start = ((f32[16,2,3,2,8,128]{5,4,3,2,1,0:T(8,128)}), f32[16,2,3,2,1,128]{5,4,3,2,1,0:T(1,128)S(1)}, s32[]{:S(2)}) async-start(f32[16,2,3,2,8,128]{5,4,3,2,1,0:T(8,128)} %copy-done.1), calls=%async_computation | async-start | bytes 196608 | tf_op jit(solution)/shard_map/slice.72
  67.4 107.0 %copy-start.2 = (f32[16,2,3,2,8,128]{5,4,3,2,1,0:T(8,128)S(1)}, f32[16,2,3,2,8,128]{5,4,3,2,1,0:T(8,128)}, u32[]{:S(2)}) copy-start(f32[16,2,3,2,8,128]{5,4,3,2,1,0:T(8,128)} %copy-done.1) | copy-start | bytes 2359300
  67.5 10.3 %collective-permute-start = (f32[2,2,16,384]{3,2,1,0:T(8,128)S(1)}, f32[2,2,16,384]{3,2,1,0:T(8,128)S(1)}, u32[]{:S(2)}, u32[]{:S(2)}) collective-permute-start(f32[2,2,16,384]{3,2,1,0:T(8,128)S(1)} %broadcast_select_fusion.4), channel_id=1, source_target_pairs={{0,64},{64,128},{128,192},{192,256},{256,320},{320,384},{384,448},... | collective-permute-start | bytes 294920 | tf_op jit(solution)/shard_map/while/body/eval_jaxpr/ppermute | solution.py:31
  77.8 2.0 copy-start.5
  80.7 10.1 %collective-permute-start = (f32[2,2,16,384]{3,2,1,0:T(8,128)S(1)}, f32[2,2,16,384]{3,2,1,0:T(8,128)S(1)}, u32[]{:S(2)}, u32[]{:S(2)}) collective-permute-start(f32[2,2,16,384]{3,2,1,0:T(8,128)S(1)} %broadcast_select_fusion.4), channel_id=1, source_target_pairs={{0,64},{64,128},{128,192},{192,256},{256,320},{320,384},{384,448},... | collective-permute-start | bytes 294920 | tf_op jit(solution)/shard_map/while/body/eval_jaxpr/ppermute | solution.py:31
  93.7 10.1 %collective-permute-start = (f32[2,2,16,384]{3,2,1,0:T(8,128)S(1)}, f32[2,2,16,384]{3,2,1,0:T(8,128)S(1)}, u32[]{:S(2)}, u32[]{:S(2)}) collective-permute-start(f32[2,2,16,384]{3,2,1,0:T(8,128)S(1)} %broadcast_select_fusion.4), channel_id=1, source_target_pairs={{0,64},{64,128},{128,192},{192,256},{256,320},{320,384},{384,448},... | collective-permute-start | bytes 294920 | tf_op jit(solution)/shard_map/while/body/eval_jaxpr/ppermute | solution.py:31
  103.8 2.0 copy-start.5
  106.7 10.1 %collective-permute-start = (f32[2,2,16,384]{3,2,1,0:T(8,128)S(1)}, f32[2,2,16,384]{3,2,1,0:T(8,128)S(1)}, u32[]{:S(2)}, u32[]{:S(2)}) collective-permute-start(f32[2,2,16,384]{3,2,1,0:T(8,128)S(1)} %broadcast_select_fusion.4), channel_id=1, source_target_pairs={{0,64},{64,128},{128,192},{192,256},{256,320},{320,384},{384,448},... | collective-permute-start | bytes 294920 | tf_op jit(solution)/shard_map/while/body/eval_jaxpr/ppermute | solution.py:31
  119.8 10.1 %collective-permute-start = (f32[2,2,16,384]{3,2,1,0:T(8,128)S(1)}, f32[2,2,16,384]{3,2,1,0:T(8,128)S(1)}, u32[]{:S(2)}, u32[]{:S(2)}) collective-permute-start(f32[2,2,16,384]{3,2,1,0:T(8,128)S(1)} %broadcast_select_fusion.4), channel_id=1, source_target_pairs={{0,64},{64,128},{128,192},{192,256},{256,320},{320,384},{384,448},... | collective-permute-start | bytes 294920 | tf_op jit(solution)/shard_map/while/body/eval_jaxpr/ppermute | solution.py:31
  132.8 10.1 %collective-permute-start = (f32[2,2,16,384]{3,2,1,0:T(8,128)S(1)}, f32[2,2,16,384]{3,2,1,0:T(8,128)S(1)}, u32[]{:S(2)}, u32[]{:S(2)}) collective-permute-start(f32[2,2,16,384]{3,2,1,0:T(8,128)S(1)} %broadcast_select_fusion.4), channel_id=1, source_target_pairs={{0,64},{64,128},{128,192},{192,256},{256,320},{320,384},{384,448},... | collective-permute-start | bytes 294920 | tf_op jit(solution)/shard_map/while/body/eval_jaxpr/ppermute | solution.py:31
  142.9 2.0 copy-start.5
  145.8 10.3 %collective-permute-start = (f32[2,2,16,384]{3,2,1,0:T(8,128)S(1)}, f32[2,2,16,384]{3,2,1,0:T(8,128)S(1)}, u32[]{:S(2)}, u32[]{:S(2)}) collective-permute-start(f32[2,2,16,384]{3,2,1,0:T(8,128)S(1)} %broadcast_select_fusion.4), channel_id=1, source_target_pairs={{0,64},{64,128},{128,192},{192,256},{256,320},{320,384},{384,448},... | collective-permute-start | bytes 294920 | tf_op jit(solution)/shard_map/while/body/eval_jaxpr/ppermute | solution.py:31
  159.1 11.2 %collective-permute-start = (f32[2,2,16,384]{3,2,1,0:T(8,128)S(1)}, f32[2,2,16,384]{3,2,1,0:T(8,128)S(1)}, u32[]{:S(2)}, u32[]{:S(2)}) collective-permute-start(f32[2,2,16,384]{3,2,1,0:T(8,128)S(1)} %broadcast_select_fusion.4), channel_id=1, source_target_pairs={{0,64},{64,128},{128,192},{192,256},{256,320},{320,384},{384,448},... | collective-permute-start | bytes 294920 | tf_op jit(solution)/shard_map/while/body/eval_jaxpr/ppermute | solution.py:31
  180.1 10.0 %collective-permute-start.5 = (f32[16,2,3,1,8,128]{5,4,3,2,1,0:T(8,128)S(1)}, f32[16,2,3,1,8,128]{5,4,3,2,1,0:T(8,128)S(1)}, u32[]{:S(2)}, u32[]{:S(2)}) collective-permute-start(f32[16,2,3,1,8,128]{5,4,3,2,1,0:T(8,128)S(1)} %get-tuple-element.105), channel_id=1, source_target_pairs={{1,0},{2,1},{3,2},{4,3},{5,4},{6,5},{7,6},{8,7},{9,8},{10,9},{11,1... | collective-permute-start | bytes 1179656 | tf_op jit(solution)/shard_map/ppermute | solution.py:23
  182.1 11.8 %collective-permute-start.6 = (f32[16,2,3,1,8,128]{5,4,3,2,1,0:T(8,128)S(1)}, f32[16,2,3,1,8,128]{5,4,3,2,1,0:T(8,128)S(1)}, u32[]{:S(2)}, u32[]{:S(2)}) collective-permute-start(f32[16,2,3,1,8,128]{5,4,3,2,1,0:T(8,128)S(1)} %get-tuple-element.104), channel_id=1, source_target_pairs={{0,1},{1,2},{2,3},{3,4},{4,5},{5,6},{6,7},{7,8},{8,9},{9,10},{10,1... | collective-permute-start | bytes 1179656 | tf_op jit(solution)/shard_map/ppermute | solution.py:22
  199.8 8.6 %collective-permute-start.7 = (f32[16,2,3,1,8,128]{5,4,3,2,1,0:T(8,128)S(1)}, f32[16,2,3,1,8,128]{5,4,3,2,1,0:T(8,128)S(1)}, u32[]{:S(2)}, u32[]{:S(2)}) collective-permute-start(f32[16,2,3,1,8,128]{5,4,3,2,1,0:T(8,128)S(1)} %get-tuple-element.101), channel_id=1, source_target_pairs={{1,0},{2,1},{3,2},{4,3},{5,4},{6,5},{7,6},{8,7},{9,8},{10,9},{11,1... | collective-permute-start | bytes 1179656 | tf_op jit(solution)/shard_map/ppermute | solution.py:23
  201.7 11.2 %collective-permute-start.8 = (f32[16,2,3,1,8,128]{5,4,3,2,1,0:T(8,128)S(1)}, f32[16,2,3,1,8,128]{5,4,3,2,1,0:T(8,128)S(1)}, u32[]{:S(2)}, u32[]{:S(2)}) collective-permute-start(f32[16,2,3,1,8,128]{5,4,3,2,1,0:T(8,128)S(1)} %get-tuple-element.100), channel_id=1, source_target_pairs={{0,1},{1,2},{2,3},{3,4},{4,5},{5,6},{6,7},{7,8},{8,9},{9,10},{10,1... | collective-permute-start | bytes 1179656 | tf_op jit(solution)/shard_map/ppermute | solution.py:22
  (13 other events, 20.1 us)
where the time goes:
time: 221 us; the launch traced here: 220 us
  waiting for transfers between devices  103 us (47%)
  other arithmetic  50.6 us (23%)
  starting transfers between devices  34.4 us (16%)
  matrix products  15.9 us (7%)
  local copies, waits for them, and re-layouts  13.5 us (6%)
  between operations  2.51 us (1%)
    ppermute x8, waiting for transfers between devices, from_behind(): return lax.ppermute(block, axis, route)  65.3 us
    ppermute x4, waiting for transfers between devices, extended(): after = lax.ppermute(first, axis, down)  23.4 us
    ppermute x8, starting transfers between devices, from_behind(): return lax.ppermute(block, axis, route)  16.9 us
    dot_general x8, matrix products, apply_blocks(): jnp.einsum('xpri,xpio->xpro', vectors, blocks, precision=lax.Precision.HI...  15.9 us
    div x1, other arithmetic, first_step(): step_scale = RELAX_WEIGHT / (diag_real * diag_real + diag_imag * diag_imag)  15.1 us
    ppermute x4, waiting for transfers between devices, extended(): before = lax.ppermute(last, axis, up)  13.8 us
    concatenate x8, other arithmetic, extended(): x = jnp.concatenate([before, x, after], axis=dim)  12.9 us
    ppermute x4, starting transfers between devices, extended(): before = lax.ppermute(last, axis, up)  9.64 us
  transfers between devices with their start and end apart: 16, of which 16 were waited for; matrix products, arithmetic and copies ran while one was open for 0% of the time, Pallas kernels for 0%

commit v1 on v0

v1 whole, which is shorter than its diff:
```python
import functools

import jax
import jax.numpy as jnp
from jax import lax
from jax.experimental import pallas as pl
import jax.experimental.pallas.tpu as pltpu
from jax.sharding import PartitionSpec as P

PATCH = 64
RELAX_WEIGHT = 0.8
SIGMA_PEAK = 3.0
PARTS, COMPS = 2, 3
PC = PARTS * COMPS
WIDTH = 2
HALO = 2
COLS = WIDTH + 2 * HALO
DEEP = 3
COEFFS = 11
WR, WI, A, AB, H, AM, ABM, HM, AP, ABP, HP = range(COEFFS)
VMEM = pl.BlockSpec(memory_space=pltpu.VMEM)
SMEM = pl.BlockSpec(memory_space=pltpu.SMEM)
LIMIT = 24 * 1024 * 1024


def call(body, outs, operands, specs=None, scratch=(), aliases=None, flops=0):
    return pl.pallas_call(
        body,
        out_shape=[jax.ShapeDtypeStruct(shape, dtype) for shape, dtype in outs],
        in_specs=specs or [VMEM] * len(operands),
        out_specs=[VMEM] * len(outs),
        scratch_shapes=list(scratch),
        input_output_aliases=aliases or {},
        compiler_params=pltpu.CompilerParams(vmem_limit_bytes=LIMIT),
        cost_estimate=pl.CostEstimate(flops=flops, bytes_accessed=1 << 20, transcendentals=0),
    )(*operands)


def pack_kernel(shots, depth, src, soil, low, high):
    stride = PC * WIDTH * depth

    def put(target, place, d, col, pc):
        rows = src[pl.ds((pc * WIDTH + col) * depth + d, shots, stride=stride), :]
        target[pl.ds(place * shots, shots), :] = rows

    first_high = depth - DEEP
    for d in range(first_high, depth):
        for col in range(WIDTH):
            for pc in range(PC):
                put(high, ((d - first_high) * WIDTH + col) * PC + pc, d, col, pc)
    high[pl.ds(DEEP * WIDTH * PC * shots, WIDTH * depth), :] = (soil[...] + 1).astype(jnp.float32)
    for d in range(first_high):
        for col in range(WIDTH):
            for pc in range(PC):
                put(low, (d * WIDTH + col) * PC + pc, d, col, pc)


def plus(*terms):
    terms = [t for t in terms if t is not None]
    return functools.reduce(lambda a, b: a + b, terms) if terms else None


def minus(a, b):
    if b is None:
        return a
    return -b if a is None else a - b


def times(c, a):
    return None if a is None else c * a


def coupling(field, coef, x, z):
    def step(c):
        return minus(field(x + 1, z, c), field(x - 1, z, c))

    def dive(col, c):
        return minus(field(col, z + 1, c), field(col, z - 1, c))

    def sides(c):
        return plus(field(x + 1, z, c), field(x - 1, z, c))

    def ends(c):
        return plus(field(x, z + 1, c), field(x, z - 1, c))

    length = 128
    results = []
    for c in range(COMPS):
        own = field(x, z, c)
        if c == 0:
            total = plus(
                times(coef(AB), sides(0)),
                times(coef(A), ends(0)),
                times(coef(H), minus(dive(x + 1, 2), dive(x - 1, 2))),
            )
            cross = step(1)
        elif c == 1:
            total = times(coef(A), plus(sides(1), ends(1)))
            cross = plus(step(0), dive(x, 2))
        else:
            total = plus(
                times(coef(A), sides(2)),
                times(coef(AB), ends(2)),
                times(coef(H), minus(dive(x + 1, 0), dive(x - 1, 0))),
            )
            cross = dive(x, 1)
        before, after = (ABM, ABP) if c == 1 else (AM, AP)
        ahead = plus(times(coef(before), own), times(coef(HM), cross))
        behind = minus(times(coef(after), own), times(coef(HP), cross))
        if ahead is not None:
            total = plus(total, pltpu.roll(ahead, length - 1, 1), pltpu.roll(behind, 1, 1))
        results.append(total)
    return results


def relaxed(field, first, coef, x, z):
    real = coupling(lambda i, k, c: field(i, k, c), coef, x, z)
    imag = coupling(lambda i, k, c: field(i, k, COMPS + c), coef, x, z)
    wr, wi = coef(WR), coef(WI)
    out = []
    for part in range(PARTS):
        for c in range(COMPS):
            pc = part * COMPS + c
            if part == 0:
                update = minus(times(wr, real[c]), times(wi, imag[c]))
            else:
                update = plus(times(wr, imag[c]), times(wi, real[c]))
            out.append(plus(times(1.0 - RELAX_WEIGHT, field(x, z, pc)), first(x, z, pc), update))
    return out


def scaled(fr, fi, coef):
    wr, wi = coef(WR), coef(WI)
    return wr * fr - wi * fi, wr * fi + wi * fr


def memo(fn):
    cache = {}

    def get(*key):
        if key not in cache:
            cache[key] = fn(*key)
        return cache[key]

    return get


def coef_of(coeffs, col, depth, z):
    return memo(lambda j: coeffs[pl.ds((col * COEFFS + j) * depth + z, 1), :])


def rolled_zero(x, shift):
    lane = lax.broadcasted_iota(jnp.int32, x.shape, 1)
    length = x.shape[1]
    if shift == 1:
        return jnp.where(lane == 0, 0.0, pltpu.roll(x, 1, 1))
    return jnp.where(lane == length - 1, 0.0, pltpu.roll(x, length - 1, 1))


def fill_coeffs(coeffs, soils, table, widths, depth, layers):
    shape = soils[0].shape
    level = lax.broadcasted_iota(jnp.int32, shape, 0)
    top, bottom = widths[0, 0], widths[0, 1]
    zero = jnp.zeros(shape, jnp.int32)
    upper = jnp.maximum(top - level, 0).astype(jnp.float32) / (zero + top).astype(jnp.float32)
    lower = jnp.maximum(bottom - (depth - 1 - level), 0).astype(jnp.float32) / (
        zero + bottom
    ).astype(jnp.float32)
    sigma = SIGMA_PEAK * upper * upper + SIGMA_PEAK * lower * lower
    for col, soil in enumerate(soils):
        rows = []
        for row in range(3):
            picked = jnp.zeros(shape, jnp.float32)
            for layer in range(layers):
                picked = jnp.where(soil == layer + 1.0, table[row, layer], picked)
            rows.append(picked)
        shear, lame, kappa = rows
        stiff = lame + shear
        diag_r = 6.0 * shear + 2.0 * stiff + kappa
        diag_i = kappa * sigma
        inside = soil > 0.0
        size = jnp.where(inside, diag_r * diag_r + diag_i * diag_i, 1.0)
        scale = jnp.where(inside, RELAX_WEIGHT / size, 0.0)
        both, quarter = shear + stiff, 0.25 * stiff
        values = {
            WR: scale * diag_r,
            WI: -scale * diag_i,
            A: shear,
            AB: both,
            H: quarter,
            AM: rolled_zero(shear, 1),
            ABM: rolled_zero(both, 1),
            HM: rolled_zero(quarter, 1),
            AP: rolled_zero(shear, -1),
            ABP: rolled_zero(both, -1),
            HP: rolled_zero(quarter, -1),
        }
        for j, value in values.items():
            coeffs[pl.ds((col * COEFFS + j) * depth, depth), :] = value


def tile_of(col):
    return (0, col) if col < HALO else (1, col - HALO) if col < HALO + WIDTH else (2, col - HALO - WIDTH)


def slot(z, col, pc):
    return (z * COLS + col) * PC + pc


def bottom_kernel(shots, depth, layers, own, left, right, table, widths, start, bottom, coeffs, v1, v2):
    tiles = (left, own, right)
    at = DEEP * WIDTH * PC * shots
    soils = []
    for col in range(COLS):
        which, place = tile_of(col)
        soils.append(tiles[which][pl.ds(at + place * depth, depth), :])
    fill_coeffs(coeffs, soils, table, widths, depth, layers)
    base = depth - DEEP

    def block(ref, number):
        return ref.at[pl.ds(number * shots, shots), :]

    for z in range(DEEP):
        for col in range(COLS):
            which, place = tile_of(col)
            coef = coef_of(coeffs, col, depth, base + z)
            for c in range(COMPS):
                fr = block(tiles[which], (z * WIDTH + place) * PC + c)[...]
                fi = block(tiles[which], (z * WIDTH + place) * PC + COMPS + c)[...]
                vr, vi = scaled(fr, fi, coef)
                block(v1, slot(z, col, c))[...] = vr
                block(v1, slot(z, col, COMPS + c))[...] = vi

    def first(x, z, pc):
        return block(v1, slot(z, x, pc))[...] if z < DEEP else None

    def second(x, z, pc):
        return block(v2, slot(z, x, pc))[...] if z < DEEP else None

    for z in range(1, DEEP):
        for x in range(1, COLS - 1):
            got = relaxed(memo(first), first, coef_of(coeffs, x, depth, base + z), x, z)
            for pc in range(PC):
                block(v2, slot(z, x, pc))[...] = got[pc]
    lane = lax.broadcasted_iota(jnp.int32, (shots, 2 * PATCH), 1)
    for x in range(HALO, HALO + WIDTH):
        got = relaxed(memo(second), first, coef_of(coeffs, x, depth, depth - 1), x, DEEP - 1)
        for pair in range(PC // 2):
            even, odd = got[2 * pair], got[2 * pair + 1]
            both = (
                jnp.where(lane < PATCH, even, pltpu.roll(odd, PATCH, 1)),
                jnp.where(lane < PATCH, pltpu.roll(even, PATCH, 1), odd),
            )
            for patch in range(2):
                where = (
                    pl.ds(((x - HALO) * 2 + patch) * shots, shots),
                    pl.ds(pair * 2 * PATCH, 2 * PATCH),
                )
                bottom[where] = both[patch] + start[where]


def full_kernel(shots, depth, coeffs, low, low_l, low_r, high, high_l, high_r, out, v1, v2):
    stride = PC * WIDTH * depth
    lows, highs = (low_l, low, low_r), (high_l, high, high_r)
    plane = COLS * PC * shots

    def at(z, col, pc):
        return pl.ds(pl.multiple_of((z + 1) * plane + (col * PC + pc) * shots, shots), shots)

    for ref in (v1, v2):
        for z in (-1, depth):
            for n in range(COLS * PC):
                ref[pl.ds((z + 1) * plane + n * shots, shots), :] = jnp.zeros((shots, 2 * PATCH), jnp.float32)

    def begin(tiles, shift):
        def run(z, carry):
            for col in range(COLS):
                which, place = tile_of(col)
                coef = coef_of(coeffs, col, depth, z)
                for c in range(COMPS):
                    number = ((z - shift) * WIDTH + place) * PC + c
                    fr = tiles[which][pl.ds(pl.multiple_of(number * shots, shots), shots), :]
                    fi = tiles[which][pl.ds(pl.multiple_of((number + COMPS) * shots, shots), shots), :]
                    vr, vi = scaled(fr, fi, coef)
                    v1[at(z, col, c), :] = vr
                    v1[at(z, col, COMPS + c), :] = vi
            return carry

        return run

    lax.fori_loop(0, depth - DEEP, begin(lows, 0), 0)
    lax.fori_loop(depth - DEEP, depth, begin(highs, depth - DEEP), 0)

    def first(x, z, pc):
        return v1[at(z, x, pc), :]

    def second(x, z, pc):
        return v2[at(z, x, pc), :]

    def middle(z, carry):
        for x in range(1, COLS - 1):
            got = relaxed(first, first, coef_of(coeffs, x, depth, z), x, z)
            for pc in range(PC):
                v2[at(z, x, pc), :] = got[pc]
        return carry

    lax.fori_loop(0, depth, middle, 0)

    def last(z, carry):
        for x in range(HALO, HALO + WIDTH):
            got = relaxed(second, first, coef_of(coeffs, x, depth, z), x, z)
            for pc in range(PC):
                out[pl.ds((pc * WIDTH + x - HALO) * depth + z, shots, stride=stride), :] = got[pc]
        return carry

    lax.fori_loop(0, depth, last, 0)


def inject_kernel(shots, depth, coeffs, own, l0, l1, r0, r1, base, out, v1, v2):
    stride = PC * WIDTH * depth

    def block(ref, number):
        return ref.at[pl.ds(number * shots, shots), :]

    lane = lax.broadcasted_iota(jnp.int32, (shots, 2 * PATCH), 1)
    for col in range(COLS):
        which, place = tile_of(col)
        coef = coef_of(coeffs, col, depth, 0)
        planes = []
        for pair in range(PC // 2):
            halves = []
            for patch in range(2):
                where = (
                    pl.ds((place * 2 + patch) * shots, shots),
                    pl.ds(pair * 2 * PATCH, 2 * PATCH),
                )
                halves.append((l0[where] + l1[where], own[where], r0[where] + r1[where])[which] if which != 1 else own[where])
            planes.append(jnp.where(lane < PATCH, halves[0], pltpu.roll(halves[1], PATCH, 1)))
            planes.append(jnp.where(lane < PATCH, pltpu.roll(halves[0], PATCH, 1), halves[1]))
        shear = coef(A)
        for c in range(COMPS):
            vr, vi = scaled(shear * planes[c], shear * planes[COMPS + c], coef)
            block(v1, slot(0, col, c))[...] = vr
            block(v1, slot(0, col, COMPS + c))[...] = vi

    def first(x, z, pc):
        return block(v1, slot(0, x, pc))[...] if z == 0 else None

    def second(x, z, pc):
        return block(v2, slot(z, x, pc))[...] if 0 <= z < 2 else None

    for z in range(2):
        for x in range(1, COLS - 1):
            got = relaxed(memo(first), first, coef_of(coeffs, x, depth, z), x, z)
            for pc in range(PC):
                block(v2, slot(z, x, pc))[...] = got[pc]
    out[...] = base[...]
    for z in range(3):
        for x in range(HALO, HALO + WIDTH):
            got = relaxed(memo(second), first, coef_of(coeffs, x, depth, z), x, z)
            for pc in range(PC):
                where = (pl.ds((pc * WIDTH + x - HALO) * depth + z, shots, stride=stride), slice(None))
                out[where] = base[where] + got[pc]


def split_kernel(blocks, high, low):
    whole = blocks[...]
    top = whole.astype(jnp.bfloat16)
    high[...] = top
    low[...] = (whole - top.astype(jnp.float32)).astype(jnp.bfloat16)


def product(shots, x, high, low, add, out):
    size = x.shape[1]
    for chain in range(x.shape[0] // shots):
        rows = pl.ds(chain * shots, shots)
        whole = x[rows, :]
        top = whole.astype(jnp.bfloat16)
        rest = (whole - top.astype(jnp.float32)).astype(jnp.bfloat16)
        block = pl.ds(chain * size, size)
        wide = jnp.dot(
            jnp.concatenate([top, rest], axis=0), high[block, :], preferred_element_type=jnp.float32
        )
        thin = jnp.dot(top, low[block, :], preferred_element_type=jnp.float32)
        total = wide[:shots] + wide[shots:] + thin
        out[rows, :] = total if add is None else total + add[rows, :]


def start_kernel(shots, slab, inflow, high, low, out):
    @pl.when(slab[0] == 0)
    def _():
        product(shots, inflow, high, low, None, out)

    @pl.when(slab[0] != 0)
    def _():
        out[...] = jnp.zeros(out.shape, jnp.float32)


def hop_kernel(shots, turn, slab, arrived, high, low, bottom, trace, held, new_trace, new_held):
    @pl.when(slab[0] == turn)
    def _():
        product(shots, arrived, high, low, bottom, new_trace)
        new_held[...] = arrived[...]

    @pl.when(slab[0] != turn)
    def _():
        new_trace[...] = trace[...]
        new_held[...] = held[...]


def per_device(source, soil_index, soil_table, pml_width, interface_blocks, inflow):
    shots, _, _, width, depth, length = source.shape
    layers = soil_table.shape[1]
    size = interface_blocks.shape[-1]
    slabs, tiles = lax.axis_size("slab"), lax.axis_size("tile")
    f32, bf16 = jnp.float32, jnp.bfloat16
    slab = lax.axis_index("slab").astype(jnp.int32).reshape(1)
    chains = width * (length // PATCH)
    low_rows = (depth - DEEP) * width * PC * shots
    high_rows = DEEP * width * PC * shots + width * depth

    def across(x, axes, moves):
        return lax.ppermute(x, axes, moves)

    up = [(t, t + 1) for t in range(tiles - 1)]
    down = [(t + 1, t) for t in range(tiles - 1)]

    def pairs(slab_moves, tile_moves):
        return [(a * tiles + t, b * tiles + u) for a, b in slab_moves for t, u in tile_moves]

    def both(x, moves):
        return lax.ppermute(x, ("slab", "tile"), moves)

    low, high = call(
        functools.partial(pack_kernel, shots, depth),
        [((low_rows, length), f32), ((high_rows, length), f32)],
        [source.reshape(-1, length), soil_index.reshape(-1, length)],
    )
    high_l = across(high, "tile", up)
    high_r = across(high, "tile", down)

    blocks = interface_blocks.reshape(chains * size, size)
    heavy, light = call(split_kernel, [(blocks.shape, bf16)] * 2, [blocks])
    held = inflow.reshape(chains * shots, size)
    row_shape = ((chains * shots, size), f32)
    (start,) = call(
        functools.partial(start_kernel, shots),
        [row_shape],
        [slab, held, heavy, light],
        [SMEM, VMEM, VMEM, VMEM],
    )
    bottom, coeffs = call(
        functools.partial(bottom_kernel, shots, depth, layers),
        [row_shape, ((COLS * COEFFS * depth, length), f32)],
        [high, high_l, high_r, soil_table, pml_width, start],
        [VMEM, VMEM, VMEM, SMEM, SMEM, VMEM],
        [pltpu.VMEM((DEEP * COLS * PC * shots, length), f32)] * 2,
    )

    trace = bottom
    halos = []
    low_l = low_r = solved = None
    for hop in range(slabs - 1):
        arrived = both(trace, pairs([(hop, hop + 1)], [(t, t) for t in range(tiles)]))
        if hop == slabs - 3:
            mine = jnp.where(slab[0] == hop, trace, held)
            moves = [(s, s) for s in range(hop)] + [(hop, hop + 1)]
            halos.append((both(mine, pairs(moves, up)), both(mine, pairs(moves, down))))
        if hop == slabs - 2:
            mine = jnp.where(slab[0] == hop, trace, held)
            moves = [(hop - 1, hop - 1), (hop, hop + 1)]
            halos.append((both(mine, pairs(moves, up)), both(mine, pairs(moves, down))))
        if hop == 1:
            ready, _ = lax.optimization_barrier((low, trace))
            low_l = across(ready, "tile", up)
            low_r = across(ready, "tile", down)
        if hop == slabs // 2:
            lows, _ = lax.optimization_barrier(((low, low_l, low_r), trace))
            (solved,) = call(
                functools.partial(full_kernel, shots, depth),
                [((shots * PC * width * depth, length), f32)],
                [coeffs, *lows, high, high_l, high_r],
                None,
                [pltpu.VMEM(((depth + 2) * COLS * PC * shots, length), f32)] * 2,
                flops=10_000_000,
            )
            arrived, solved = lax.optimization_barrier((arrived, solved))
        trace, held = call(
            functools.partial(hop_kernel, shots, hop + 1),
            [row_shape, row_shape],
            [slab, arrived, heavy, light, bottom, trace, held],
            [SMEM] + [VMEM] * 6,
        )
    (result,) = call(
        functools.partial(inject_kernel, shots, depth),
        [(solved.shape, f32)],
        [coeffs, held, halos[0][0], halos[1][0], halos[0][1], halos[1][1], solved],
        None,
        [pltpu.VMEM((DEEP * COLS * PC * shots, length), f32)] * 2,
    )
    traces = trace.reshape(width, 1, length // PATCH, shots, size)
    return result.reshape(source.shape), traces


def solution(mesh):
    in_specs = (
        P(None, None, None, "tile", "slab", None),
        P("tile", "slab", None),
        P(),
        P("slab", None),
        P("tile", "slab", None, None, None),
        P("tile", None, None, None),
    )
    out_specs = (P(None, None, None, "tile", "slab", None), P("tile", "slab", None, None, None))
    return jax.shard_map(
        per_device, mesh=mesh, in_specs=in_specs, out_specs=out_specs, check_vma=False
    )
```

time: 221 us -> 76.9 us (0.35)
  the two profiles are of different devices: /device:TPU:248 before, /device:TPU:251 now
where the time goes in v1:
time: 76.9 us; the launch traced here: 76.3 us
  starting transfers between devices  29.5 us (38%)
  waiting for transfers between devices  28.7 us (37%)
  Pallas kernels  11.5 us (15%)
  local copies, waits for them, and re-layouts  5.62 us (7%)
  between operations  0.96 us (1%)
    ppermute x11, starting transfers between devices, both(): return lax.ppermute(x, ('slab', 'tile'), moves)  17.8 us
    ppermute x11, waiting for transfers between devices, both(): return lax.ppermute(x, ('slab', 'tile'), moves)  16.9 us
    ppermute x4, waiting for transfers between devices, across(): return lax.ppermute(x, axes, moves)  11.8 us
    ppermute x4, starting transfers between devices, across(): return lax.ppermute(x, axes, moves)  11.7 us
    pallas_call x13, Pallas kernels, call(): pl.pallas_call(body, out_shape=[jax.ShapeDtypeStruct(shape, dtype) for sh...  11.5 us
    unnamed x22, local copies, waits for them, and re-layouts  5.62 us
  transfers between devices with their start and end apart: 15, of which 4 were waited for; matrix products, arithmetic and copies ran while one was open for 0% of the time, Pallas kernels for 8%

profile of v1, /device:TPU:251, one launch (start us, length us, event | category | flops | bytes accessed | tf_op | source)
XLA Modules:
  0.0 76.3 jit_solution(7674531043455814679)
XLA Ops:
  0.6 1.1 %copy-done.4 = f32[16,2,3,2,8,128]{5,4,3,2,1,0:T(8,128)S(1)} copy-done((f32[16,2,3,2,8,128]{5,4,3,2,1,0:T(8,128)S(1)}, f32[16,2,3,2,8,128]{5,4,3,2,1,0:T(8,128)}, u32[]{:S(2)}) %copy-start.4) | copy-done | bytes 786456
  1.8 0.7 copy-done.8
  2.5 1.2 %shard_map.77 = (f32[960,128]{1,0:T(8,128)}, f32[592,128]{1,0:T(8,128)S(1)}) custom-call(f32[1536,128]{1,0:T(8,128)S(1)} %bitcast.10, s32[16,128]{1,0:T(8,128)S(1)} %bitcast.13), custom_call_target="tpu_custom_call" | custom-call | bytes 1048576 | tf_op jit(solution)/shard_map/pallas_call | solution.py:27
  3.7 5.5 %collective-permute-start = (f32[592,128]{1,0:T(8,128)S(1)}, f32[592,128]{1,0:T(8,128)S(1)}, u32[]{:S(2)}, u32[]{:S(2)}) collective-permute-start(f32[592,128]{1,0:T(8,128)S(1)} %get-tuple-element.28.own.high), channel_id=1, source_target_pairs={{0,1},{1,2},{2,3},{3,4},{4,5},{5,6},{6,7},{7,8},{8,9},{9,10},{10,1... | collective-permute-start | bytes 909320 | tf_op jit(solution)/shard_map/ppermute | solution.py:423
  9.2 1.9 %collective-permute-start.1 = (f32[592,128]{1,0:T(8,128)S(1)}, f32[592,128]{1,0:T(8,128)S(1)}, u32[]{:S(2)}, u32[]{:S(2)}) collective-permute-start(f32[592,128]{1,0:T(8,128)S(1)} %get-tuple-element.28.own.high), channel_id=1, source_target_pairs={{1,0},{2,1},{3,2},{4,3},{5,4},{6,5},{7,6},{8,7},{9,8},{10,9},{11,1... | collective-permute-start | bytes 909320 | tf_op jit(solution)/shard_map/ppermute | solution.py:423
  11.1 1.7 %copy-done = f32[2,1,2,384,384]{4,3,2,1,0:T(8,128)S(1)} copy-done((f32[2,1,2,384,384]{4,3,2,1,0:T(8,128)S(1)}, f32[2,1,2,384,384]{4,3,2,1,0:T(8,128)}, u32[]{:S(2)}) %copy-start) | copy-done | bytes 2359320
  12.8 0.4 shard_map.78
  13.2 0.5 copy-done.5
  13.7 5.7 %collective-permute-done.1.right.high_r = f32[592,128]{1,0:T(8,128)S(1)} collective-permute-done((f32[592,128]{1,0:T(8,128)S(1)}, f32[592,128]{1,0:T(8,128)S(1)}, u32[]{:S(2)}, u32[]{:S(2)}) %collective-permute-start.1) | collective-permute-done | bytes 303136 | tf_op jit(solution)/shard_map/ppermute | solution.py:423
  19.4 1.2 %shard_map.80 = (f32[64,384]{1,0:T(8,128)S(1)}, f32[528,128]{1,0:T(8,128)S(1)}) custom-call(f32[592,128]{1,0:T(8,128)S(1)} %get-tuple-element.28.own.high, f32[592,128]{1,0:T(8,128)S(1)} %collective-permute-done.left.high_l, f32[592,128]{1,0:T(8,128)S(1)} %collective-permute-done.1.right.high_r, f32[3,8]{1,0:T(4,128)S(1)} %copy-done.9, ...), custom_call_target="tpu_custom_call" | custom-call | bytes 1048576 | tf_op jit(solution)/shard_map/pallas_call | solution.py:27
  20.6 0.7 collective-permute-start.2
  21.4 1.9 %collective-permute-start.7 = (f32[960,128]{1,0:T(8,128)}, f32[960,128]{1,0:T(8,128)}, u32[]{:S(2)}, u32[]{:S(2)}) collective-permute-start(f32[960,128]{1,0:T(8,128)} %get-tuple-element.42.low), channel_id=1, source_target_pairs={{0,1},{1,2},{2,3},{3,4},{4,5},{5,6},{6,7},{7,8},{8,9},{9,10},{10,1... | collective-permute-start | bytes 1474568 | tf_op jit(solution)/shard_map/ppermute | solution.py:423
  23.3 2.4 %collective-permute-start.8 = (f32[960,128]{1,0:T(8,128)}, f32[960,128]{1,0:T(8,128)}, u32[]{:S(2)}, u32[]{:S(2)}) collective-permute-start(f32[960,128]{1,0:T(8,128)} %get-tuple-element.42.low), channel_id=1, source_target_pairs={{1,0},{2,1},{3,2},{4,3},{5,4},{6,5},{7,6},{8,7},{9,8},{10,9},{11,1... | collective-permute-start | bytes 1474568 | tf_op jit(solution)/shard_map/ppermute | solution.py:423
  25.7 0.7 collective-permute-start.3
  26.4 0.7 collective-permute-start.4
  27.2 0.7 collective-permute-start.5
  27.9 0.6 copy-done.6
  28.5 1.3 %collective-permute-start.6 = (f32[64,384]{1,0:T(8,128)S(1)}, f32[64,384]{1,0:T(8,128)}, u32[]{:S(2)}, u32[]{:S(2)}) collective-permute-start(f32[64,384]{1,0:T(8,128)S(1)} %get-tuple-element.39.trace), channel_id=1, source_target_pairs={{256,320},{257,321},{258,322},{259,323},{260,324},{261,325},{262,3... | collective-permute-start | bytes 294920 | tf_op jit(solution)/shard_map/ppermute | solution.py:432
  29.8 6.0 %collective-permute-done.8.low_r = f32[960,128]{1,0:T(8,128)} collective-permute-done((f32[960,128]{1,0:T(8,128)}, f32[960,128]{1,0:T(8,128)}, u32[]{:S(2)}, u32[]{:S(2)}) %collective-permute-start.8) | collective-permute-done | bytes 491552 | tf_op jit(solution)/shard_map/ppermute | solution.py:423
  35.9 1.0 %copy-done.2 = f32[528,128]{1,0:T(8,128)S(1)} copy-done((f32[528,128]{1,0:T(8,128)S(1)}, f32[528,128]{1,0:T(8,128)}, u32[]{:S(2)}) %copy-start.2) | copy-done | bytes 270360
  36.8 4.8 %shard_map.85.base = f32[1536,128]{1,0:T(8,128)S(1)} custom-call(f32[528,128]{1,0:T(8,128)S(1)} %copy-done.2, f32[960,128]{1,0:T(8,128)} %get-tuple-element.42.low, f32[960,128]{1,0:T(8,128)} %collective-permute-done.7.low_l, f32[960,128]{1,0:T(8,128)} %collective-permute-done.8.low_r, f32[592,128]{1,0:T(8,128)S(1)} %get-tuple-element.28.own.high, ...), custom_call_target="tpu_custom_call" | custom-call | flops 10000000 | bytes 1048576 | tf_op jit(solution)/shard_map/pallas_call | solution.py:27
  41.6 11.5 %collective-permute-done.6.arrived = f32[64,384]{1,0:T(8,128)} collective-permute-done((f32[64,384]{1,0:T(8,128)S(1)}, f32[64,384]{1,0:T(8,128)}, u32[]{:S(2)}, u32[]{:S(2)}) %collective-permute-start.6) | collective-permute-done | bytes 98336 | tf_op jit(solution)/shard_map/ppermute | solution.py:432
  53.1 1.3 %shard_map.86 = (f32[64,384]{1,0:T(8,128)S(1)}, f32[64,384]{1,0:T(8,128)S(1)}) custom-call(s32[1]{0:T(128)} %bitcast.2.slab, f32[64,384]{1,0:T(8,128)} %collective-permute-done.6.arrived, bf16[1536,384]{1,0:T(8,128)(2,1)S(1)} %get-tuple-element.29.high, bf16[1536,384]{1,0:T(8,128)(2,1)S(1)} %get-tuple-element.30.low, ...), custom_call_target="tpu_custom_call" | custom-call | bytes 1048576 | tf_op jit(solution)/shard_map/pallas_call | solution.py:27
  54.4 1.3 %collective-permute-start.9 = (f32[64,384]{1,0:T(8,128)S(1)}, f32[64,384]{1,0:T(8,128)S(1)}, u32[]{:S(2)}, u32[]{:S(2)}) collective-permute-start(f32[64,384]{1,0:T(8,128)S(1)} %get-tuple-element.47.trace), channel_id=1, source_target_pairs={{320,384},{321,385},{322,386},{323,387},{324,388},{325,389},{326,3... | collective-permute-start | bytes 294920 | tf_op jit(solution)/shard_map/ppermute | solution.py:432
  55.8 1.3 %collective-permute-start.11 = (f32[64,384]{1,0:T(8,128)S(1)}, f32[64,384]{1,0:T(8,128)S(1)}, u32[]{:S(2)}, u32[]{:S(2)}) collective-permute-start(f32[64,384]{1,0:T(8,128)S(1)} %broadcast_select_fusion.1), channel_id=1, source_target_pairs={{0,1},{1,2},{2,3},{3,4},{4,5},{5,6},{6,7},{7,8},{8,9},{9,10},{10,1... | collective-permute-start | bytes 294920 | tf_op jit(solution)/shard_map/ppermute | solution.py:432
  57.1 1.3 %collective-permute-start.13 = (f32[64,384]{1,0:T(8,128)S(1)}, f32[64,384]{1,0:T(8,128)S(1)}, u32[]{:S(2)}, u32[]{:S(2)}) collective-permute-start(f32[64,384]{1,0:T(8,128)S(1)} %broadcast_select_fusion.1), channel_id=1, source_target_pairs={{1,0},{2,1},{3,2},{4,3},{5,4},{6,5},{7,6},{8,7},{9,8},{10,9},{11,1... | collective-permute-start | bytes 294920 | tf_op jit(solution)/shard_map/ppermute | solution.py:432
  58.4 0.7 collective-permute-start.10
  59.1 7.4 %collective-permute-start.12 = (f32[64,384]{1,0:T(8,128)S(1)}, f32[64,384]{1,0:T(8,128)S(1)}, u32[]{:S(2)}, u32[]{:S(2)}) collective-permute-start(f32[64,384]{1,0:T(8,128)S(1)} %broadcast_select_fusion), channel_id=1, source_target_pairs={{320,321},{321,322},{322,323},{323,324},{324,325},{325,326},{326,3... | collective-permute-start | bytes 294920 | tf_op jit(solution)/shard_map/ppermute | solution.py:432
  66.5 1.9 %collective-permute-start.14 = (f32[64,384]{1,0:T(8,128)S(1)}, f32[64,384]{1,0:T(8,128)S(1)}, u32[]{:S(2)}, u32[]{:S(2)}) collective-permute-start(f32[64,384]{1,0:T(8,128)S(1)} %broadcast_select_fusion), channel_id=1, source_target_pairs={{321,320},{322,321},{323,322},{324,323},{325,324},{326,325},{327,3... | collective-permute-start | bytes 294920 | tf_op jit(solution)/shard_map/ppermute | solution.py:432
  68.4 0.7 shard_map.88
  69.1 5.4 %collective-permute-done.14.r1 = f32[64,384]{1,0:T(8,128)S(1)} collective-permute-done((f32[64,384]{1,0:T(8,128)S(1)}, f32[64,384]{1,0:T(8,128)S(1)}, u32[]{:S(2)}, u32[]{:S(2)}) %collective-permute-start.14) | collective-permute-done | bytes 98336 | tf_op jit(solution)/shard_map/ppermute | solution.py:432
  74.5 1.8 %shard_map.89 = f32[1536,128]{1,0:T(8,128)} custom-call(f32[528,128]{1,0:T(8,128)S(1)} %copy-done.3, f32[64,384]{1,0:T(8,128)S(1)} %get-tuple-element.51.own, f32[64,384]{1,0:T(8,128)S(1)} %collective-permute-done.11.l0, f32[64,384]{1,0:T(8,128)S(1)} %collective-permute-done.12.l1, f32[64,384]{1,0:T(8,128)S(1)} %collective-permute-done.13.r0, ...), custom_call_target="tpu_custom_call" | custom-call | bytes 1048576 | tf_op jit(solution)/shard_map/pallas_call | solution.py:27
  (35 shorter events, 0.2 us)
Async XLA Ops:
  0.6 1.1 %copy-start.4 = (f32[16,2,3,2,8,128]{5,4,3,2,1,0:T(8,128)S(1)}, f32[16,2,3,2,8,128]{5,4,3,2,1,0:T(8,128)}, u32[]{:S(2)}) copy-start(f32[16,2,3,2,8,128]{5,4,3,2,1,0:T(8,128)} %param.6) | copy-start | bytes 2359300
  1.8 0.7 copy-start.8
  3.7 10.0 %collective-permute-start = (f32[592,128]{1,0:T(8,128)S(1)}, f32[592,128]{1,0:T(8,128)S(1)}, u32[]{:S(2)}, u32[]{:S(2)}) collective-permute-start(f32[592,128]{1,0:T(8,128)S(1)} %get-tuple-element.28.own.high), channel_id=1, source_target_pairs={{0,1},{1,2},{2,3},{3,4},{4,5},{5,6},{6,7},{7,8},{8,9},{9,10},{10,1... | collective-permute-start | bytes 909320 | tf_op jit(solution)/shard_map/ppermute | solution.py:423
  9.2 10.2 %collective-permute-start.1 = (f32[592,128]{1,0:T(8,128)S(1)}, f32[592,128]{1,0:T(8,128)S(1)}, u32[]{:S(2)}, u32[]{:S(2)}) collective-permute-start(f32[592,128]{1,0:T(8,128)S(1)} %get-tuple-element.28.own.high), channel_id=1, source_target_pairs={{1,0},{2,1},{3,2},{4,3},{5,4},{6,5},{7,6},{8,7},{9,8},{10,9},{11,1... | collective-permute-start | bytes 909320 | tf_op jit(solution)/shard_map/ppermute | solution.py:423
  11.1 1.7 %copy-start = (f32[2,1,2,384,384]{4,3,2,1,0:T(8,128)S(1)}, f32[2,1,2,384,384]{4,3,2,1,0:T(8,128)}, u32[]{:S(2)}) copy-start(f32[2,1,2,384,384]{4,3,2,1,0:T(8,128)} %param.10) | copy-start | bytes 7077892
  12.8 0.9 %copy-start.5 = (f32[2,2,16,384]{3,2,1,0:T(8,128)S(1)}, f32[2,2,16,384]{3,2,1,0:T(8,128)}, u32[]{:S(2)}) copy-start(f32[2,2,16,384]{3,2,1,0:T(8,128)} %param.11) | copy-start | bytes 294916
  13.7 5.7 %copy-start.9 = (f32[3,8]{1,0:T(4,128)S(1)}, f32[3,8]{1,0:T(4,128)}, u32[]{:S(2)}) copy-start(f32[3,8]{1,0:T(4,128)} %table.1) | copy-start | bytes 292
  13.7 5.7 %copy-start.10 = (s32[1,2]{1,0:T(1,128)S(1)}, s32[1,2]{1,0:T(1,128)}, u32[]{:S(2)}) copy-start(s32[1,2]{1,0:T(1,128)} %widths.1) | copy-start | bytes 28
  20.6 0.7 copy-start.1
  20.6 0.7 collective-permute-start.2
  21.4 8.5 %collective-permute-start.7 = (f32[960,128]{1,0:T(8,128)}, f32[960,128]{1,0:T(8,128)}, u32[]{:S(2)}, u32[]{:S(2)}) collective-permute-start(f32[960,128]{1,0:T(8,128)} %get-tuple-element.42.low), channel_id=1, source_target_pairs={{0,1},{1,2},{2,3},{3,4},{4,5},{5,6},{6,7},{7,8},{8,9},{9,10},{10,1... | collective-permute-start | bytes 1474568 | tf_op jit(solution)/shard_map/ppermute | solution.py:423
  23.3 12.6 %collective-permute-start.8 = (f32[960,128]{1,0:T(8,128)}, f32[960,128]{1,0:T(8,128)}, u32[]{:S(2)}, u32[]{:S(2)}) collective-permute-start(f32[960,128]{1,0:T(8,128)} %get-tuple-element.42.low), channel_id=1, source_target_pairs={{1,0},{2,1},{3,2},{4,3},{5,4},{6,5},{7,6},{8,7},{9,8},{10,9},{11,1... | collective-permute-start | bytes 1474568 | tf_op jit(solution)/shard_map/ppermute | solution.py:423
  25.7 0.7 collective-permute-start.3
  26.4 0.7 collective-permute-start.4
  27.2 0.7 collective-permute-start.5
  27.9 0.6 copy-start.6
  28.5 24.6 %collective-permute-start.6 = (f32[64,384]{1,0:T(8,128)S(1)}, f32[64,384]{1,0:T(8,128)}, u32[]{:S(2)}, u32[]{:S(2)}) collective-permute-start(f32[64,384]{1,0:T(8,128)S(1)} %get-tuple-element.39.trace), channel_id=1, source_target_pairs={{256,320},{257,321},{258,322},{259,323},{260,324},{261,325},{262,3... | collective-permute-start | bytes 294920 | tf_op jit(solution)/shard_map/ppermute | solution.py:432
  35.9 1.0 %copy-start.2 = (f32[528,128]{1,0:T(8,128)S(1)}, f32[528,128]{1,0:T(8,128)}, u32[]{:S(2)}) copy-start(f32[528,128]{1,0:T(8,128)} %copy-done.1) | copy-start | bytes 811012
  36.8 16.3 %copy-start.7 = (f32[64,384]{1,0:T(8,128)S(1)}, f32[64,384]{1,0:T(8,128)}, u32[]{:S(2)}) copy-start(f32[64,384]{1,0:T(8,128)} %copy-done.6) | copy-start | bytes 294916
  54.4 3.9 %collective-permute-start.9 = (f32[64,384]{1,0:T(8,128)S(1)}, f32[64,384]{1,0:T(8,128)S(1)}, u32[]{:S(2)}, u32[]{:S(2)}) collective-permute-start(f32[64,384]{1,0:T(8,128)S(1)} %get-tuple-element.47.trace), channel_id=1, source_target_pairs={{320,384},{321,385},{322,386},{323,387},{324,388},{325,389},{326,3... | collective-permute-start | bytes 294920 | tf_op jit(solution)/shard_map/ppermute | solution.py:432
  55.8 13.3 %collective-permute-start.11 = (f32[64,384]{1,0:T(8,128)S(1)}, f32[64,384]{1,0:T(8,128)S(1)}, u32[]{:S(2)}, u32[]{:S(2)}) collective-permute-start(f32[64,384]{1,0:T(8,128)S(1)} %broadcast_select_fusion.1), channel_id=1, source_target_pairs={{0,1},{1,2},{2,3},{3,4},{4,5},{5,6},{6,7},{7,8},{8,9},{9,10},{10,1... | collective-permute-start | bytes 294920 | tf_op jit(solution)/shard_map/ppermute | solution.py:432
  57.1 12.0 %collective-permute-start.13 = (f32[64,384]{1,0:T(8,128)S(1)}, f32[64,384]{1,0:T(8,128)S(1)}, u32[]{:S(2)}, u32[]{:S(2)}) collective-permute-start(f32[64,384]{1,0:T(8,128)S(1)} %broadcast_select_fusion.1), channel_id=1, source_target_pairs={{1,0},{2,1},{3,2},{4,3},{5,4},{6,5},{7,6},{8,7},{9,8},{10,9},{11,1... | collective-permute-start | bytes 294920 | tf_op jit(solution)/shard_map/ppermute | solution.py:432
  58.4 10.0 %collective-permute-start.10 = (f32[64,384]{1,0:T(8,128)S(1)}, f32[64,384]{1,0:T(8,128)S(1)}, u32[]{:S(2)}, u32[]{:S(2)}) collective-permute-start(f32[64,384]{1,0:T(8,128)S(1)} %get-tuple-element.49.trace), channel_id=1, source_target_pairs={{384,448},{385,449},{386,450},{387,451},{388,452},{389,453},{390,4... | collective-permute-start | bytes 294920 | tf_op jit(solution)/shard_map/ppermute | solution.py:432
  59.1 15.4 %copy-start.3 = (f32[528,128]{1,0:T(8,128)S(1)}, f32[528,128]{1,0:T(8,128)}, u32[]{:S(2)}) copy-start(f32[528,128]{1,0:T(8,128)} %copy-done.1) | copy-start | bytes 811012
  59.1 10.0 %collective-permute-start.12 = (f32[64,384]{1,0:T(8,128)S(1)}, f32[64,384]{1,0:T(8,128)S(1)}, u32[]{:S(2)}, u32[]{:S(2)}) collective-permute-start(f32[64,384]{1,0:T(8,128)S(1)} %broadcast_select_fusion), channel_id=1, source_target_pairs={{320,321},{321,322},{322,323},{323,324},{324,325},{325,326},{326,3... | collective-permute-start | bytes 294920 | tf_op jit(solution)/shard_map/ppermute | solution.py:432
  66.5 8.0 %collective-permute-start.14 = (f32[64,384]{1,0:T(8,128)S(1)}, f32[64,384]{1,0:T(8,128)S(1)}, u32[]{:S(2)}, u32[]{:S(2)}) collective-permute-start(f32[64,384]{1,0:T(8,128)S(1)} %broadcast_select_fusion), channel_id=1, source_target_pairs={{321,320},{322,321},{323,322},{324,323},{325,324},{326,325},{327,3... | collective-permute-start | bytes 294920 | tf_op jit(solution)/shard_map/ppermute | solution.py:432

commit v2 on v1

--- a/solution.py
+++ b/solution.py
@@ -20,39 +20,54 @@
 WR, WI, A, AB, H, AM, ABM, HM, AP, ABP, HP = range(COEFFS)
 VMEM = pl.BlockSpec(memory_space=pltpu.VMEM)
 SMEM = pl.BlockSpec(memory_space=pltpu.SMEM)
-LIMIT = 24 * 1024 * 1024
-
-
-def call(body, outs, operands, specs=None, scratch=(), aliases=None, flops=0):
+ANY = pl.BlockSpec(memory_space=pl.ANY)
+MIB = 1024 * 1024
+LIMIT = 6 * MIB
+HOP_COST = 2_000_000_000
+FULL_COST = 5_000_000_000
+
+
+def call(name, body, outs, operands, specs=None, scratch=(), flops=0, limit=LIMIT):
     return pl.pallas_call(
         body,
+        name=name,
         out_shape=[jax.ShapeDtypeStruct(shape, dtype) for shape, dtype in outs],
         in_specs=specs or [VMEM] * len(operands),
         out_specs=[VMEM] * len(outs),
         scratch_shapes=list(scratch),
-        input_output_aliases=aliases or {},
-        compiler_params=pltpu.CompilerParams(vmem_limit_bytes=LIMIT),
+        compiler_params=pltpu.CompilerParams(vmem_limit_bytes=limit),
         cost_estimate=pl.CostEstimate(flops=flops, bytes_accessed=1 << 20, transcendentals=0),
     )(*operands)
 
 
-def pack_kernel(shots, depth, src, soil, low, high):
+def put(src, target, shots, depth, d, col, pc, place):
     stride = PC * WIDTH * depth
-
-    def put(target, place, d, col, pc):
-        rows = src[pl.ds((pc * WIDTH + col) * depth + d, shots, stride=stride), :]
-        target[pl.ds(place * shots, shots), :] = rows
-
-    first_high = depth - DEEP
-    for d in range(first_high, depth):
+    rows = src[pl.ds((pc * WIDTH + col) * depth + d, shots, stride=stride), :]
+    target[pl.ds(((place * WIDTH + col) * PC + pc) * shots, shots), :] = rows
+
+
+def pack_high_kernel(shots, depth, src_hbm, soil_hbm, high, src, soil, sems):
+    copies = (
+        pltpu.make_async_copy(src_hbm, src, sems.at[0]),
+        pltpu.make_async_copy(soil_hbm, soil, sems.at[1]),
+    )
+    for copy in copies:
+        copy.start()
+    for copy in copies:
+        copy.wait()
+    for place in range(DEEP):
         for col in range(WIDTH):
             for pc in range(PC):
-                put(high, ((d - first_high) * WIDTH + col) * PC + pc, d, col, pc)
-    high[pl.ds(DEEP * WIDTH * PC * shots, WIDTH * depth), :] = (soil[...] + 1).astype(jnp.float32)
-    for d in range(first_high):
+                put(src, high, shots, depth, depth - DEEP + place, col, pc, place)
+    tail = pl.ds(DEEP * WIDTH * PC * shots, WIDTH * depth)
+    high[tail, :] = (soil[...] + 1).astype(jnp.float32)
+
+
+def pack_low_kernel(shots, depth, src, low):
+    for d in range(depth - DEEP):
         for col in range(WIDTH):
             for pc in range(PC):
-                put(low, (d * WIDTH + col) * PC + pc, d, col, pc)
+                put(src, low, shots, depth, d, col, pc, d)
 
 
 def plus(*terms):
@@ -200,7 +215,11 @@
 
 
 def tile_of(col):
-    return (0, col) if col < HALO else (1, col - HALO) if col < HALO + WIDTH else (2, col - HALO - WIDTH)
+    if col < HALO:
+        return 0, col
+    if col < HALO + WIDTH:
+        return 1, col - HALO
+    return 2, col - HALO - WIDTH
 
 
 def slot(z, col, pc):
@@ -316,7 +335,10 @@
     lax.fori_loop(0, depth, last, 0)
 
 
-def inject_kernel(shots, depth, coeffs, own, l0, l1, r0, r1, base, out, v1, v2):
+def inject_kernel(shots, depth, coeffs, own, base, *refs):
+    *halos, out, v1, v2 = refs
+    half = len(halos) // 2
+    sources = (halos[:half], [own], halos[half:])
     stride = PC * WIDTH * depth
 
     def block(ref, number):
@@ -334,7 +356,7 @@
                     pl.ds((place * 2 + patch) * shots, shots),
                     pl.ds(pair * 2 * PATCH, 2 * PATCH),
                 )
-                halves.append((l0[where] + l1[where], own[where], r0[where] + r1[where])[which] if which != 1 else own[where])
+                halves.append(plus(*[ref[where] for ref in sources[which]]))
             planes.append(jnp.where(lane < PATCH, halves[0], pltpu.roll(halves[1], PATCH, 1)))
             planes.append(jnp.where(lane < PATCH, pltpu.roll(halves[0], PATCH, 1), halves[1]))
         shear = coef(A)
@@ -386,26 +408,47 @@
         out[rows, :] = total if add is None else total + add[rows, :]
 
 
-def start_kernel(shots, slab, inflow, high, low, out):
-    @pl.when(slab[0] == 0)
+def start_kernel(shots, inflow, high, low, out):
+    slab = lax.axis_index("slab")
+
+    @pl.when(slab == 0)
     def _():
         product(shots, inflow, high, low, None, out)
 
-    @pl.when(slab[0] != 0)
+    @pl.when(slab != 0)
     def _():
         out[...] = jnp.zeros(out.shape, jnp.float32)
 
 
-def hop_kernel(shots, turn, slab, arrived, high, low, bottom, trace, held, new_trace, new_held):
-    @pl.when(slab[0] == turn)
+def hop_kernel(shots, turn, mixed, arrived, high, low, bottom, trace, held, *refs):
+    slab = lax.axis_index("slab")
+    half = max(len(refs) - 4, 0) // 2
+    sides, (new_trace, new_held, *others) = refs[: 2 * half], refs[2 * half :]
+
+    @pl.when(slab == turn)
     def _():
         product(shots, arrived, high, low, bottom, new_trace)
         new_held[...] = arrived[...]
 
-    @pl.when(slab[0] != turn)
+    @pl.when(slab != turn)
     def _():
         new_trace[...] = trace[...]
         new_held[...] = held[...]
+
+    if mixed:
+        (mine,) = others
+
+        @pl.when(slab == turn)
+        def _():
+            mine[...] = new_trace[...]
+
+        @pl.when(slab != turn)
+        def _():
+            mine[...] = held[...]
+
+    else:
+        for number, ref in enumerate(others):
+            ref[...] = plus(*[side[...] for side in sides[number * half : (number + 1) * half]])
 
 
 def per_device(source, soil_index, soil_table, pml_width, interface_blocks, inflow):
@@ -414,7 +457,6 @@
     size = interface_blocks.shape[-1]
     slabs, tiles = lax.axis_size("slab"), lax.axis_size("tile")
     f32, bf16 = jnp.float32, jnp.bfloat16
-    slab = lax.axis_index("slab").astype(jnp.int32).reshape(1)
     chains = width * (length // PATCH)
     low_rows = (depth - DEEP) * width * PC * shots
     high_rows = DEEP * width * PC * shots + width * depth
@@ -431,25 +473,34 @@
     def both(x, moves):
         return lax.ppermute(x, ("slab", "tile"), moves)
 
-    low, high = call(
-        functools.partial(pack_kernel, shots, depth),
-        [((low_rows, length), f32), ((high_rows, length), f32)],
-        [source.reshape(-1, length), soil_index.reshape(-1, length)],
+    src, soil = source.reshape(-1, length), soil_index.reshape(-1, length)
+    (high,) = call(
+        "pack_high",
+        functools.partial(pack_high_kernel, shots, depth),
+        [((high_rows, length), f32)],
+        [pltpu.with_memory_space_constraint(x, pltpu.HBM) for x in (src, soil)],
+        [ANY, ANY],
+        [
+            pltpu.VMEM(src.shape, f32),
+            pltpu.VMEM(soil.shape, jnp.int32),
+            pltpu.SemaphoreType.DMA((2,)),
+        ],
     )
     high_l = across(high, "tile", up)
     high_r = across(high, "tile", down)
 
     blocks = interface_blocks.reshape(chains * size, size)
-    heavy, light = call(split_kernel, [(blocks.shape, bf16)] * 2, [blocks])
+    heavy, light = call("split", split_kernel, [(blocks.shape, bf16)] * 2, [blocks])
     held = inflow.reshape(chains * shots, size)
     row_shape = ((chains * shots, size), f32)
     (start,) = call(
+        "start",
         functools.partial(start_kernel, shots),
         [row_shape],
-        [slab, held, heavy, light],
-        [SMEM, VMEM, VMEM, VMEM],
+        [held, heavy, light],
     )
     bottom, coeffs = call(
+        "bottom",
         functools.partial(bottom_kernel, shots, depth, layers),
         [row_shape, ((COLS * COEFFS * depth, length), f32)],
         [high, high_l, high_r, soil_table, pml_width, start],
@@ -458,43 +509,54 @@
     )
 
     trace = bottom
-    halos = []
-    low_l = low_r = solved = None
+    lefts, rights = [], []
+    first_far = slabs // 2
     for hop in range(slabs - 1):
         arrived = both(trace, pairs([(hop, hop + 1)], [(t, t) for t in range(tiles)]))
-        if hop == slabs - 3:
-            mine = jnp.where(slab[0] == hop, trace, held)
-            moves = [(s, s) for s in range(hop)] + [(hop, hop + 1)]
-            halos.append((both(mine, pairs(moves, up)), both(mine, pairs(moves, down))))
-        if hop == slabs - 2:
-            mine = jnp.where(slab[0] == hop, trace, held)
-            moves = [(hop - 1, hop - 1), (hop, hop + 1)]
-            halos.append((both(mine, pairs(moves, up)), both(mine, pairs(moves, down))))
+        sides, mixed = [*lefts, *rights], first_far - 1 <= hop <= first_far
+        if hop >= first_far:
+            mine = gathered[0] if hop <= first_far + 1 else trace
+            near = range(hop) if hop == first_far else [first_far] if hop == first_far + 1 else []
+            moves = [(hop, hop + 1)] + [(s, s) for s in near]
+            from_left, from_right = both(mine, pairs(moves, up)), both(mine, pairs(moves, down))
         if hop == 1:
-            ready, _ = lax.optimization_barrier((low, trace))
-            low_l = across(ready, "tile", up)
-            low_r = across(ready, "tile", down)
-        if hop == slabs // 2:
+            again, _ = lax.optimization_barrier((src, trace))
+            (low,) = call(
+                "pack_low",
+                functools.partial(pack_low_kernel, shots, depth),
+                [((low_rows, length), f32)],
+                [again],
+            )
+            low_l = across(low, "tile", up)
+            low_r = across(low, "tile", down)
+        if hop == first_far - 1:
             lows, _ = lax.optimization_barrier(((low, low_l, low_r), trace))
             (solved,) = call(
+                "full",
                 functools.partial(full_kernel, shots, depth),
                 [((shots * PC * width * depth, length), f32)],
                 [coeffs, *lows, high, high_l, high_r],
                 None,
                 [pltpu.VMEM(((depth + 2) * COLS * PC * shots, length), f32)] * 2,
-                flops=10_000_000,
+                flops=FULL_COST,
+                limit=12 * MIB,
             )
             arrived, solved = lax.optimization_barrier((arrived, solved))
-        trace, held = call(
-            functools.partial(hop_kernel, shots, hop + 1),
-            [row_shape, row_shape],
-            [slab, arrived, heavy, light, bottom, trace, held],
-            [SMEM] + [VMEM] * 6,
+        trace, held, *gathered = call(
+            f"hop{hop}",
+            functools.partial(hop_kernel, shots, hop + 1, mixed),
+            [row_shape] * (4 if sides else 3 if mixed else 2),
+            [arrived, heavy, light, bottom, trace, held, *sides],
+            flops=HOP_COST,
         )
+        if hop >= first_far:
+            done_l, done_r = ([], []) if mixed else (gathered[:1], gathered[1:])
+            lefts, rights = done_l + [from_left], done_r + [from_right]
     (result,) = call(
+        "inject",
         functools.partial(inject_kernel, shots, depth),
         [(solved.shape, f32)],
-        [coeffs, held, halos[0][0], halos[1][0], halos[0][1], halos[1][1], solved],
+        [coeffs, held, solved, *lefts, *rights],
         None,
         [pltpu.VMEM((DEEP * COLS * PC * shots, length), f32)] * 2,
     )

time: 76.9 us -> 65.5 us (0.85)
  the two profiles are of different devices: /device:TPU:251 before, /device:TPU:255 now
where the time goes in v2:
time: 65.5 us; the launch traced here: 65.1 us
  waiting for transfers between devices  29.8 us (45%)
  starting transfers between devices  22.4 us (34%)
  Pallas kernels  9.65 us (15%)
  local copies, waits for them, and re-layouts  2.2 us (3%)
  between operations  0.97 us (1%)
    ppermute x13, waiting for transfers between devices, both(): return lax.ppermute(x, ('slab', 'tile'), moves)  15.7 us
    ppermute x4, waiting for transfers between devices, across(): return lax.ppermute(x, axes, moves)  14.1 us
    ppermute x4, starting transfers between devices, across(): return lax.ppermute(x, axes, moves)  11.7 us
    ppermute x13, starting transfers between devices, both(): return lax.ppermute(x, ('slab', 'tile'), moves)  10.7 us
    pallas_call x14, Pallas kernels, call(): pl.pallas_call(body, name=name, out_shape=[jax.ShapeDtypeStruct(shape, dt...  9.65 us
    unnamed x10, local copies, waits for them, and re-layouts  2.2 us
  transfers between devices with their start and end apart: 17, of which 6 were waited for; matrix products, arithmetic and copies ran while one was open for 0% of the time, Pallas kernels for 8%

profile of v2, /device:TPU:255, one launch (start us, length us, event | category | flops | bytes accessed | tf_op | source)
XLA Modules:
  0.0 65.1 jit_solution(15859497311267937335)
XLA Ops:
  0.6 1.3 %pack_high.1.own.high = f32[592,128]{1,0:T(8,128)S(1)} custom-call(f32[1536,128]{1,0:T(8,128)} %bitcast.8, s32[16,128]{1,0:T(8,128)} %bitcast.14), custom_call_target="tpu_custom_call" | custom-call | bytes 1048576 | tf_op jit(solution)/shard_map/pack_high/pallas_call | solution.py:31
  2.0 5.5 %collective-permute-start = (f32[592,128]{1,0:T(8,128)S(1)}, f32[592,128]{1,0:T(8,128)S(1)}, u32[]{:S(2)}, u32[]{:S(2)}) collective-permute-start(f32[592,128]{1,0:T(8,128)S(1)} %pack_high.1.own.high), channel_id=1, source_target_pairs={{0,1},{1,2},{2,3},{3,4},{4,5},{5,6},{6,7},{7,8},{8,9},{9,10},{10,1... | collective-permute-start | bytes 909320 | tf_op jit(solution)/shard_map/ppermute | solution.py:465
  7.5 1.9 %collective-permute-start.1 = (f32[592,128]{1,0:T(8,128)S(1)}, f32[592,128]{1,0:T(8,128)S(1)}, u32[]{:S(2)}, u32[]{:S(2)}) collective-permute-start(f32[592,128]{1,0:T(8,128)S(1)} %pack_high.1.own.high), channel_id=1, source_target_pairs={{1,0},{2,1},{3,2},{4,3},{5,4},{6,5},{7,6},{8,7},{9,8},{10,9},{11,1... | collective-permute-start | bytes 909320 | tf_op jit(solution)/shard_map/ppermute | solution.py:465
  9.4 1.7 %copy-done.1 = f32[2,1,2,384,384]{4,3,2,1,0:T(8,128)S(1)} copy-done((f32[2,1,2,384,384]{4,3,2,1,0:T(8,128)S(1)}, f32[2,1,2,384,384]{4,3,2,1,0:T(8,128)}, u32[]{:S(2)}) %copy-start.1) | copy-done | bytes 2359320
  11.1 0.4 split.1
  11.4 0.5 copy-done.2
  12.0 5.7 %collective-permute-done.1.right.high_r = f32[592,128]{1,0:T(8,128)S(1)} collective-permute-done((f32[592,128]{1,0:T(8,128)S(1)}, f32[592,128]{1,0:T(8,128)S(1)}, u32[]{:S(2)}, u32[]{:S(2)}) %collective-permute-start.1) | collective-permute-done | bytes 303136 | tf_op jit(solution)/shard_map/ppermute | solution.py:465
  17.7 1.2 %bottom.1 = (f32[64,384]{1,0:T(8,128)S(1)}, f32[528,128]{1,0:T(8,128)S(1)}) custom-call(f32[592,128]{1,0:T(8,128)S(1)} %pack_high.1.own.high, f32[592,128]{1,0:T(8,128)S(1)} %collective-permute-done.left.high_l, f32[592,128]{1,0:T(8,128)S(1)} %collective-permute-done.1.right.high_r, f32[3,8]{1,0:T(4,128)S(1)} %copy-done.3, s32[1,2]{1,0:T(1,128)S(1)} %copy-done.4, ...), custom_call_target="tpu_custom_call" | custom-call | bytes 1048576 | tf_op jit(solution)/shard_map/bottom/pallas_call | solution.py:31
  18.9 0.8 %collective-permute-start.2 = (f32[64,384]{1,0:T(8,128)S(1)}, f32[64,384]{1,0:T(8,128)S(1)}, u32[]{:S(2)}, u32[]{:S(2)}) collective-permute-start(f32[64,384]{1,0:T(8,128)S(1)} %get-tuple-element.35.bottom.trace), channel_id=1, source_target_pairs={{0,64},{1,65},{2,66},{3,67},{4,68},{5,69},{6,70},{7,71},{8,72},{9,... | collective-permute-start | bytes 294920 | tf_op jit(solution)/shard_map/ppermute | solution.py:474
  19.8 0.7 %collective-permute-start.3 = (f32[64,384]{1,0:T(8,128)S(1)}, f32[64,384]{1,0:T(8,128)S(1)}, u32[]{:S(2)}, u32[]{:S(2)}) collective-permute-start(f32[64,384]{1,0:T(8,128)S(1)} %get-tuple-element.36.trace), channel_id=1, source_target_pairs={{64,128},{65,129},{66,130},{67,131},{68,132},{69,133},{70,134},{71... | collective-permute-start | bytes 294920 | tf_op jit(solution)/shard_map/ppermute | solution.py:474
  20.5 0.3 pack_low.1.low
  20.8 1.9 %collective-permute-start.6 = (f32[960,128]{1,0:T(8,128)S(1)}, f32[960,128]{1,0:T(8,128)S(1)}, u32[]{:S(2)}, u32[]{:S(2)}) collective-permute-start(f32[960,128]{1,0:T(8,128)S(1)} %pack_low.1.low), channel_id=1, source_target_pairs={{0,1},{1,2},{2,3},{3,4},{4,5},{5,6},{6,7},{7,8},{8,9},{9,10},{10,1... | collective-permute-start | bytes 1474568 | tf_op jit(solution)/shard_map/ppermute | solution.py:465
  22.7 2.4 %collective-permute-start.7 = (f32[960,128]{1,0:T(8,128)S(1)}, f32[960,128]{1,0:T(8,128)S(1)}, u32[]{:S(2)}, u32[]{:S(2)}) collective-permute-start(f32[960,128]{1,0:T(8,128)S(1)} %pack_low.1.low), channel_id=1, source_target_pairs={{1,0},{2,1},{3,2},{4,3},{5,4},{6,5},{7,6},{8,7},{9,8},{10,9},{11,1... | collective-permute-start | bytes 1474568 | tf_op jit(solution)/shard_map/ppermute | solution.py:465
  25.2 0.7 %collective-permute-start.4 = (f32[64,384]{1,0:T(8,128)S(1)}, f32[64,384]{1,0:T(8,128)S(1)}, u32[]{:S(2)}, u32[]{:S(2)}) collective-permute-start(f32[64,384]{1,0:T(8,128)S(1)} %get-tuple-element.38.trace), channel_id=1, source_target_pairs={{128,192},{129,193},{130,194},{131,195},{132,196},{133,197},{134,1... | collective-permute-start | bytes 294920 | tf_op jit(solution)/shard_map/ppermute | solution.py:474
  25.9 0.7 %collective-permute-start.5 = (f32[64,384]{1,0:T(8,128)S(1)}, f32[64,384]{1,0:T(8,128)S(1)}, u32[]{:S(2)}, u32[]{:S(2)}) collective-permute-start(f32[64,384]{1,0:T(8,128)S(1)} %get-tuple-element.40.trace), channel_id=1, source_target_pairs={{192,256},{193,257},{194,258},{195,259},{196,260},{197,261},{198,2... | collective-permute-start | bytes 294920 | tf_op jit(solution)/shard_map/ppermute | solution.py:474
  26.6 1.9 %collective-permute-done.6.low_l = f32[960,128]{1,0:T(8,128)S(1)} collective-permute-done((f32[960,128]{1,0:T(8,128)S(1)}, f32[960,128]{1,0:T(8,128)S(1)}, u32[]{:S(2)}, u32[]{:S(2)}) %collective-permute-start.6) | collective-permute-done | bytes 491552 | tf_op jit(solution)/shard_map/ppermute | solution.py:465
  28.5 6.5 %collective-permute-done.7.low_r = f32[960,128]{1,0:T(8,128)S(1)} collective-permute-done((f32[960,128]{1,0:T(8,128)S(1)}, f32[960,128]{1,0:T(8,128)S(1)}, u32[]{:S(2)}, u32[]{:S(2)}) %collective-permute-start.7) | collective-permute-done | bytes 491552 | tf_op jit(solution)/shard_map/ppermute | solution.py:465
  35.0 3.4 %full.1.base = f32[1536,128]{1,0:T(8,128)S(1)} custom-call(f32[528,128]{1,0:T(8,128)S(1)} %get-tuple-element.34.coeffs, f32[960,128]{1,0:T(8,128)S(1)} %pack_low.1.low, f32[960,128]{1,0:T(8,128)S(1)} %collective-permute-done.6.low_l, f32[960,128]{1,0:T(8,128)S(1)} %collective-permute-done.7.low_r, f32[592,128]{1,0:T(8,128)S(1)} %pack_high.1.own.high, ...), custom_call_target="tpu_custom_call" | custom-call | flops 5000000000 | bytes 1048576 | tf_op jit(solution)/shard_map/full/pallas_call | solution.py:31
  38.4 0.7 %collective-permute-start.8 = (f32[64,384]{1,0:T(8,128)S(1)}, f32[64,384]{1,0:T(8,128)S(1)}, u32[]{:S(2)}, u32[]{:S(2)}) collective-permute-start(f32[64,384]{1,0:T(8,128)S(1)} %get-tuple-element.47.trace), channel_id=1, source_target_pairs={{256,320},{257,321},{258,322},{259,323},{260,324},{261,325},{262,3... | collective-permute-start | bytes 294920 | tf_op jit(solution)/shard_map/ppermute | solution.py:474
  39.1 0.7 %collective-permute-start.10 = (f32[64,384]{1,0:T(8,128)S(1)}, f32[64,384]{1,0:T(8,128)S(1)}, u32[]{:S(2)}, u32[]{:S(2)}) collective-permute-start(f32[64,384]{1,0:T(8,128)S(1)} %get-tuple-element.51), channel_id=1, source_target_pairs={{256,321},{257,322},{258,323},{259,324},{260,325},{261,326},{262,3... | collective-permute-start | bytes 294920 | tf_op jit(solution)/shard_map/ppermute | solution.py:474
  39.8 0.7 %collective-permute-start.11 = (f32[64,384]{1,0:T(8,128)S(1)}, f32[64,384]{1,0:T(8,128)S(1)}, u32[]{:S(2)}, u32[]{:S(2)}) collective-permute-start(f32[64,384]{1,0:T(8,128)S(1)} %get-tuple-element.51), channel_id=1, source_target_pairs={{257,320},{258,321},{259,322},{260,323},{261,324},{262,325},{263,3... | collective-permute-start | bytes 294920 | tf_op jit(solution)/shard_map/ppermute | solution.py:474
  40.5 0.7 %collective-permute-start.9 = (f32[64,384]{1,0:T(8,128)S(1)}, f32[64,384]{1,0:T(8,128)S(1)}, u32[]{:S(2)}, u32[]{:S(2)}) collective-permute-start(f32[64,384]{1,0:T(8,128)S(1)} %get-tuple-element.49.trace), channel_id=1, source_target_pairs={{320,384},{321,385},{322,386},{323,387},{324,388},{325,389},{326,3... | collective-permute-start | bytes 294920 | tf_op jit(solution)/shard_map/ppermute | solution.py:474
  41.2 0.7 %collective-permute-start.13 = (f32[64,384]{1,0:T(8,128)S(1)}, f32[64,384]{1,0:T(8,128)S(1)}, u32[]{:S(2)}, u32[]{:S(2)}) collective-permute-start(f32[64,384]{1,0:T(8,128)S(1)} %get-tuple-element.55), channel_id=1, source_target_pairs={{320,385},{321,386},{322,387},{323,388},{324,389},{325,390},{326,3... | collective-permute-start | bytes 294920 | tf_op jit(solution)/shard_map/ppermute | solution.py:474
  41.9 0.7 %collective-permute-start.14 = (f32[64,384]{1,0:T(8,128)S(1)}, f32[64,384]{1,0:T(8,128)S(1)}, u32[]{:S(2)}, u32[]{:S(2)}) collective-permute-start(f32[64,384]{1,0:T(8,128)S(1)} %get-tuple-element.55), channel_id=1, source_target_pairs={{321,384},{322,385},{323,386},{324,387},{325,388},{326,389},{327,3... | collective-permute-start | bytes 294920 | tf_op jit(solution)/shard_map/ppermute | solution.py:474
  42.6 1.3 %collective-permute-start.12 = (f32[64,384]{1,0:T(8,128)S(1)}, f32[64,384]{1,0:T(8,128)S(1)}, u32[]{:S(2)}, u32[]{:S(2)}) collective-permute-start(f32[64,384]{1,0:T(8,128)S(1)} %get-tuple-element.52.trace), channel_id=1, source_target_pairs={{384,448},{385,449},{386,450},{387,451},{388,452},{389,453},{390,4... | collective-permute-start | bytes 294920 | tf_op jit(solution)/shard_map/ppermute | solution.py:474
  43.9 1.3 %collective-permute-start.15 = (f32[64,384]{1,0:T(8,128)S(1)}, f32[64,384]{1,0:T(8,128)S(1)}, u32[]{:S(2)}, u32[]{:S(2)}) collective-permute-start(f32[64,384]{1,0:T(8,128)S(1)} %get-tuple-element.52.trace), channel_id=1, source_target_pairs={{384,449},{385,450},{386,451},{387,452},{388,453},{389,454},{390,4... | collective-permute-start | bytes 294920 | tf_op jit(solution)/shard_map/ppermute | solution.py:474
  45.2 1.3 %collective-permute-start.16 = (f32[64,384]{1,0:T(8,128)S(1)}, f32[64,384]{1,0:T(8,128)S(1)}, u32[]{:S(2)}, u32[]{:S(2)}) collective-permute-start(f32[64,384]{1,0:T(8,128)S(1)} %get-tuple-element.52.trace), channel_id=1, source_target_pairs={{385,448},{386,449},{387,450},{388,451},{389,452},{390,453},{391,4... | collective-permute-start | bytes 294920 | tf_op jit(solution)/shard_map/ppermute | solution.py:474
  46.5 10.4 %collective-permute-done.12.arrived = f32[64,384]{1,0:T(8,128)S(1)} collective-permute-done((f32[64,384]{1,0:T(8,128)S(1)}, f32[64,384]{1,0:T(8,128)S(1)}, u32[]{:S(2)}, u32[]{:S(2)}) %collective-permute-start.12) | collective-permute-done | bytes 98336 | tf_op jit(solution)/shard_map/ppermute | solution.py:474
  57.0 1.1 %hop6.1 = (f32[64,384]{1,0:T(8,128)}, f32[64,384]{1,0:T(8,128)S(1)}, f32[64,384]{1,0:T(8,128)S(1)}, f32[64,384]{1,0:T(8,128)S(1)}) custom-call(f32[64,384]{1,0:T(8,128)S(1)} %collective-permute-done.12.arrived, bf16[1536,384]{1,0:T(8,128)(2,1)S(1)} %get-tuple-element.32.high, bf16[1536,384]{1,0:T(8,128)(2,1)S(1)} %get-tuple-element.33.low, ...), custom_call_target="tpu_custom_call" | custom-call | flops 2000000000 | bytes 1048576 | tf_op jit(solution)/shard_map/hop6/pallas_call | solution.py:31
  58.1 1.0 %collective-permute-done.15.refs_1_ = f32[64,384]{1,0:T(8,128)S(1)} collective-permute-done((f32[64,384]{1,0:T(8,128)S(1)}, f32[64,384]{1,0:T(8,128)S(1)}, u32[]{:S(2)}, u32[]{:S(2)}) %collective-permute-start.15) | collective-permute-done | bytes 98336 | tf_op jit(solution)/shard_map/ppermute | solution.py:474
  59.1 4.2 %collective-permute-done.16.refs_3_ = f32[64,384]{1,0:T(8,128)S(1)} collective-permute-done((f32[64,384]{1,0:T(8,128)S(1)}, f32[64,384]{1,0:T(8,128)S(1)}, u32[]{:S(2)}, u32[]{:S(2)}) %collective-permute-start.16) | collective-permute-done | bytes 98336 | tf_op jit(solution)/shard_map/ppermute | solution.py:474
  63.3 1.7 %inject.1 = f32[1536,128]{1,0:T(8,128)} custom-call(f32[528,128]{1,0:T(8,128)S(1)} %get-tuple-element.34.coeffs, f32[64,384]{1,0:T(8,128)S(1)} %get-tuple-element.57.own, f32[1536,128]{1,0:T(8,128)S(1)} %full.1.base, f32[64,384]{1,0:T(8,128)S(1)} %get-tuple-element.59.refs_0_, f32[64,384]{1,0:T(8,128)S(1)} %collective-permute-done.15.refs_1_, ...), custom_call_target="tpu_custom_call" | custom-call | bytes 1048576 | tf_op jit(solution)/shard_map/inject/pallas_call | solution.py:31
  (26 shorter events, 0.3 us)
Async XLA Ops:
  2.0 10.0 %collective-permute-start = (f32[592,128]{1,0:T(8,128)S(1)}, f32[592,128]{1,0:T(8,128)S(1)}, u32[]{:S(2)}, u32[]{:S(2)}) collective-permute-start(f32[592,128]{1,0:T(8,128)S(1)} %pack_high.1.own.high), channel_id=1, source_target_pairs={{0,1},{1,2},{2,3},{3,4},{4,5},{5,6},{6,7},{7,8},{8,9},{9,10},{10,1... | collective-permute-start | bytes 909320 | tf_op jit(solution)/shard_map/ppermute | solution.py:465
  7.5 10.2 %collective-permute-start.1 = (f32[592,128]{1,0:T(8,128)S(1)}, f32[592,128]{1,0:T(8,128)S(1)}, u32[]{:S(2)}, u32[]{:S(2)}) collective-permute-start(f32[592,128]{1,0:T(8,128)S(1)} %pack_high.1.own.high), channel_id=1, source_target_pairs={{1,0},{2,1},{3,2},{4,3},{5,4},{6,5},{7,6},{8,7},{9,8},{10,9},{11,1... | collective-permute-start | bytes 909320 | tf_op jit(solution)/shard_map/ppermute | solution.py:465
  9.4 1.7 %copy-start.1 = (f32[2,1,2,384,384]{4,3,2,1,0:T(8,128)S(1)}, f32[2,1,2,384,384]{4,3,2,1,0:T(8,128)}, u32[]{:S(2)}) copy-start(f32[2,1,2,384,384]{4,3,2,1,0:T(8,128)} %param.10) | copy-start | bytes 7077892
  11.1 0.9 %copy-start.2 = (f32[2,2,16,384]{3,2,1,0:T(8,128)S(1)}, f32[2,2,16,384]{3,2,1,0:T(8,128)}, u32[]{:S(2)}) copy-start(f32[2,2,16,384]{3,2,1,0:T(8,128)} %param.11) | copy-start | bytes 294916
  12.0 5.8 %copy-start.3 = (f32[3,8]{1,0:T(4,128)S(1)}, f32[3,8]{1,0:T(4,128)}, u32[]{:S(2)}) copy-start(f32[3,8]{1,0:T(4,128)} %table.1) | copy-start | bytes 292
  12.0 5.8 %copy-start.4 = (s32[1,2]{1,0:T(1,128)S(1)}, s32[1,2]{1,0:T(1,128)}, u32[]{:S(2)}) copy-start(s32[1,2]{1,0:T(1,128)} %widths.1) | copy-start | bytes 28
  18.9 1.5 %copy-start = (f32[16,2,3,2,8,128]{5,4,3,2,1,0:T(8,128)S(1)}, f32[16,2,3,2,8,128]{5,4,3,2,1,0:T(8,128)}, u32[]{:S(2)}) copy-start(f32[16,2,3,2,8,128]{5,4,3,2,1,0:T(8,128)} %param.6) | copy-start | bytes 2359300
  18.9 0.8 %collective-permute-start.2 = (f32[64,384]{1,0:T(8,128)S(1)}, f32[64,384]{1,0:T(8,128)S(1)}, u32[]{:S(2)}, u32[]{:S(2)}) collective-permute-start(f32[64,384]{1,0:T(8,128)S(1)} %get-tuple-element.35.bottom.trace), channel_id=1, source_target_pairs={{0,64},{1,65},{2,66},{3,67},{4,68},{5,69},{6,70},{7,71},{8,72},{9,... | collective-permute-start | bytes 294920 | tf_op jit(solution)/shard_map/ppermute | solution.py:474
  19.8 5.3 %collective-permute-start.3 = (f32[64,384]{1,0:T(8,128)S(1)}, f32[64,384]{1,0:T(8,128)S(1)}, u32[]{:S(2)}, u32[]{:S(2)}) collective-permute-start(f32[64,384]{1,0:T(8,128)S(1)} %get-tuple-element.36.trace), channel_id=1, source_target_pairs={{64,128},{65,129},{66,130},{67,131},{68,132},{69,133},{70,134},{71... | collective-permute-start | bytes 294920 | tf_op jit(solution)/shard_map/ppermute | solution.py:474
  20.8 7.7 %collective-permute-start.6 = (f32[960,128]{1,0:T(8,128)S(1)}, f32[960,128]{1,0:T(8,128)S(1)}, u32[]{:S(2)}, u32[]{:S(2)}) collective-permute-start(f32[960,128]{1,0:T(8,128)S(1)} %pack_low.1.low), channel_id=1, source_target_pairs={{0,1},{1,2},{2,3},{3,4},{4,5},{5,6},{6,7},{7,8},{8,9},{9,10},{10,1... | collective-permute-start | bytes 1474568 | tf_op jit(solution)/shard_map/ppermute | solution.py:465
  22.7 12.3 %collective-permute-start.7 = (f32[960,128]{1,0:T(8,128)S(1)}, f32[960,128]{1,0:T(8,128)S(1)}, u32[]{:S(2)}, u32[]{:S(2)}) collective-permute-start(f32[960,128]{1,0:T(8,128)S(1)} %pack_low.1.low), channel_id=1, source_target_pairs={{1,0},{2,1},{3,2},{4,3},{5,4},{6,5},{7,6},{8,7},{9,8},{10,9},{11,1... | collective-permute-start | bytes 1474568 | tf_op jit(solution)/shard_map/ppermute | solution.py:465
  25.2 0.7 %collective-permute-start.4 = (f32[64,384]{1,0:T(8,128)S(1)}, f32[64,384]{1,0:T(8,128)S(1)}, u32[]{:S(2)}, u32[]{:S(2)}) collective-permute-start(f32[64,384]{1,0:T(8,128)S(1)} %get-tuple-element.38.trace), channel_id=1, source_target_pairs={{128,192},{129,193},{130,194},{131,195},{132,196},{133,197},{134,1... | collective-permute-start | bytes 294920 | tf_op jit(solution)/shard_map/ppermute | solution.py:474
  25.9 12.5 %collective-permute-start.5 = (f32[64,384]{1,0:T(8,128)S(1)}, f32[64,384]{1,0:T(8,128)S(1)}, u32[]{:S(2)}, u32[]{:S(2)}) collective-permute-start(f32[64,384]{1,0:T(8,128)S(1)} %get-tuple-element.40.trace), channel_id=1, source_target_pairs={{192,256},{193,257},{194,258},{195,259},{196,260},{197,261},{198,2... | collective-permute-start | bytes 294920 | tf_op jit(solution)/shard_map/ppermute | solution.py:474
  38.4 2.0 %collective-permute-start.8 = (f32[64,384]{1,0:T(8,128)S(1)}, f32[64,384]{1,0:T(8,128)S(1)}, u32[]{:S(2)}, u32[]{:S(2)}) collective-permute-start(f32[64,384]{1,0:T(8,128)S(1)} %get-tuple-element.47.trace), channel_id=1, source_target_pairs={{256,320},{257,321},{258,322},{259,323},{260,324},{261,325},{262,3... | collective-permute-start | bytes 294920 | tf_op jit(solution)/shard_map/ppermute | solution.py:474
  39.1 3.4 %collective-permute-start.10 = (f32[64,384]{1,0:T(8,128)S(1)}, f32[64,384]{1,0:T(8,128)S(1)}, u32[]{:S(2)}, u32[]{:S(2)}) collective-permute-start(f32[64,384]{1,0:T(8,128)S(1)} %get-tuple-element.51), channel_id=1, source_target_pairs={{256,321},{257,322},{258,323},{259,324},{260,325},{261,326},{262,3... | collective-permute-start | bytes 294920 | tf_op jit(solution)/shard_map/ppermute | solution.py:474
  39.8 2.8 %collective-permute-start.11 = (f32[64,384]{1,0:T(8,128)S(1)}, f32[64,384]{1,0:T(8,128)S(1)}, u32[]{:S(2)}, u32[]{:S(2)}) collective-permute-start(f32[64,384]{1,0:T(8,128)S(1)} %get-tuple-element.51), channel_id=1, source_target_pairs={{257,320},{258,321},{259,322},{260,323},{261,324},{262,325},{263,3... | collective-permute-start | bytes 294920 | tf_op jit(solution)/shard_map/ppermute | solution.py:474
  40.5 2.0 %collective-permute-start.9 = (f32[64,384]{1,0:T(8,128)S(1)}, f32[64,384]{1,0:T(8,128)S(1)}, u32[]{:S(2)}, u32[]{:S(2)}) collective-permute-start(f32[64,384]{1,0:T(8,128)S(1)} %get-tuple-element.49.trace), channel_id=1, source_target_pairs={{320,384},{321,385},{322,386},{323,387},{324,388},{325,389},{326,3... | collective-permute-start | bytes 294920 | tf_op jit(solution)/shard_map/ppermute | solution.py:474
  41.2 5.3 %collective-permute-start.13 = (f32[64,384]{1,0:T(8,128)S(1)}, f32[64,384]{1,0:T(8,128)S(1)}, u32[]{:S(2)}, u32[]{:S(2)}) collective-permute-start(f32[64,384]{1,0:T(8,128)S(1)} %get-tuple-element.55), channel_id=1, source_target_pairs={{320,385},{321,386},{322,387},{323,388},{324,389},{325,390},{326,3... | collective-permute-start | bytes 294920 | tf_op jit(solution)/shard_map/ppermute | solution.py:474
  41.9 4.7 %collective-permute-start.14 = (f32[64,384]{1,0:T(8,128)S(1)}, f32[64,384]{1,0:T(8,128)S(1)}, u32[]{:S(2)}, u32[]{:S(2)}) collective-permute-start(f32[64,384]{1,0:T(8,128)S(1)} %get-tuple-element.55), channel_id=1, source_target_pairs={{321,384},{322,385},{323,386},{324,387},{325,388},{326,389},{327,3... | collective-permute-start | bytes 294920 | tf_op jit(solution)/shard_map/ppermute | solution.py:474
  42.6 14.3 %collective-permute-start.12 = (f32[64,384]{1,0:T(8,128)S(1)}, f32[64,384]{1,0:T(8,128)S(1)}, u32[]{:S(2)}, u32[]{:S(2)}) collective-permute-start(f32[64,384]{1,0:T(8,128)S(1)} %get-tuple-element.52.trace), channel_id=1, source_target_pairs={{384,448},{385,449},{386,450},{387,451},{388,452},{389,453},{390,4... | collective-permute-start | bytes 294920 | tf_op jit(solution)/shard_map/ppermute | solution.py:474
  43.9 15.2 %collective-permute-start.15 = (f32[64,384]{1,0:T(8,128)S(1)}, f32[64,384]{1,0:T(8,128)S(1)}, u32[]{:S(2)}, u32[]{:S(2)}) collective-permute-start(f32[64,384]{1,0:T(8,128)S(1)} %get-tuple-element.52.trace), channel_id=1, source_target_pairs={{384,449},{385,450},{386,451},{387,452},{388,453},{389,454},{390,4... | collective-permute-start | bytes 294920 | tf_op jit(solution)/shard_map/ppermute | solution.py:474
  45.2 18.1 %collective-permute-start.16 = (f32[64,384]{1,0:T(8,128)S(1)}, f32[64,384]{1,0:T(8,128)S(1)}, u32[]{:S(2)}, u32[]{:S(2)}) collective-permute-start(f32[64,384]{1,0:T(8,128)S(1)} %get-tuple-element.52.trace), channel_id=1, source_target_pairs={{385,448},{386,449},{387,450},{388,451},{389,452},{390,453},{391,4... | collective-permute-start | bytes 294920 | tf_op jit(solution)/shard_map/ppermute | solution.py:474

commit v3 on v2

--- a/solution.py
+++ b/solution.py
@@ -24,10 +24,13 @@
 MIB = 1024 * 1024
 LIMIT = 6 * MIB
 HOP_COST = 2_000_000_000
+LOW_COST = 2000000000.0
+HOP_COSTS = (2000000000.0, 2000000000.0, 2000000000.0, 2000000000.0, 1000000.0, 1000000.0, 2000000000.0)
+GATHER_COST = 2000000000.0
 FULL_COST = 5_000_000_000
 
 
-def call(name, body, outs, operands, specs=None, scratch=(), flops=0, limit=LIMIT):
+def call(name, body, outs, operands, specs=None, scratch=(), flops=5e8, limit=LIMIT):
     return pl.pallas_call(
         body,
         name=name,
@@ -36,7 +39,7 @@
         out_specs=[VMEM] * len(outs),
         scratch_shapes=list(scratch),
         compiler_params=pltpu.CompilerParams(vmem_limit_bytes=limit),
-        cost_estimate=pl.CostEstimate(flops=flops, bytes_accessed=1 << 20, transcendentals=0),
+        cost_estimate=pl.CostEstimate(flops=int(flops), bytes_accessed=0, transcendentals=0),
     )(*operands)
 
 
@@ -222,17 +225,42 @@
     return 2, col - HALO - WIDTH
 
 
+def pick(which, own, off, on, read):
+    if which == 1:
+        return read(own)
+    even = lax.axis_index("tile") % 2 == 0
+    first, second = read(off), read(on)
+    return jnp.where(even, first, second) if which == 0 else jnp.where(even, second, first)
+
+
 def slot(z, col, pc):
     return (z * COLS + col) * PC + pc
 
 
-def bottom_kernel(shots, depth, layers, own, left, right, table, widths, start, bottom, coeffs, v1, v2):
-    tiles = (left, own, right)
+def bottom_kernel(shots, depth, layers, first_only, own, off, on, table, widths, start, *refs):
+    bottoms, coeffs, v1, v2 = refs[:WIDTH], *refs[WIDTH:]
+    work = functools.partial(
+        bottom_planes, shots, depth, layers, own, off, on, table, widths, start, bottoms, coeffs, v1, v2
+    )
+    if not first_only:
+        work()
+        return
+    slab = lax.axis_index("slab")
+    pl.when(slab == 0)(work)
+
+    @pl.when(slab != 0)
+    def _():
+        for ref in bottoms:
+            ref[...] = jnp.zeros(ref.shape, jnp.float32)
+
+
+def bottom_planes(shots, depth, layers, own, off, on, table, widths, start, bottoms, coeffs, v1, v2):
     at = DEEP * WIDTH * PC * shots
     soils = []
     for col in range(COLS):
         which, place = tile_of(col)
-        soils.append(tiles[which][pl.ds(at + place * depth, depth), :])
+        where = pl.ds(at + place * depth, depth)
+        soils.append(pick(which, own, off, on, lambda ref: ref[where, :]))
     fill_coeffs(coeffs, soils, table, widths, depth, layers)
     base = depth - DEEP
 
@@ -244,8 +272,10 @@
             which, place = tile_of(col)
             coef = coef_of(coeffs, col, depth, base + z)
             for c in range(COMPS):
-                fr = block(tiles[which], (z * WIDTH + place) * PC + c)[...]
-                fi = block(tiles[which], (z * WIDTH + place) * PC + COMPS + c)[...]
+                fr, fi = (
+                    pick(which, own, off, on, lambda ref: block(ref, (z * WIDTH + place) * PC + pc)[...])
+                    for pc in (c, COMPS + c)
+                )
                 vr, vi = scaled(fr, fi, coef)
                 block(v1, slot(z, col, c))[...] = vr
                 block(v1, slot(z, col, COMPS + c))[...] = vi
@@ -271,16 +301,14 @@
                 jnp.where(lane < PATCH, pltpu.roll(even, PATCH, 1), odd),
             )
             for patch in range(2):
-                where = (
-                    pl.ds(((x - HALO) * 2 + patch) * shots, shots),
-                    pl.ds(pair * 2 * PATCH, 2 * PATCH),
-                )
-                bottom[where] = both[patch] + start[where]
-
-
-def full_kernel(shots, depth, coeffs, low, low_l, low_r, high, high_l, high_r, out, v1, v2):
+                lanes = pl.ds(pair * 2 * PATCH, 2 * PATCH)
+                given = start[pl.ds(((x - HALO) * 2 + patch) * shots, shots), lanes]
+                bottoms[x - HALO][pl.ds(patch * shots, shots), lanes] = both[patch] + given
+
+
+def full_kernel(shots, depth, coeffs, low, low_off, low_on, high, high_off, high_on, out, v1, v2):
     stride = PC * WIDTH * depth
-    lows, highs = (low_l, low, low_r), (high_l, high, high_r)
+    lows, highs = (low, low_off, low_on), (high, high_off, high_on)
     plane = COLS * PC * shots
 
     def at(z, col, pc):
@@ -298,8 +326,10 @@
                 coef = coef_of(coeffs, col, depth, z)
                 for c in range(COMPS):
                     number = ((z - shift) * WIDTH + place) * PC + c
-                    fr = tiles[which][pl.ds(pl.multiple_of(number * shots, shots), shots), :]
-                    fi = tiles[which][pl.ds(pl.multiple_of((number + COMPS) * shots, shots), shots), :]
+                    fr, fi = (
+                        pick(which, *tiles, lambda ref: ref[pl.ds(pl.multiple_of(n * shots, shots), shots), :])
+                        for n in (number, number + COMPS)
+                    )
                     vr, vi = scaled(fr, fi, coef)
                     v1[at(z, col, c), :] = vr
                     v1[at(z, col, COMPS + c), :] = vi
@@ -335,10 +365,10 @@
     lax.fori_loop(0, depth, last, 0)
 
 
-def inject_kernel(shots, depth, coeffs, own, base, *refs):
-    *halos, out, v1, v2 = refs
+def inject_kernel(shots, depth, coeffs, base, *refs):
+    own, halos, (out, v1, v2) = refs[:WIDTH], refs[WIDTH:-3], refs[-3:]
     half = len(halos) // 2
-    sources = (halos[:half], [own], halos[half:])
+    off, on = halos[:half], halos[half:]
     stride = PC * WIDTH * depth
 
     def block(ref, number):
@@ -356,7 +386,12 @@
                     pl.ds((place * 2 + patch) * shots, shots),
                     pl.ds(pair * 2 * PATCH, 2 * PATCH),
                 )
-                halves.append(plus(*[ref[where] for ref in sources[which]]))
+                if which == 1:
+                    halves.append(own[place][pl.ds(patch * shots, shots), where[1]])
+                else:
+                    halves.append(
+                        pick(which, None, off, on, lambda refs: plus(*[ref[where] for ref in refs]))
+                    )
             planes.append(jnp.where(lane < PATCH, halves[0], pltpu.roll(halves[1], PATCH, 1)))
             planes.append(jnp.where(lane < PATCH, pltpu.roll(halves[0], PATCH, 1), halves[1]))
         shear = coef(A)
@@ -392,14 +427,14 @@
     low[...] = (whole - top.astype(jnp.float32)).astype(jnp.bfloat16)
 
 
-def product(shots, x, high, low, add, out):
+def product(shots, x, high, low, add, out, first):
     size = x.shape[1]
     for chain in range(x.shape[0] // shots):
         rows = pl.ds(chain * shots, shots)
         whole = x[rows, :]
         top = whole.astype(jnp.bfloat16)
         rest = (whole - top.astype(jnp.float32)).astype(jnp.bfloat16)
-        block = pl.ds(chain * size, size)
+        block = pl.ds((first + chain) * size, size)
         wide = jnp.dot(
             jnp.concatenate([top, rest], axis=0), high[block, :], preferred_element_type=jnp.float32
         )
@@ -408,26 +443,29 @@
         out[rows, :] = total if add is None else total + add[rows, :]
 
 
-def start_kernel(shots, inflow, high, low, out):
+def start_kernel(shots, inflow, high, low, out, *helds):
     slab = lax.axis_index("slab")
 
     @pl.when(slab == 0)
     def _():
-        product(shots, inflow, high, low, None, out)
+        product(shots, inflow, high, low, None, out, 0)
 
     @pl.when(slab != 0)
     def _():
         out[...] = jnp.zeros(out.shape, jnp.float32)
 
-
-def hop_kernel(shots, turn, mixed, arrived, high, low, bottom, trace, held, *refs):
+    for col, ref in enumerate(helds):
+        ref[...] = inflow[pl.ds(col * ref.shape[0], ref.shape[0]), :]
+
+
+def hop_kernel(shots, turn, col, groups, *refs):
+    arrived, high, low, bottom, trace, held, *rest = refs
+    sides, (new_trace, new_held, *sums) = rest[: sum(groups)], rest[sum(groups) :]
     slab = lax.axis_index("slab")
-    half = max(len(refs) - 4, 0) // 2
-    sides, (new_trace, new_held, *others) = refs[: 2 * half], refs[2 * half :]
 
     @pl.when(slab == turn)
     def _():
-        product(shots, arrived, high, low, bottom, new_trace)
+        product(shots, arrived, high, low, bottom, new_trace, col * (arrived.shape[0] // shots))
         new_held[...] = arrived[...]
 
     @pl.when(slab != turn)
@@ -435,20 +473,22 @@
         new_trace[...] = trace[...]
         new_held[...] = held[...]
 
-    if mixed:
-        (mine,) = others
-
-        @pl.when(slab == turn)
-        def _():
-            mine[...] = new_trace[...]
-
-        @pl.when(slab != turn)
-        def _():
-            mine[...] = held[...]
-
-    else:
-        for number, ref in enumerate(others):
-            ref[...] = plus(*[side[...] for side in sides[number * half : (number + 1) * half]])
+    for ref, count in zip(sums, [g for g in groups if g]):
+        ref[...] = plus(*[side[...] for side in sides[:count]])
+        sides = sides[count:]
+
+
+def gather_kernel(turn, *refs):
+    mine, rows = refs[-1], refs[0].shape[0]
+    traces, helds = refs[:WIDTH], refs[WIDTH:-1]
+
+    def fill(parts):
+        for number, part in enumerate(parts):
+            mine[pl.ds(number * rows, rows), :] = part[...]
+
+    slab = lax.axis_index("slab")
+    pl.when(slab == turn)(lambda: fill(traces))
+    pl.when(slab != turn)(lambda: fill(helds))
 
 
 def per_device(source, soil_index, soil_table, pml_width, interface_blocks, inflow):
@@ -461,11 +501,11 @@
     low_rows = (depth - DEEP) * width * PC * shots
     high_rows = DEEP * width * PC * shots + width * depth
 
-    def across(x, axes, moves):
-        return lax.ppermute(x, axes, moves)
-
-    up = [(t, t + 1) for t in range(tiles - 1)]
-    down = [(t + 1, t) for t in range(tiles - 1)]
+    off = [p for t in range(1, tiles - 1, 2) for p in ((t, t + 1), (t + 1, t))]
+    on = [p for t in range(0, tiles - 1, 2) for p in ((t, t + 1), (t + 1, t))]
+
+    def exchange(x):
+        return lax.ppermute(x, "tile", off), lax.ppermute(x, "tile", on)
 
     def pairs(slab_moves, tile_moves):
         return [(a * tiles + t, b * tiles + u) for a, b in slab_moves for t, u in tile_moves]
@@ -486,81 +526,113 @@
             pltpu.SemaphoreType.DMA((2,)),
         ],
     )
-    high_l = across(high, "tile", up)
-    high_r = across(high, "tile", down)
+    high_off, high_on = exchange(high)
 
     blocks = interface_blocks.reshape(chains * size, size)
     heavy, light = call("split", split_kernel, [(blocks.shape, bf16)] * 2, [blocks])
     held = inflow.reshape(chains * shots, size)
     row_shape = ((chains * shots, size), f32)
-    (start,) = call(
+    chunk = (chains // width * shots, size)
+    start, *helds = call(
         "start",
         functools.partial(start_kernel, shots),
-        [row_shape],
+        [row_shape] + [(chunk, f32)] * width,
         [held, heavy, light],
     )
-    bottom, coeffs = call(
+    table_shape = (COLS * COEFFS * depth, length)
+    planes = [pltpu.VMEM((DEEP * COLS * PC * shots, length), f32)] * 2
+    near = [high, high_off, high_on, soil_table, pml_width, start]
+    near_specs = [VMEM, VMEM, VMEM, SMEM, SMEM, VMEM]
+    traces = call(
+        "first",
+        functools.partial(bottom_kernel, shots, depth, layers, True),
+        [(chunk, f32)] * width,
+        near,
+        near_specs,
+        [pltpu.VMEM(table_shape, f32)] + planes,
+    )
+    *bottoms, coeffs = call(
         "bottom",
-        functools.partial(bottom_kernel, shots, depth, layers),
-        [row_shape, ((COLS * COEFFS * depth, length), f32)],
-        [high, high_l, high_r, soil_table, pml_width, start],
-        [VMEM, VMEM, VMEM, SMEM, SMEM, VMEM],
-        [pltpu.VMEM((DEEP * COLS * PC * shots, length), f32)] * 2,
-    )
-
-    trace = bottom
-    lefts, rights = [], []
-    first_far = slabs // 2
+        functools.partial(bottom_kernel, shots, depth, layers, False),
+        [(chunk, f32)] * width + [(table_shape, f32)],
+        near,
+        near_specs,
+        planes,
+        flops=HOP_COST,
+    )
+    offs, ons = [], []
+    first_far, mine = slabs // 2, None
     for hop in range(slabs - 1):
-        arrived = both(trace, pairs([(hop, hop + 1)], [(t, t) for t in range(tiles)]))
-        sides, mixed = [*lefts, *rights], first_far - 1 <= hop <= first_far
+        step = pairs([(hop, hop + 1)], [(t, t) for t in range(tiles)])
+        arrived = [both(trace, step) for trace in traces]
+        groups = (len(offs), len(ons))
+        sides = [*offs, *ons]
+        from_off, from_on = [], []
         if hop >= first_far:
-            mine = gathered[0] if hop <= first_far + 1 else trace
-            near = range(hop) if hop == first_far else [first_far] if hop == first_far + 1 else []
-            moves = [(hop, hop + 1)] + [(s, s) for s in near]
-            from_left, from_right = both(mine, pairs(moves, up)), both(mine, pairs(moves, down))
+            same = range(hop) if hop == first_far else [first_far] if hop == first_far + 1 else []
+            from_off = [both(mine, pairs([(hop, hop + 1)] + [(s, s) for s in same], off))]
+        if hop > first_far:
+            same = range(hop) if hop == slabs - 2 else []
+            from_on = [both(mine, pairs([(hop, hop + 1)] + [(s, s) for s in same], on))]
         if hop == 1:
-            again, _ = lax.optimization_barrier((src, trace))
+            again, _ = lax.optimization_barrier((src, traces))
             (low,) = call(
                 "pack_low",
                 functools.partial(pack_low_kernel, shots, depth),
                 [((low_rows, length), f32)],
                 [again],
+                flops=LOW_COST,
             )
-            low_l = across(low, "tile", up)
-            low_r = across(low, "tile", down)
+            low_off, low_on = exchange(low)
         if hop == first_far - 1:
-            lows, _ = lax.optimization_barrier(((low, low_l, low_r), trace))
+            lows, _ = lax.optimization_barrier(((low, low_off, low_on), traces))
             (solved,) = call(
                 "full",
                 functools.partial(full_kernel, shots, depth),
                 [((shots * PC * width * depth, length), f32)],
-                [coeffs, *lows, high, high_l, high_r],
+                [coeffs, *lows, high, high_off, high_on],
                 None,
                 [pltpu.VMEM(((depth + 2) * COLS * PC * shots, length), f32)] * 2,
                 flops=FULL_COST,
                 limit=12 * MIB,
             )
             arrived, solved = lax.optimization_barrier((arrived, solved))
-        trace, held, *gathered = call(
-            f"hop{hop}",
-            functools.partial(hop_kernel, shots, hop + 1, mixed),
-            [row_shape] * (4 if sides else 3 if mixed else 2),
-            [arrived, heavy, light, bottom, trace, held, *sides],
-            flops=HOP_COST,
-        )
-        if hop >= first_far:
-            done_l, done_r = ([], []) if mixed else (gathered[:1], gathered[1:])
-            lefts, rights = done_l + [from_left], done_r + [from_right]
+        if hop in (1, slabs - 2):
+            arrived = lax.optimization_barrier(arrived)
+        new_traces, new_helds = [], []
+        for col in range(width):
+            counts = groups if col == width - 1 else (0, 0)
+            trace, kept, *sums = call(
+                f"hop{hop}_{col}",
+                functools.partial(hop_kernel, shots, hop + 1, col, counts),
+                [(chunk, f32)] * 2 + [row_shape] * sum(c > 0 for c in counts),
+                [arrived[col], heavy, light, bottoms[col], traces[col], helds[col]]
+                + (sides if col == width - 1 else []),
+                flops=HOP_COSTS[hop],
+            )
+            new_traces.append(trace)
+            new_helds.append(kept)
+        traces, helds = new_traces, new_helds
+        if first_far - 1 <= hop < slabs - 2:
+            (mine,) = call(
+                f"gather{hop}",
+                functools.partial(gather_kernel, hop + 1),
+                [row_shape],
+                [*traces, *helds],
+                flops=GATHER_COST,
+            )
+        offs = ([sums.pop(0)] if groups[0] else []) + from_off
+        ons = ([sums.pop(0)] if groups[1] else []) + from_on
+    (whole,) = call("whole", functools.partial(gather_kernel, slabs), [row_shape], [*helds, *traces])
     (result,) = call(
         "inject",
         functools.partial(inject_kernel, shots, depth),
         [(solved.shape, f32)],
-        [coeffs, held, solved, *lefts, *rights],
+        [coeffs, solved, *helds, *offs, *ons],
         None,
-        [pltpu.VMEM((DEEP * COLS * PC * shots, length), f32)] * 2,
-    )
-    traces = trace.reshape(width, 1, length // PATCH, shots, size)
+        planes,
+    )
+    traces = whole.reshape(width, 1, length // PATCH, shots, size)
     return result.reshape(source.shape), traces
 
 

time: 65.5 us -> 61.5 us (0.939)
  the two profiles are of different devices: /device:TPU:255 before, /device:TPU:478 now
where the time goes in v3:
time: 61.5 us; the launch traced here: 61 us
  starting transfers between devices  24.4 us (40%)
  waiting for transfers between devices  22.1 us (36%)
  Pallas kernels  10.8 us (18%)
  local copies, waits for them, and re-layouts  2.49 us (4%)
  between operations  1.11 us (2%)
    ppermute x19, starting transfers between devices, both(): return lax.ppermute(x, ('slab', 'tile'), moves)  15.3 us
    ppermute x19, waiting for transfers between devices, both(): return lax.ppermute(x, ('slab', 'tile'), moves)  11.3 us
    ppermute x4, waiting for transfers between devices, exchange(): return (lax.ppermute(x, 'tile', off), lax.ppermute(x, 'tile', on))  10.9 us
    pallas_call x26, Pallas kernels, call(): pl.pallas_call(body, name=name, out_shape=[jax.ShapeDtypeStruct(shape, dt...  10.8 us
    ppermute x4, starting transfers between devices, exchange(): return (lax.ppermute(x, 'tile', off), lax.ppermute(x, 'tile', on))  9.14 us
    unnamed x10, local copies, waits for them, and re-layouts  2.49 us
  transfers between devices with their start and end apart: 23, of which 5 were waited for; matrix products, arithmetic and copies ran while one was open for 0% of the time, Pallas kernels for 12%

profile of v3, /device:TPU:478, one launch (start us, length us, event | category | flops | bytes accessed | tf_op | source)
XLA Modules:
  0.0 61.0 jit_solution(13992105536133826828)
XLA Ops:
  0.6 1.3 %pack_high.1.own.high = f32[592,128]{1,0:T(8,128)S(1)} custom-call(f32[1536,128]{1,0:T(8,128)} %bitcast.10, s32[16,128]{1,0:T(8,128)} %bitcast.13), custom_call_target="tpu_custom_call" | custom-call | flops 500000000 | tf_op jit(solution)/shard_map/pack_high/pallas_call | solution.py:34
  2.0 2.1 %collective-permute-start = (f32[592,128]{1,0:T(8,128)S(1)}, f32[592,128]{1,0:T(8,128)S(1)}, u32[]{:S(2)}, u32[]{:S(2)}) collective-permute-start(f32[592,128]{1,0:T(8,128)S(1)} %pack_high.1.own.high), channel_id=1, source_target_pairs={{1,2},{2,1},{3,4},{4,3},{5,6},{6,5},{7,8},{8,7},{9,10},{10,9},{11,... | collective-permute-start | bytes 909320 | tf_op jit(solution)/shard_map/ppermute | solution.py:508
  4.1 3.0 %collective-permute-start.1 = (f32[592,128]{1,0:T(8,128)S(1)}, f32[592,128]{1,0:T(8,128)S(1)}, u32[]{:S(2)}, u32[]{:S(2)}) collective-permute-start(f32[592,128]{1,0:T(8,128)S(1)} %pack_high.1.own.high), channel_id=1, source_target_pairs={{0,1},{1,0},{2,3},{3,2},{4,5},{5,4},{6,7},{7,6},{8,9},{9,8},{10,11... | collective-permute-start | bytes 909320 | tf_op jit(solution)/shard_map/ppermute | solution.py:508
  7.1 1.7 %copy-done = f32[2,1,2,384,384]{4,3,2,1,0:T(8,128)S(1)} copy-done((f32[2,1,2,384,384]{4,3,2,1,0:T(8,128)S(1)}, f32[2,1,2,384,384]{4,3,2,1,0:T(8,128)}, u32[]{:S(2)}) %copy-start) | copy-done | bytes 2359320
  9.7 3.6 %collective-permute-done.off.high_off = f32[592,128]{1,0:T(8,128)S(1)} collective-permute-done((f32[592,128]{1,0:T(8,128)S(1)}, f32[592,128]{1,0:T(8,128)S(1)}, u32[]{:S(2)}, u32[]{:S(2)}) %collective-permute-start) | collective-permute-done | bytes 303136 | tf_op jit(solution)/shard_map/ppermute | solution.py:508
  14.0 0.7 %collective-permute-start.4 = (f32[32,384]{1,0:T(8,128)S(1)}, f32[32,384]{1,0:T(8,128)S(1)}, u32[]{:S(2)}, u32[]{:S(2)}) collective-permute-start(f32[32,384]{1,0:T(8,128)S(1)} %get-tuple-element.62.refs_4_), channel_id=1, source_target_pairs={{0,64},{1,65},{2,66},{3,67},{4,68},{5,69},{6,70},{7,71},{8,72},{9,... | collective-permute-start | bytes 147464 | tf_op jit(solution)/shard_map/ppermute | solution.py:514
  14.6 0.7 %collective-permute-start.2 = (f32[32,384]{1,0:T(8,128)S(1)}, f32[32,384]{1,0:T(8,128)S(1)}, u32[]{:S(2)}, u32[]{:S(2)}) collective-permute-start(f32[32,384]{1,0:T(8,128)S(1)} %get-tuple-element.58.refs_4_), channel_id=1, source_target_pairs={{0,64},{1,65},{2,66},{3,67},{4,68},{5,69},{6,70},{7,71},{8,72},{9,... | collective-permute-start | bytes 147464 | tf_op jit(solution)/shard_map/ppermute | solution.py:514
  15.3 1.3 %bottom.1 = (f32[32,384]{1,0:T(8,128)S(1)}, f32[32,384]{1,0:T(8,128)S(1)}, f32[528,128]{1,0:T(8,128)S(1)}) custom-call(f32[592,128]{1,0:T(8,128)S(1)} %pack_high.1.own.high, f32[592,128]{1,0:T(8,128)S(1)} %collective-permute-done.off.high_off, f32[592,128]{1,0:T(8,128)S(1)} %collective-permute-done.1.on.high_on, f32[3,8]{1,0:T(4,128)S(1)} %copy-done.3, ...), custom_call_target="tpu_custom_call" | custom-call | flops 2000000000 | tf_op jit(solution)/shard_map/bottom/pallas_call | solution.py:34
  16.6 0.7 %collective-permute-start.5 = (f32[32,384]{1,0:T(8,128)S(1)}, f32[32,384]{1,0:T(8,128)S(1)}, u32[]{:S(2)}, u32[]{:S(2)}) collective-permute-start(f32[32,384]{1,0:T(8,128)S(1)} %get-tuple-element.65.refs_4_), channel_id=1, source_target_pairs={{64,128},{65,129},{66,130},{67,131},{68,132},{69,133},{70,134},{71... | collective-permute-start | bytes 147464 | tf_op jit(solution)/shard_map/ppermute | solution.py:514
  17.3 0.8 %collective-permute-start.3 = (f32[32,384]{1,0:T(8,128)S(1)}, f32[32,384]{1,0:T(8,128)S(1)}, u32[]{:S(2)}, u32[]{:S(2)}) collective-permute-start(f32[32,384]{1,0:T(8,128)S(1)} %get-tuple-element.61.refs_4_), channel_id=1, source_target_pairs={{64,128},{65,129},{66,130},{67,131},{68,132},{69,133},{70,134},{71... | collective-permute-start | bytes 147464 | tf_op jit(solution)/shard_map/ppermute | solution.py:514
  18.7 2.1 %collective-permute-start.10 = (f32[960,128]{1,0:T(8,128)S(1)}, f32[960,128]{1,0:T(8,128)S(1)}, u32[]{:S(2)}, u32[]{:S(2)}) collective-permute-start(f32[960,128]{1,0:T(8,128)S(1)} %pack_low.1.low), channel_id=1, source_target_pairs={{1,2},{2,1},{3,4},{4,3},{5,6},{6,5},{7,8},{8,7},{9,10},{10,9},{11,... | collective-permute-start | bytes 1474568 | tf_op jit(solution)/shard_map/ppermute | solution.py:508
  20.8 1.9 %collective-permute-start.11 = (f32[960,128]{1,0:T(8,128)S(1)}, f32[960,128]{1,0:T(8,128)S(1)}, u32[]{:S(2)}, u32[]{:S(2)}) collective-permute-start(f32[960,128]{1,0:T(8,128)S(1)} %pack_low.1.low), channel_id=1, source_target_pairs={{0,1},{1,0},{2,3},{3,2},{4,5},{5,4},{6,7},{7,6},{8,9},{9,8},{10,11... | collective-permute-start | bytes 1474568 | tf_op jit(solution)/shard_map/ppermute | solution.py:508
  22.8 0.7 %collective-permute-start.8 = (f32[32,384]{1,0:T(8,128)S(1)}, f32[32,384]{1,0:T(8,128)S(1)}, u32[]{:S(2)}, u32[]{:S(2)}) collective-permute-start(f32[32,384]{1,0:T(8,128)S(1)} %get-tuple-element.73.refs_4_), channel_id=1, source_target_pairs={{128,192},{129,193},{130,194},{131,195},{132,196},{133,197},{134,1... | collective-permute-start | bytes 147464 | tf_op jit(solution)/shard_map/ppermute | solution.py:514
  23.5 0.7 %collective-permute-start.6 = (f32[32,384]{1,0:T(8,128)S(1)}, f32[32,384]{1,0:T(8,128)S(1)}, u32[]{:S(2)}, u32[]{:S(2)}) collective-permute-start(f32[32,384]{1,0:T(8,128)S(1)} %get-tuple-element.68.refs_4_), channel_id=1, source_target_pairs={{128,192},{129,193},{130,194},{131,195},{132,196},{133,197},{134,1... | collective-permute-start | bytes 147464 | tf_op jit(solution)/shard_map/ppermute | solution.py:514
  24.2 0.7 %collective-permute-start.9 = (f32[32,384]{1,0:T(8,128)S(1)}, f32[32,384]{1,0:T(8,128)S(1)}, u32[]{:S(2)}, u32[]{:S(2)}) collective-permute-start(f32[32,384]{1,0:T(8,128)S(1)} %get-tuple-element.75.refs_4_), channel_id=1, source_target_pairs={{192,256},{193,257},{194,258},{195,259},{196,260},{197,261},{198,2... | collective-permute-start | bytes 147464 | tf_op jit(solution)/shard_map/ppermute | solution.py:514
  24.9 0.7 %collective-permute-start.7 = (f32[32,384]{1,0:T(8,128)S(1)}, f32[32,384]{1,0:T(8,128)S(1)}, u32[]{:S(2)}, u32[]{:S(2)}) collective-permute-start(f32[32,384]{1,0:T(8,128)S(1)} %get-tuple-element.70.refs_4_), channel_id=1, source_target_pairs={{192,256},{193,257},{194,258},{195,259},{196,260},{197,261},{198,2... | collective-permute-start | bytes 147464 | tf_op jit(solution)/shard_map/ppermute | solution.py:514
  25.6 7.2 %collective-permute-done.10.low_off = f32[960,128]{1,0:T(8,128)S(1)} collective-permute-done((f32[960,128]{1,0:T(8,128)S(1)}, f32[960,128]{1,0:T(8,128)S(1)}, u32[]{:S(2)}, u32[]{:S(2)}) %collective-permute-start.10) | collective-permute-done | bytes 491552 | tf_op jit(solution)/shard_map/ppermute | solution.py:508
  32.8 3.6 %full.1.base = f32[1536,128]{1,0:T(8,128)S(1)} custom-call(f32[528,128]{1,0:T(8,128)S(1)} %get-tuple-element.57.coeffs, f32[960,128]{1,0:T(8,128)S(1)} %pack_low.1.low, f32[960,128]{1,0:T(8,128)S(1)} %collective-permute-done.10.low_off, f32[960,128]{1,0:T(8,128)S(1)} %collective-permute-done.11.low_on, f32[592,128]{1,0:T(8,128)S(1)} %pack_high.1.own.high, ...), custom_call_target="tpu_custom_call" | custom-call | flops 5000000000 | tf_op jit(solution)/shard_map/full/pallas_call | solution.py:34
  36.5 0.7 %collective-permute-start.15 = (f32[32,384]{1,0:T(8,128)S(1)}, f32[32,384]{1,0:T(8,128)S(1)}, u32[]{:S(2)}, u32[]{:S(2)}) collective-permute-start(f32[32,384]{1,0:T(8,128)S(1)} %get-tuple-element.90.refs_4_.refs_1_), channel_id=1, source_target_pairs={{256,320},{257,321},{258,322},{259,323},{260,324},{261,325},{262,3... | collective-permute-start | bytes 147464 | tf_op jit(solution)/shard_map/ppermute | solution.py:514
  37.2 0.7 %collective-permute-start.12 = (f32[32,384]{1,0:T(8,128)S(1)}, f32[32,384]{1,0:T(8,128)S(1)}, u32[]{:S(2)}, u32[]{:S(2)}) collective-permute-start(f32[32,384]{1,0:T(8,128)S(1)} %get-tuple-element.83.refs_4_.refs_0_), channel_id=1, source_target_pairs={{256,320},{257,321},{258,322},{259,323},{260,324},{261,325},{262,3... | collective-permute-start | bytes 147464 | tf_op jit(solution)/shard_map/ppermute | solution.py:514
  37.9 0.7 %collective-permute-start.17 = (f32[64,384]{1,0:T(8,128)S(1)}, f32[64,384]{1,0:T(8,128)S(1)}, u32[]{:S(2)}, u32[]{:S(2)}) collective-permute-start(f32[64,384]{1,0:T(8,128)S(1)} %gather3.1), channel_id=1, source_target_pairs={{257,322},{258,321},{259,324},{260,323},{261,326},{262,325},{263,3... | collective-permute-start | bytes 294920 | tf_op jit(solution)/shard_map/ppermute | solution.py:514
  38.6 0.7 %collective-permute-start.16 = (f32[32,384]{1,0:T(8,128)S(1)}, f32[32,384]{1,0:T(8,128)S(1)}, u32[]{:S(2)}, u32[]{:S(2)}) collective-permute-start(f32[32,384]{1,0:T(8,128)S(1)} %get-tuple-element.92.refs_4_.refs_1_), channel_id=1, source_target_pairs={{320,384},{321,385},{322,386},{323,387},{324,388},{325,389},{326,3... | collective-permute-start | bytes 147464 | tf_op jit(solution)/shard_map/ppermute | solution.py:514
  40.0 0.7 %collective-permute-start.19 = (f32[64,384]{1,0:T(8,128)S(1)}, f32[64,384]{1,0:T(8,128)S(1)}, u32[]{:S(2)}, u32[]{:S(2)}) collective-permute-start(f32[64,384]{1,0:T(8,128)S(1)} %gather4.1), channel_id=1, source_target_pairs={{321,386},{322,385},{323,388},{324,387},{325,390},{326,389},{327,3... | collective-permute-start | bytes 294920 | tf_op jit(solution)/shard_map/ppermute | solution.py:514
  40.7 0.7 %collective-permute-start.20 = (f32[64,384]{1,0:T(8,128)S(1)}, f32[64,384]{1,0:T(8,128)S(1)}, u32[]{:S(2)}, u32[]{:S(2)}) collective-permute-start(f32[64,384]{1,0:T(8,128)S(1)} %gather4.1), channel_id=1, source_target_pairs={{320,385},{321,384},{322,387},{323,386},{324,389},{325,388},{326,3... | collective-permute-start | bytes 294920 | tf_op jit(solution)/shard_map/ppermute | solution.py:514
  41.4 1.3 %collective-permute-start.18 = (f32[32,384]{1,0:T(8,128)S(1)}, f32[32,384]{1,0:T(8,128)S(1)}, u32[]{:S(2)}, u32[]{:S(2)}) collective-permute-start(f32[32,384]{1,0:T(8,128)S(1)} %get-tuple-element.94.refs_4_.refs_1_), channel_id=1, source_target_pairs={{384,448},{385,449},{386,450},{387,451},{388,452},{389,453},{390,4... | collective-permute-start | bytes 147464 | tf_op jit(solution)/shard_map/ppermute | solution.py:514
  42.8 1.3 %collective-permute-start.14 = (f32[32,384]{1,0:T(8,128)S(1)}, f32[32,384]{1,0:T(8,128)S(1)}, u32[]{:S(2)}, u32[]{:S(2)}) collective-permute-start(f32[32,384]{1,0:T(8,128)S(1)} %get-tuple-element.87.refs_4_.refs_0_), channel_id=1, source_target_pairs={{384,448},{385,449},{386,450},{387,451},{388,452},{389,453},{390,4... | collective-permute-start | bytes 147464 | tf_op jit(solution)/shard_map/ppermute | solution.py:514
  44.1 1.3 %collective-permute-start.21 = (f32[64,384]{1,0:T(8,128)S(1)}, f32[64,384]{1,0:T(8,128)S(1)}, u32[]{:S(2)}, u32[]{:S(2)}) collective-permute-start(f32[64,384]{1,0:T(8,128)S(1)} %gather5.1), channel_id=1, source_target_pairs={{385,450},{386,449},{387,452},{388,451},{389,454},{390,453},{391,4... | collective-permute-start | bytes 294920 | tf_op jit(solution)/shard_map/ppermute | solution.py:514
  45.4 7.9 %collective-permute-done.18.refs_0_ = f32[32,384]{1,0:T(8,128)S(1)} collective-permute-done((f32[32,384]{1,0:T(8,128)S(1)}, f32[32,384]{1,0:T(8,128)S(1)}, u32[]{:S(2)}, u32[]{:S(2)}) %collective-permute-start.18) | collective-permute-done | bytes 49184 | tf_op jit(solution)/shard_map/ppermute | solution.py:514
  53.3 1.3 %collective-permute-start.22 = (f32[64,384]{1,0:T(8,128)S(1)}, f32[64,384]{1,0:T(8,128)S(1)}, u32[]{:S(2)}, u32[]{:S(2)}) collective-permute-start(f32[64,384]{1,0:T(8,128)S(1)} %gather5.1), channel_id=1, source_target_pairs={{384,449},{385,448},{386,451},{387,450},{388,453},{389,452},{390,4... | collective-permute-start | bytes 294920 | tf_op jit(solution)/shard_map/ppermute | solution.py:514
  55.5 0.7 %whole.1 = f32[64,384]{1,0:T(8,128)} custom-call(f32[32,384]{1,0:T(8,128)S(1)} %get-tuple-element.97.refs_0_, f32[32,384]{1,0:T(8,128)S(1)} %get-tuple-element.101.refs_1_, f32[32,384]{1,0:T(8,128)S(1)} %get-tuple-element.104.refs_2_, f32[32,384]{1,0:T(8,128)S(1)} %get-tuple-element.105.refs_3_), custom_call_target="tpu_custom_call" | custom-call | flops 500000000 | tf_op jit(solution)/shard_map/whole/pallas_call | solution.py:34
  56.2 3.0 %collective-permute-done.22.refs_5_ = f32[64,384]{1,0:T(8,128)S(1)} collective-permute-done((f32[64,384]{1,0:T(8,128)S(1)}, f32[64,384]{1,0:T(8,128)S(1)}, u32[]{:S(2)}, u32[]{:S(2)}) %collective-permute-start.22) | collective-permute-done | bytes 98336 | tf_op jit(solution)/shard_map/ppermute | solution.py:514
  59.2 1.8 %inject.1 = f32[1536,128]{1,0:T(8,128)} custom-call(f32[528,128]{1,0:T(8,128)S(1)} %get-tuple-element.57.coeffs, f32[1536,128]{1,0:T(8,128)S(1)} %full.1.base, f32[32,384]{1,0:T(8,128)S(1)} %get-tuple-element.97.refs_0_, f32[32,384]{1,0:T(8,128)S(1)} %get-tuple-element.101.refs_1_, f32[64,384]{1,0:T(8,128)S(1)} %get-tuple-element.102.refs_2_, ...), custom_call_target="tpu_custom_call" | custom-call | flops 500000000 | tf_op jit(solution)/shard_map/inject/pallas_call | solution.py:34
  (50 shorter events, 4.1 us)
Async XLA Ops:
  2.0 11.4 %collective-permute-start = (f32[592,128]{1,0:T(8,128)S(1)}, f32[592,128]{1,0:T(8,128)S(1)}, u32[]{:S(2)}, u32[]{:S(2)}) collective-permute-start(f32[592,128]{1,0:T(8,128)S(1)} %pack_high.1.own.high), channel_id=1, source_target_pairs={{1,2},{2,1},{3,4},{4,3},{5,6},{6,5},{7,8},{8,7},{9,10},{10,9},{11,... | collective-permute-start | bytes 909320 | tf_op jit(solution)/shard_map/ppermute | solution.py:508
  4.1 9.3 %collective-permute-start.1 = (f32[592,128]{1,0:T(8,128)S(1)}, f32[592,128]{1,0:T(8,128)S(1)}, u32[]{:S(2)}, u32[]{:S(2)}) collective-permute-start(f32[592,128]{1,0:T(8,128)S(1)} %pack_high.1.own.high), channel_id=1, source_target_pairs={{0,1},{1,0},{2,3},{3,2},{4,5},{5,4},{6,7},{7,6},{8,9},{9,8},{10,11... | collective-permute-start | bytes 909320 | tf_op jit(solution)/shard_map/ppermute | solution.py:508
  7.1 1.7 %copy-start = (f32[2,1,2,384,384]{4,3,2,1,0:T(8,128)S(1)}, f32[2,1,2,384,384]{4,3,2,1,0:T(8,128)}, u32[]{:S(2)}) copy-start(f32[2,1,2,384,384]{4,3,2,1,0:T(8,128)} %param.10) | copy-start | bytes 7077892
  8.8 0.9 %copy-start.1 = (f32[2,2,16,384]{3,2,1,0:T(8,128)S(1)}, f32[2,2,16,384]{3,2,1,0:T(8,128)}, u32[]{:S(2)}) copy-start(f32[2,2,16,384]{3,2,1,0:T(8,128)} %param.11) | copy-start | bytes 294916
  9.7 3.7 %copy-start.3 = (f32[3,8]{1,0:T(4,128)S(1)}, f32[3,8]{1,0:T(4,128)}, u32[]{:S(2)}) copy-start(f32[3,8]{1,0:T(4,128)} %table.3) | copy-start | bytes 292
  9.7 3.7 %copy-start.4 = (s32[1,2]{1,0:T(1,128)S(1)}, s32[1,2]{1,0:T(1,128)}, u32[]{:S(2)}) copy-start(s32[1,2]{1,0:T(1,128)} %widths.3) | copy-start | bytes 28
  14.0 2.6 %collective-permute-start.4 = (f32[32,384]{1,0:T(8,128)S(1)}, f32[32,384]{1,0:T(8,128)S(1)}, u32[]{:S(2)}, u32[]{:S(2)}) collective-permute-start(f32[32,384]{1,0:T(8,128)S(1)} %get-tuple-element.62.refs_4_), channel_id=1, source_target_pairs={{0,64},{1,65},{2,66},{3,67},{4,68},{5,69},{6,70},{7,71},{8,72},{9,... | collective-permute-start | bytes 147464 | tf_op jit(solution)/shard_map/ppermute | solution.py:514
  14.6 2.7 %collective-permute-start.2 = (f32[32,384]{1,0:T(8,128)S(1)}, f32[32,384]{1,0:T(8,128)S(1)}, u32[]{:S(2)}, u32[]{:S(2)}) collective-permute-start(f32[32,384]{1,0:T(8,128)S(1)} %get-tuple-element.58.refs_4_), channel_id=1, source_target_pairs={{0,64},{1,65},{2,66},{3,67},{4,68},{5,69},{6,70},{7,71},{8,72},{9,... | collective-permute-start | bytes 147464 | tf_op jit(solution)/shard_map/ppermute | solution.py:514
  16.6 6.1 %collective-permute-start.5 = (f32[32,384]{1,0:T(8,128)S(1)}, f32[32,384]{1,0:T(8,128)S(1)}, u32[]{:S(2)}, u32[]{:S(2)}) collective-permute-start(f32[32,384]{1,0:T(8,128)S(1)} %get-tuple-element.65.refs_4_), channel_id=1, source_target_pairs={{64,128},{65,129},{66,130},{67,131},{68,132},{69,133},{70,134},{71... | collective-permute-start | bytes 147464 | tf_op jit(solution)/shard_map/ppermute | solution.py:514
  17.3 1.1 %copy-start.2 = (f32[16,2,3,2,8,128]{5,4,3,2,1,0:T(8,128)S(1)}, f32[16,2,3,2,8,128]{5,4,3,2,1,0:T(8,128)}, u32[]{:S(2)}) copy-start(f32[16,2,3,2,8,128]{5,4,3,2,1,0:T(8,128)} %param.6) | copy-start | bytes 2359300
  17.3 5.4 %collective-permute-start.3 = (f32[32,384]{1,0:T(8,128)S(1)}, f32[32,384]{1,0:T(8,128)S(1)}, u32[]{:S(2)}, u32[]{:S(2)}) collective-permute-start(f32[32,384]{1,0:T(8,128)S(1)} %get-tuple-element.61.refs_4_), channel_id=1, source_target_pairs={{64,128},{65,129},{66,130},{67,131},{68,132},{69,133},{70,134},{71... | collective-permute-start | bytes 147464 | tf_op jit(solution)/shard_map/ppermute | solution.py:514
  18.7 14.1 %collective-permute-start.10 = (f32[960,128]{1,0:T(8,128)S(1)}, f32[960,128]{1,0:T(8,128)S(1)}, u32[]{:S(2)}, u32[]{:S(2)}) collective-permute-start(f32[960,128]{1,0:T(8,128)S(1)} %pack_low.1.low), channel_id=1, source_target_pairs={{1,2},{2,1},{3,4},{4,3},{5,6},{6,5},{7,8},{8,7},{9,10},{10,9},{11,... | collective-permute-start | bytes 1474568 | tf_op jit(solution)/shard_map/ppermute | solution.py:508
  20.8 12.0 %collective-permute-start.11 = (f32[960,128]{1,0:T(8,128)S(1)}, f32[960,128]{1,0:T(8,128)S(1)}, u32[]{:S(2)}, u32[]{:S(2)}) collective-permute-start(f32[960,128]{1,0:T(8,128)S(1)} %pack_low.1.low), channel_id=1, source_target_pairs={{0,1},{1,0},{2,3},{3,2},{4,5},{5,4},{6,7},{7,6},{8,9},{9,8},{10,11... | collective-permute-start | bytes 1474568 | tf_op jit(solution)/shard_map/ppermute | solution.py:508
  22.8 1.4 %collective-permute-start.8 = (f32[32,384]{1,0:T(8,128)S(1)}, f32[32,384]{1,0:T(8,128)S(1)}, u32[]{:S(2)}, u32[]{:S(2)}) collective-permute-start(f32[32,384]{1,0:T(8,128)S(1)} %get-tuple-element.73.refs_4_), channel_id=1, source_target_pairs={{128,192},{129,193},{130,194},{131,195},{132,196},{133,197},{134,1... | collective-permute-start | bytes 147464 | tf_op jit(solution)/shard_map/ppermute | solution.py:514
  23.5 1.4 %collective-permute-start.6 = (f32[32,384]{1,0:T(8,128)S(1)}, f32[32,384]{1,0:T(8,128)S(1)}, u32[]{:S(2)}, u32[]{:S(2)}) collective-permute-start(f32[32,384]{1,0:T(8,128)S(1)} %get-tuple-element.68.refs_4_), channel_id=1, source_target_pairs={{128,192},{129,193},{130,194},{131,195},{132,196},{133,197},{134,1... | collective-permute-start | bytes 147464 | tf_op jit(solution)/shard_map/ppermute | solution.py:514
  24.2 12.2 %collective-permute-start.9 = (f32[32,384]{1,0:T(8,128)S(1)}, f32[32,384]{1,0:T(8,128)S(1)}, u32[]{:S(2)}, u32[]{:S(2)}) collective-permute-start(f32[32,384]{1,0:T(8,128)S(1)} %get-tuple-element.75.refs_4_), channel_id=1, source_target_pairs={{192,256},{193,257},{194,258},{195,259},{196,260},{197,261},{198,2... | collective-permute-start | bytes 147464 | tf_op jit(solution)/shard_map/ppermute | solution.py:514
  24.9 11.5 %collective-permute-start.7 = (f32[32,384]{1,0:T(8,128)S(1)}, f32[32,384]{1,0:T(8,128)S(1)}, u32[]{:S(2)}, u32[]{:S(2)}) collective-permute-start(f32[32,384]{1,0:T(8,128)S(1)} %get-tuple-element.70.refs_4_), channel_id=1, source_target_pairs={{192,256},{193,257},{194,258},{195,259},{196,260},{197,261},{198,2... | collective-permute-start | bytes 147464 | tf_op jit(solution)/shard_map/ppermute | solution.py:514
  36.5 2.1 %collective-permute-start.15 = (f32[32,384]{1,0:T(8,128)S(1)}, f32[32,384]{1,0:T(8,128)S(1)}, u32[]{:S(2)}, u32[]{:S(2)}) collective-permute-start(f32[32,384]{1,0:T(8,128)S(1)} %get-tuple-element.90.refs_4_.refs_1_), channel_id=1, source_target_pairs={{256,320},{257,321},{258,322},{259,323},{260,324},{261,325},{262,3... | collective-permute-start | bytes 147464 | tf_op jit(solution)/shard_map/ppermute | solution.py:514
  37.2 2.1 %collective-permute-start.12 = (f32[32,384]{1,0:T(8,128)S(1)}, f32[32,384]{1,0:T(8,128)S(1)}, u32[]{:S(2)}, u32[]{:S(2)}) collective-permute-start(f32[32,384]{1,0:T(8,128)S(1)} %get-tuple-element.83.refs_4_.refs_0_), channel_id=1, source_target_pairs={{256,320},{257,321},{258,322},{259,323},{260,324},{261,325},{262,3... | collective-permute-start | bytes 147464 | tf_op jit(solution)/shard_map/ppermute | solution.py:514
  37.9 3.5 %collective-permute-start.17 = (f32[64,384]{1,0:T(8,128)S(1)}, f32[64,384]{1,0:T(8,128)S(1)}, u32[]{:S(2)}, u32[]{:S(2)}) collective-permute-start(f32[64,384]{1,0:T(8,128)S(1)} %gather3.1), channel_id=1, source_target_pairs={{257,322},{258,321},{259,324},{260,323},{261,326},{262,325},{263,3... | collective-permute-start | bytes 294920 | tf_op jit(solution)/shard_map/ppermute | solution.py:514
  38.6 2.8 %collective-permute-start.16 = (f32[32,384]{1,0:T(8,128)S(1)}, f32[32,384]{1,0:T(8,128)S(1)}, u32[]{:S(2)}, u32[]{:S(2)}) collective-permute-start(f32[32,384]{1,0:T(8,128)S(1)} %get-tuple-element.92.refs_4_.refs_1_), channel_id=1, source_target_pairs={{320,384},{321,385},{322,386},{323,387},{324,388},{325,389},{326,3... | collective-permute-start | bytes 147464 | tf_op jit(solution)/shard_map/ppermute | solution.py:514
  39.3 3.4 %collective-permute-start.13 = (f32[32,384]{1,0:T(8,128)S(1)}, f32[32,384]{1,0:T(8,128)S(1)}, u32[]{:S(2)}, u32[]{:S(2)}) collective-permute-start(f32[32,384]{1,0:T(8,128)S(1)} %get-tuple-element.85.refs_4_.refs_0_), channel_id=1, source_target_pairs={{320,384},{321,385},{322,386},{323,387},{324,388},{325,389},{326,3... | collective-permute-start | bytes 147464 | tf_op jit(solution)/shard_map/ppermute | solution.py:514
  40.0 15.2 %collective-permute-start.19 = (f32[64,384]{1,0:T(8,128)S(1)}, f32[64,384]{1,0:T(8,128)S(1)}, u32[]{:S(2)}, u32[]{:S(2)}) collective-permute-start(f32[64,384]{1,0:T(8,128)S(1)} %gather4.1), channel_id=1, source_target_pairs={{321,386},{322,385},{323,388},{324,387},{325,390},{326,389},{327,3... | collective-permute-start | bytes 294920 | tf_op jit(solution)/shard_map/ppermute | solution.py:514
  40.7 14.5 %collective-permute-start.20 = (f32[64,384]{1,0:T(8,128)S(1)}, f32[64,384]{1,0:T(8,128)S(1)}, u32[]{:S(2)}, u32[]{:S(2)}) collective-permute-start(f32[64,384]{1,0:T(8,128)S(1)} %gather4.1), channel_id=1, source_target_pairs={{320,385},{321,384},{322,387},{323,386},{324,389},{325,388},{326,3... | collective-permute-start | bytes 294920 | tf_op jit(solution)/shard_map/ppermute | solution.py:514
  41.4 11.9 %collective-permute-start.18 = (f32[32,384]{1,0:T(8,128)S(1)}, f32[32,384]{1,0:T(8,128)S(1)}, u32[]{:S(2)}, u32[]{:S(2)}) collective-permute-start(f32[32,384]{1,0:T(8,128)S(1)} %get-tuple-element.94.refs_4_.refs_1_), channel_id=1, source_target_pairs={{384,448},{385,449},{386,450},{387,451},{388,452},{389,453},{390,4... | collective-permute-start | bytes 147464 | tf_op jit(solution)/shard_map/ppermute | solution.py:514
  42.8 12.1 %collective-permute-start.14 = (f32[32,384]{1,0:T(8,128)S(1)}, f32[32,384]{1,0:T(8,128)S(1)}, u32[]{:S(2)}, u32[]{:S(2)}) collective-permute-start(f32[32,384]{1,0:T(8,128)S(1)} %get-tuple-element.87.refs_4_.refs_0_), channel_id=1, source_target_pairs={{384,448},{385,449},{386,450},{387,451},{388,452},{389,453},{390,4... | collective-permute-start | bytes 147464 | tf_op jit(solution)/shard_map/ppermute | solution.py:514
  44.1 12.1 %collective-permute-start.21 = (f32[64,384]{1,0:T(8,128)S(1)}, f32[64,384]{1,0:T(8,128)S(1)}, u32[]{:S(2)}, u32[]{:S(2)}) collective-permute-start(f32[64,384]{1,0:T(8,128)S(1)} %gather5.1), channel_id=1, source_target_pairs={{385,450},{386,449},{387,452},{388,451},{389,454},{390,453},{391,4... | collective-permute-start | bytes 294920 | tf_op jit(solution)/shard_map/ppermute | solution.py:514
  53.3 5.9 %collective-permute-start.22 = (f32[64,384]{1,0:T(8,128)S(1)}, f32[64,384]{1,0:T(8,128)S(1)}, u32[]{:S(2)}, u32[]{:S(2)}) collective-permute-start(f32[64,384]{1,0:T(8,128)S(1)} %gather5.1), channel_id=1, source_target_pairs={{384,449},{385,448},{386,451},{387,450},{388,453},{389,452},{390,4... | collective-permute-start | bytes 294920 | tf_op jit(solution)/shard_map/ppermute | solution.py:514

commit v4 on v3

--- a/solution.py
+++ b/solution.py
@@ -23,11 +23,11 @@
 ANY = pl.BlockSpec(memory_space=pl.ANY)
 MIB = 1024 * 1024
 LIMIT = 6 * MIB
-HOP_COST = 2_000_000_000
-LOW_COST = 2000000000.0
-HOP_COSTS = (2000000000.0, 2000000000.0, 2000000000.0, 2000000000.0, 1000000.0, 1000000.0, 2000000000.0)
-GATHER_COST = 2000000000.0
-FULL_COST = 5_000_000_000
+HOP_COST = 2e9
+LOW_COST = 2e9
+HOP_COSTS = (2e9, 2e9, 2e9, 2e9, 1e6, 1e6, 2e9)
+GATHER_COST = 2e9
+FULL_COST = 5e9
 
 
 def call(name, body, outs, operands, specs=None, scratch=(), flops=5e8, limit=LIMIT):
@@ -175,8 +175,8 @@
     return jnp.where(lane == length - 1, 0.0, pltpu.roll(x, length - 1, 1))
 
 
-def fill_coeffs(coeffs, soils, table, widths, depth, layers):
-    shape = soils[0].shape
+def consts_kernel(depth, layers, table, widths, out):
+    shape = (depth, out.shape[1])
     level = lax.broadcasted_iota(jnp.int32, shape, 0)
     top, bottom = widths[0, 0], widths[0, 1]
     zero = jnp.zeros(shape, jnp.int32)
@@ -184,13 +184,23 @@
     lower = jnp.maximum(bottom - (depth - 1 - level), 0).astype(jnp.float32) / (
         zero + bottom
     ).astype(jnp.float32)
-    sigma = SIGMA_PEAK * upper * upper + SIGMA_PEAK * lower * lower
+    out[pl.ds(0, depth), :] = SIGMA_PEAK * upper * upper + SIGMA_PEAK * lower * lower
+    for row in range(3):
+        for layer in range(layers):
+            value = jnp.full((1, out.shape[1]), table[row, layer], jnp.float32)
+            out[pl.ds(depth + row * layers + layer, 1), :] = value
+
+
+def fill_coeffs(coeffs, soils, consts, depth, layers):
+    shape = soils[0].shape
+    sigma = consts[pl.ds(0, depth), :]
     for col, soil in enumerate(soils):
         rows = []
         for row in range(3):
             picked = jnp.zeros(shape, jnp.float32)
             for layer in range(layers):
-                picked = jnp.where(soil == layer + 1.0, table[row, layer], picked)
+                value = consts[pl.ds(depth + row * layers + layer, 1), :]
+                picked = jnp.where(soil == layer + 1.0, value, picked)
             rows.append(picked)
         shear, lame, kappa = rows
         stiff = lame + shear
@@ -237,10 +247,10 @@
     return (z * COLS + col) * PC + pc
 
 
-def bottom_kernel(shots, depth, layers, first_only, own, off, on, table, widths, start, *refs):
+def bottom_kernel(shots, depth, layers, first_only, own, off, on, consts, start, *refs):
     bottoms, coeffs, v1, v2 = refs[:WIDTH], *refs[WIDTH:]
     work = functools.partial(
-        bottom_planes, shots, depth, layers, own, off, on, table, widths, start, bottoms, coeffs, v1, v2
+        bottom_planes, shots, depth, layers, own, off, on, consts, start, bottoms, coeffs, v1, v2
     )
     if not first_only:
         work()
@@ -254,14 +264,14 @@
             ref[...] = jnp.zeros(ref.shape, jnp.float32)
 
 
-def bottom_planes(shots, depth, layers, own, off, on, table, widths, start, bottoms, coeffs, v1, v2):
+def bottom_planes(shots, depth, layers, own, off, on, consts, start, bottoms, coeffs, v1, v2):
     at = DEEP * WIDTH * PC * shots
     soils = []
     for col in range(COLS):
         which, place = tile_of(col)
         where = pl.ds(at + place * depth, depth)
         soils.append(pick(which, own, off, on, lambda ref: ref[where, :]))
-    fill_coeffs(coeffs, soils, table, widths, depth, layers)
+    fill_coeffs(coeffs, soils, consts, depth, layers)
     base = depth - DEEP
 
     def block(ref, number):
@@ -306,7 +316,7 @@
                 bottoms[x - HALO][pl.ds(patch * shots, shots), lanes] = both[patch] + given
 
 
-def full_kernel(shots, depth, coeffs, low, low_off, low_on, high, high_off, high_on, out, v1, v2):
+def full_kernel(shots, depth, coeffs, low, low_on, low_off, high, high_off, high_on, out, v1, v2):
     stride = PC * WIDTH * depth
     lows, highs = (low, low_off, low_on), (high, high_off, high_on)
     plane = COLS * PC * shots
@@ -365,10 +375,12 @@
     lax.fori_loop(0, depth, last, 0)
 
 
-def inject_kernel(shots, depth, coeffs, base, *refs):
-    own, halos, (out, v1, v2) = refs[:WIDTH], refs[WIDTH:-3], refs[-3:]
-    half = len(halos) // 2
-    off, on = halos[:half], halos[half:]
+def inject_kernel(shots, depth, offs, coeffs, base, *refs):
+    own, traces, halos = refs[:WIDTH], refs[WIDTH : 2 * WIDTH], refs[2 * WIDTH : -4]
+    out, whole, v1, v2 = refs[-4:]
+    for col, trace in enumerate(traces):
+        whole[pl.ds(col * trace.shape[0], trace.shape[0]), :] = trace[...]
+    off, on = halos[:offs], halos[offs:]
     stride = PC * WIDTH * depth
 
     def block(ref, number):
@@ -504,9 +516,6 @@
     off = [p for t in range(1, tiles - 1, 2) for p in ((t, t + 1), (t + 1, t))]
     on = [p for t in range(0, tiles - 1, 2) for p in ((t, t + 1), (t + 1, t))]
 
-    def exchange(x):
-        return lax.ppermute(x, "tile", off), lax.ppermute(x, "tile", on)
-
     def pairs(slab_moves, tile_moves):
         return [(a * tiles + t, b * tiles + u) for a, b in slab_moves for t, u in tile_moves]
 
@@ -526,7 +535,7 @@
             pltpu.SemaphoreType.DMA((2,)),
         ],
     )
-    high_off, high_on = exchange(high)
+    high_off, high_on = lax.ppermute(high, "tile", off), lax.ppermute(high, "tile", on)
 
     blocks = interface_blocks.reshape(chains * size, size)
     heavy, light = call("split", split_kernel, [(blocks.shape, bf16)] * 2, [blocks])
@@ -541,14 +550,20 @@
     )
     table_shape = (COLS * COEFFS * depth, length)
     planes = [pltpu.VMEM((DEEP * COLS * PC * shots, length), f32)] * 2
-    near = [high, high_off, high_on, soil_table, pml_width, start]
-    near_specs = [VMEM, VMEM, VMEM, SMEM, SMEM, VMEM]
+    (consts,) = call(
+        "consts",
+        functools.partial(consts_kernel, depth, layers),
+        [((depth + 3 * layers, length), f32)],
+        [soil_table, pml_width],
+        [SMEM, SMEM],
+    )
+    near = [high, high_off, high_on, consts, start]
     traces = call(
         "first",
         functools.partial(bottom_kernel, shots, depth, layers, True),
         [(chunk, f32)] * width,
         near,
-        near_specs,
+        None,
         [pltpu.VMEM(table_shape, f32)] + planes,
     )
     *bottoms, coeffs = call(
@@ -556,7 +571,7 @@
         functools.partial(bottom_kernel, shots, depth, layers, False),
         [(chunk, f32)] * width + [(table_shape, f32)],
         near,
-        near_specs,
+        None,
         planes,
         flops=HOP_COST,
     )
@@ -567,13 +582,21 @@
         arrived = [both(trace, step) for trace in traces]
         groups = (len(offs), len(ons))
         sides = [*offs, *ons]
+        if hop in (1, slabs - 2):
+            arrived = lax.optimization_barrier(arrived)
         from_off, from_on = [], []
         if hop >= first_far:
             same = range(hop) if hop == first_far else [first_far] if hop == first_far + 1 else []
             from_off = [both(mine, pairs([(hop, hop + 1)] + [(s, s) for s in same], off))]
-        if hop > first_far:
-            same = range(hop) if hop == slabs - 2 else []
-            from_on = [both(mine, pairs([(hop, hop + 1)] + [(s, s) for s in same], on))]
+        if hop == slabs - 2:
+            (entered,) = call(
+                "entered",
+                functools.partial(gather_kernel, hop + 1),
+                [row_shape],
+                [*arrived, *helds],
+                flops=GATHER_COST,
+            )
+            from_on = [lax.ppermute(entered, "tile", on)]
         if hop == 1:
             again, _ = lax.optimization_barrier((src, traces))
             (low,) = call(
@@ -583,9 +606,9 @@
                 [again],
                 flops=LOW_COST,
             )
-            low_off, low_on = exchange(low)
+            low_on, low_off = lax.ppermute(low, "tile", on), lax.ppermute(low, "tile", off)
         if hop == first_far - 1:
-            lows, _ = lax.optimization_barrier(((low, low_off, low_on), traces))
+            lows, _ = lax.optimization_barrier(((low, low_on, low_off), traces))
             (solved,) = call(
                 "full",
                 functools.partial(full_kernel, shots, depth),
@@ -596,13 +619,14 @@
                 flops=FULL_COST,
                 limit=12 * MIB,
             )
-            arrived, solved = lax.optimization_barrier((arrived, solved))
-        if hop in (1, slabs - 2):
-            arrived = lax.optimization_barrier(arrived)
-        new_traces, new_helds = [], []
-        for col in range(width):
+            arrived[-1], solved = lax.optimization_barrier((arrived[-1], solved))
+        sums = []
+        new_traces, new_helds = [None] * width, [None] * width
+        for col in reversed(range(width)):
+            if hop == first_far - 1 and col < width - 1:
+                arrived[col], _ = lax.optimization_barrier((arrived[col], new_traces[-1]))
             counts = groups if col == width - 1 else (0, 0)
-            trace, kept, *sums = call(
+            new_traces[col], new_helds[col], *more = call(
                 f"hop{hop}_{col}",
                 functools.partial(hop_kernel, shots, hop + 1, col, counts),
                 [(chunk, f32)] * 2 + [row_shape] * sum(c > 0 for c in counts),
@@ -610,8 +634,7 @@
                 + (sides if col == width - 1 else []),
                 flops=HOP_COSTS[hop],
             )
-            new_traces.append(trace)
-            new_helds.append(kept)
+            sums = more or sums
         traces, helds = new_traces, new_helds
         if first_far - 1 <= hop < slabs - 2:
             (mine,) = call(
@@ -623,12 +646,11 @@
             )
         offs = ([sums.pop(0)] if groups[0] else []) + from_off
         ons = ([sums.pop(0)] if groups[1] else []) + from_on
-    (whole,) = call("whole", functools.partial(gather_kernel, slabs), [row_shape], [*helds, *traces])
-    (result,) = call(
+    result, whole = call(
         "inject",
-        functools.partial(inject_kernel, shots, depth),
-        [(solved.shape, f32)],
-        [coeffs, solved, *helds, *offs, *ons],
+        functools.partial(inject_kernel, shots, depth, len(offs)),
+        [(solved.shape, f32), row_shape],
+        [coeffs, solved, *helds, *traces, *offs, *ons],
         None,
         planes,
     )

time: 61.5 us -> 61.6 us (level)
  the two profiles are of different devices: /device:TPU:478 before, /device:TPU:415 now
where the time goes in v4:
time: 61.6 us; the launch traced here: 61.1 us
  starting transfers between devices  36.1 us (59%)
  waiting for transfers between devices  11.7 us (19%)
  Pallas kernels  9.57 us (16%)
  local copies, waits for them, and re-layouts  2.58 us (4%)
  between operations  1.12 us (2%)
    ppermute x17, starting transfers between devices, both(): return lax.ppermute(x, ('slab', 'tile'), moves)  13.3 us
    ppermute x1, starting transfers between devices, per_device(): from_on = [lax.ppermute(entered, 'tile', on)]  10.1 us
    pallas_call x27, Pallas kernels, call(): pl.pallas_call(body, name=name, out_shape=[jax.ShapeDtypeStruct(shape, dt...  9.57 us
    ppermute x1, waiting for transfers between devices, per_device(): lax.ppermute(low, 'tile', off)  5.73 us
    ppermute x17, waiting for transfers between devices, both(): return lax.ppermute(x, ('slab', 'tile'), moves)  5.1 us
    ppermute x1, starting transfers between devices, per_device(): lax.ppermute(low, 'tile', on)  4.82 us
    ppermute x1, starting transfers between devices, per_device(): lax.ppermute(high, 'tile', off)  3.39 us
    unnamed x10, local copies, waits for them, and re-layouts  2.58 us
  transfers between devices with their start and end apart: 22, of which 5 were waited for; matrix products, arithmetic and copies ran while one was open for 0% of the time, Pallas kernels for 10%

profile of v4, /device:TPU:415, one launch (start us, length us, event | category | flops | bytes accessed | tf_op | source)
XLA Modules:
  0.0 61.1 jit_solution(12371318241620489581)
XLA Ops:
  0.6 1.3 %pack_high.1.own.high = f32[592,128]{1,0:T(8,128)S(1)} custom-call(f32[1536,128]{1,0:T(8,128)} %bitcast.10, s32[16,128]{1,0:T(8,128)} %bitcast.12), custom_call_target="tpu_custom_call" | custom-call | flops 500000000 | tf_op jit(solution)/shard_map/pack_high/pallas_call | solution.py:34
  2.0 3.4 %collective-permute-start = (f32[592,128]{1,0:T(8,128)S(1)}, f32[592,128]{1,0:T(8,128)S(1)}, u32[]{:S(2)}, u32[]{:S(2)}) collective-permute-start(f32[592,128]{1,0:T(8,128)S(1)} %pack_high.1.own.high), channel_id=1, source_target_pairs={{1,2},{2,1},{3,4},{4,3},{5,6},{6,5},{7,8},{8,7},{9,10},{10,9},{11,... | collective-permute-start | bytes 909320 | tf_op jit(solution)/shard_map/ppermute | solution.py:538
  5.4 1.9 %collective-permute-start.1 = (f32[592,128]{1,0:T(8,128)S(1)}, f32[592,128]{1,0:T(8,128)S(1)}, u32[]{:S(2)}, u32[]{:S(2)}) collective-permute-start(f32[592,128]{1,0:T(8,128)S(1)} %pack_high.1.own.high), channel_id=1, source_target_pairs={{0,1},{1,0},{2,3},{3,2},{4,5},{5,4},{6,7},{7,6},{8,9},{9,8},{10,11... | collective-permute-start | bytes 909320 | tf_op jit(solution)/shard_map/ppermute | solution.py:538
  7.3 1.7 %copy-done = f32[2,1,2,384,384]{4,3,2,1,0:T(8,128)S(1)} copy-done((f32[2,1,2,384,384]{4,3,2,1,0:T(8,128)S(1)}, f32[2,1,2,384,384]{4,3,2,1,0:T(8,128)}, u32[]{:S(2)}) %copy-start) | copy-done | bytes 2359320
  9.6 0.6 consts.1
  10.6 0.5 collective-permute-done.off.high_off
  11.1 0.7 %collective-permute-start.4 = (f32[32,384]{1,0:T(8,128)S(1)}, f32[32,384]{1,0:T(8,128)S(1)}, u32[]{:S(2)}, u32[]{:S(2)}) collective-permute-start(f32[32,384]{1,0:T(8,128)S(1)} %get-tuple-element.63.refs_4_), channel_id=1, source_target_pairs={{0,64},{1,65},{2,66},{3,67},{4,68},{5,69},{6,70},{7,71},{8,72},{9,... | collective-permute-start | bytes 147464 | tf_op jit(solution)/shard_map/ppermute | solution.py:523
  11.8 0.7 %collective-permute-start.2 = (f32[32,384]{1,0:T(8,128)S(1)}, f32[32,384]{1,0:T(8,128)S(1)}, u32[]{:S(2)}, u32[]{:S(2)}) collective-permute-start(f32[32,384]{1,0:T(8,128)S(1)} %get-tuple-element.59.refs_4_), channel_id=1, source_target_pairs={{0,64},{1,65},{2,66},{3,67},{4,68},{5,69},{6,70},{7,71},{8,72},{9,... | collective-permute-start | bytes 147464 | tf_op jit(solution)/shard_map/ppermute | solution.py:523
  12.5 0.7 %bottom.1 = (f32[32,384]{1,0:T(8,128)S(1)}, f32[32,384]{1,0:T(8,128)S(1)}, f32[528,128]{1,0:T(8,128)S(1)}) custom-call(f32[592,128]{1,0:T(8,128)S(1)} %pack_high.1.own.high, f32[592,128]{1,0:T(8,128)S(1)} %collective-permute-done.off.high_off, f32[592,128]{1,0:T(8,128)S(1)} %collective-permute-done.1.on.high_on, f32[32,128]{1,0:T(8,128)S(1)} %consts.1, ...), custom_call_target="tpu_custom_call" | custom-call | flops 2000000000 | tf_op jit(solution)/shard_map/bottom/pallas_call | solution.py:34
  13.2 0.7 %collective-permute-start.5 = (f32[32,384]{1,0:T(8,128)S(1)}, f32[32,384]{1,0:T(8,128)S(1)}, u32[]{:S(2)}, u32[]{:S(2)}) collective-permute-start(f32[32,384]{1,0:T(8,128)S(1)} %get-tuple-element.66.refs_4_), channel_id=1, source_target_pairs={{64,128},{65,129},{66,130},{67,131},{68,132},{69,133},{70,134},{71... | collective-permute-start | bytes 147464 | tf_op jit(solution)/shard_map/ppermute | solution.py:523
  13.9 0.8 %collective-permute-start.3 = (f32[32,384]{1,0:T(8,128)S(1)}, f32[32,384]{1,0:T(8,128)S(1)}, u32[]{:S(2)}, u32[]{:S(2)}) collective-permute-start(f32[32,384]{1,0:T(8,128)S(1)} %get-tuple-element.62.refs_4_), channel_id=1, source_target_pairs={{64,128},{65,129},{66,130},{67,131},{68,132},{69,133},{70,134},{71... | collective-permute-start | bytes 147464 | tf_op jit(solution)/shard_map/ppermute | solution.py:523
  15.3 4.8 %collective-permute-start.8 = (f32[960,128]{1,0:T(8,128)S(1)}, f32[960,128]{1,0:T(8,128)S(1)}, u32[]{:S(2)}, u32[]{:S(2)}) collective-permute-start(f32[960,128]{1,0:T(8,128)S(1)} %pack_low.1.low), channel_id=1, source_target_pairs={{0,1},{1,0},{2,3},{3,2},{4,5},{5,4},{6,7},{7,6},{8,9},{9,8},{10,11... | collective-permute-start | bytes 1474568 | tf_op jit(solution)/shard_map/ppermute | solution.py:609
  20.1 2.5 %collective-permute-start.9 = (f32[960,128]{1,0:T(8,128)S(1)}, f32[960,128]{1,0:T(8,128)S(1)}, u32[]{:S(2)}, u32[]{:S(2)}) collective-permute-start(f32[960,128]{1,0:T(8,128)S(1)} %pack_low.1.low), channel_id=1, source_target_pairs={{1,2},{2,1},{3,4},{4,3},{5,6},{6,5},{7,8},{8,7},{9,10},{10,9},{11,... | collective-permute-start | bytes 1474568 | tf_op jit(solution)/shard_map/ppermute | solution.py:609
  22.7 0.7 %collective-permute-start.6 = (f32[32,384]{1,0:T(8,128)S(1)}, f32[32,384]{1,0:T(8,128)S(1)}, u32[]{:S(2)}, u32[]{:S(2)}) collective-permute-start(f32[32,384]{1,0:T(8,128)S(1)} %get-tuple-element.69.refs_4_), channel_id=1, source_target_pairs={{128,192},{129,193},{130,194},{131,195},{132,196},{133,197},{134,1... | collective-permute-start | bytes 147464 | tf_op jit(solution)/shard_map/ppermute | solution.py:523
  23.4 0.7 %collective-permute-start.10 = (f32[32,384]{1,0:T(8,128)S(1)}, f32[32,384]{1,0:T(8,128)S(1)}, u32[]{:S(2)}, u32[]{:S(2)}) collective-permute-start(f32[32,384]{1,0:T(8,128)S(1)} %get-tuple-element.75.refs_4_), channel_id=1, source_target_pairs={{128,192},{129,193},{130,194},{131,195},{132,196},{133,197},{134,1... | collective-permute-start | bytes 147464 | tf_op jit(solution)/shard_map/ppermute | solution.py:523
  24.1 0.7 %collective-permute-start.7 = (f32[32,384]{1,0:T(8,128)S(1)}, f32[32,384]{1,0:T(8,128)S(1)}, u32[]{:S(2)}, u32[]{:S(2)}) collective-permute-start(f32[32,384]{1,0:T(8,128)S(1)} %get-tuple-element.71.refs_4_), channel_id=1, source_target_pairs={{192,256},{193,257},{194,258},{195,259},{196,260},{197,261},{198,2... | collective-permute-start | bytes 147464 | tf_op jit(solution)/shard_map/ppermute | solution.py:523
  24.9 0.7 %collective-permute-start.11 = (f32[32,384]{1,0:T(8,128)S(1)}, f32[32,384]{1,0:T(8,128)S(1)}, u32[]{:S(2)}, u32[]{:S(2)}) collective-permute-start(f32[32,384]{1,0:T(8,128)S(1)} %get-tuple-element.77.refs_4_), channel_id=1, source_target_pairs={{192,256},{193,257},{194,258},{195,259},{196,260},{197,261},{198,2... | collective-permute-start | bytes 147464 | tf_op jit(solution)/shard_map/ppermute | solution.py:523
  25.5 5.7 %collective-permute-done.9.low_off = f32[960,128]{1,0:T(8,128)S(1)} collective-permute-done((f32[960,128]{1,0:T(8,128)S(1)}, f32[960,128]{1,0:T(8,128)S(1)}, u32[]{:S(2)}, u32[]{:S(2)}) %collective-permute-start.9) | collective-permute-done | bytes 491552 | tf_op jit(solution)/shard_map/ppermute | solution.py:609
  31.3 3.5 %full.1.base = f32[1536,128]{1,0:T(8,128)S(1)} custom-call(f32[528,128]{1,0:T(8,128)S(1)} %get-tuple-element.58.coeffs, f32[960,128]{1,0:T(8,128)S(1)} %pack_low.1.low, f32[960,128]{1,0:T(8,128)S(1)} %collective-permute-done.8.low_on, f32[960,128]{1,0:T(8,128)S(1)} %collective-permute-done.9.low_off, f32[592,128]{1,0:T(8,128)S(1)} %pack_high.1.own.high, ...), custom_call_target="tpu_custom_call" | custom-call | flops 5000000000 | tf_op jit(solution)/shard_map/full/pallas_call | solution.py:34
  34.8 0.7 %collective-permute-start.15 = (f32[32,384]{1,0:T(8,128)S(1)}, f32[32,384]{1,0:T(8,128)S(1)}, u32[]{:S(2)}, u32[]{:S(2)}) collective-permute-start(f32[32,384]{1,0:T(8,128)S(1)} %get-tuple-element.84.refs_4_.refs_1_), channel_id=1, source_target_pairs={{256,320},{257,321},{258,322},{259,323},{260,324},{261,325},{262,3... | collective-permute-start | bytes 147464 | tf_op jit(solution)/shard_map/ppermute | solution.py:523
  35.6 0.7 %collective-permute-start.12 = (f32[32,384]{1,0:T(8,128)S(1)}, f32[32,384]{1,0:T(8,128)S(1)}, u32[]{:S(2)}, u32[]{:S(2)}) collective-permute-start(f32[32,384]{1,0:T(8,128)S(1)} %get-tuple-element.87.refs_4_.refs_0_), channel_id=1, source_target_pairs={{256,320},{257,321},{258,322},{259,323},{260,324},{261,325},{262,3... | collective-permute-start | bytes 147464 | tf_op jit(solution)/shard_map/ppermute | solution.py:523
  36.3 0.7 %collective-permute-start.17 = (f32[64,384]{1,0:T(8,128)S(1)}, f32[64,384]{1,0:T(8,128)S(1)}, u32[]{:S(2)}, u32[]{:S(2)}) collective-permute-start(f32[64,384]{1,0:T(8,128)S(1)} %gather3.1), channel_id=1, source_target_pairs={{257,322},{258,321},{259,324},{260,323},{261,326},{262,325},{263,3... | collective-permute-start | bytes 294920 | tf_op jit(solution)/shard_map/ppermute | solution.py:523
  37.0 0.7 %collective-permute-start.16 = (f32[32,384]{1,0:T(8,128)S(1)}, f32[32,384]{1,0:T(8,128)S(1)}, u32[]{:S(2)}, u32[]{:S(2)}) collective-permute-start(f32[32,384]{1,0:T(8,128)S(1)} %get-tuple-element.93.refs_4_.refs_1_), channel_id=1, source_target_pairs={{320,384},{321,385},{322,386},{323,387},{324,388},{325,389},{326,3... | collective-permute-start | bytes 147464 | tf_op jit(solution)/shard_map/ppermute | solution.py:523
  37.7 0.7 %collective-permute-start.13 = (f32[32,384]{1,0:T(8,128)S(1)}, f32[32,384]{1,0:T(8,128)S(1)}, u32[]{:S(2)}, u32[]{:S(2)}) collective-permute-start(f32[32,384]{1,0:T(8,128)S(1)} %get-tuple-element.89.refs_4_.refs_0_), channel_id=1, source_target_pairs={{320,384},{321,385},{322,386},{323,387},{324,388},{325,389},{326,3... | collective-permute-start | bytes 147464 | tf_op jit(solution)/shard_map/ppermute | solution.py:523
  38.4 0.7 %collective-permute-start.19 = (f32[64,384]{1,0:T(8,128)S(1)}, f32[64,384]{1,0:T(8,128)S(1)}, u32[]{:S(2)}, u32[]{:S(2)}) collective-permute-start(f32[64,384]{1,0:T(8,128)S(1)} %gather4.1), channel_id=1, source_target_pairs={{321,386},{322,385},{323,388},{324,387},{325,390},{326,389},{327,3... | collective-permute-start | bytes 294920 | tf_op jit(solution)/shard_map/ppermute | solution.py:523
  39.1 1.3 %collective-permute-start.18 = (f32[32,384]{1,0:T(8,128)S(1)}, f32[32,384]{1,0:T(8,128)S(1)}, u32[]{:S(2)}, u32[]{:S(2)}) collective-permute-start(f32[32,384]{1,0:T(8,128)S(1)} %get-tuple-element.95.refs_4_.refs_1_), channel_id=1, source_target_pairs={{384,448},{385,449},{386,450},{387,451},{388,452},{389,453},{390,4... | collective-permute-start | bytes 147464 | tf_op jit(solution)/shard_map/ppermute | solution.py:523
  40.5 1.3 %collective-permute-start.14 = (f32[32,384]{1,0:T(8,128)S(1)}, f32[32,384]{1,0:T(8,128)S(1)}, u32[]{:S(2)}, u32[]{:S(2)}) collective-permute-start(f32[32,384]{1,0:T(8,128)S(1)} %get-tuple-element.91.refs_4_.refs_0_), channel_id=1, source_target_pairs={{384,448},{385,449},{386,450},{387,451},{388,452},{389,453},{390,4... | collective-permute-start | bytes 147464 | tf_op jit(solution)/shard_map/ppermute | solution.py:523
  41.8 1.3 %collective-permute-start.20 = (f32[64,384]{1,0:T(8,128)S(1)}, f32[64,384]{1,0:T(8,128)S(1)}, u32[]{:S(2)}, u32[]{:S(2)}) collective-permute-start(f32[64,384]{1,0:T(8,128)S(1)} %gather5.1), channel_id=1, source_target_pairs={{385,450},{386,449},{387,452},{388,451},{389,454},{390,453},{391,4... | collective-permute-start | bytes 294920 | tf_op jit(solution)/shard_map/ppermute | solution.py:523
  43.1 3.5 %collective-permute-done.18.refs_0_.refs_1_ = f32[32,384]{1,0:T(8,128)S(1)} collective-permute-done((f32[32,384]{1,0:T(8,128)S(1)}, f32[32,384]{1,0:T(8,128)S(1)}, u32[]{:S(2)}, u32[]{:S(2)}) %collective-permute-start.18) | collective-permute-done | bytes 49184 | tf_op jit(solution)/shard_map/ppermute | solution.py:523
  46.6 1.6 %collective-permute-done.14.refs_0_ = f32[32,384]{1,0:T(8,128)S(1)} collective-permute-done((f32[32,384]{1,0:T(8,128)S(1)}, f32[32,384]{1,0:T(8,128)S(1)}, u32[]{:S(2)}, u32[]{:S(2)}) %collective-permute-start.14) | collective-permute-done | bytes 49184 | tf_op jit(solution)/shard_map/ppermute | solution.py:523
  48.2 10.1 %collective-permute-start.21 = (f32[64,384]{1,0:T(8,128)S(1)}, f32[64,384]{1,0:T(8,128)S(1)}, u32[]{:S(2)}, u32[]{:S(2)}) collective-permute-start(f32[64,384]{1,0:T(8,128)S(1)} %entered.1), channel_id=1, source_target_pairs={{0,1},{1,0},{2,3},{3,2},{4,5},{5,4},{6,7},{7,6},{8,9},{9,8},{10,11... | collective-permute-start | bytes 294920 | tf_op jit(solution)/shard_map/ppermute | solution.py:599
  59.2 1.8 %inject.1 = (f32[1536,128]{1,0:T(8,128)}, f32[64,384]{1,0:T(8,128)}) custom-call(f32[528,128]{1,0:T(8,128)S(1)} %get-tuple-element.58.coeffs, f32[1536,128]{1,0:T(8,128)S(1)} %full.1.base, f32[32,384]{1,0:T(8,128)S(1)} %get-tuple-element.98.refs_0_, f32[32,384]{1,0:T(8,128)S(1)} %get-tuple-element.102.refs_1_, f32[32,384]{1,0:T(8,128)S(1)} %get-tuple-element.103.refs_2_, ...), custom_call_target="tpu_custom_call" | custom-call | flops 500000000 | tf_op jit(solution)/shard_map/inject/pallas_call | solution.py:34
  (49 shorter events, 2.9 us)
Async XLA Ops:
  2.0 9.1 %collective-permute-start = (f32[592,128]{1,0:T(8,128)S(1)}, f32[592,128]{1,0:T(8,128)S(1)}, u32[]{:S(2)}, u32[]{:S(2)}) collective-permute-start(f32[592,128]{1,0:T(8,128)S(1)} %pack_high.1.own.high), channel_id=1, source_target_pairs={{1,2},{2,1},{3,4},{4,3},{5,6},{6,5},{7,8},{8,7},{9,10},{10,9},{11,... | collective-permute-start | bytes 909320 | tf_op jit(solution)/shard_map/ppermute | solution.py:538
  5.4 5.7 %collective-permute-start.1 = (f32[592,128]{1,0:T(8,128)S(1)}, f32[592,128]{1,0:T(8,128)S(1)}, u32[]{:S(2)}, u32[]{:S(2)}) collective-permute-start(f32[592,128]{1,0:T(8,128)S(1)} %pack_high.1.own.high), channel_id=1, source_target_pairs={{0,1},{1,0},{2,3},{3,2},{4,5},{5,4},{6,7},{7,6},{8,9},{9,8},{10,11... | collective-permute-start | bytes 909320 | tf_op jit(solution)/shard_map/ppermute | solution.py:538
  7.3 1.7 %copy-start = (f32[2,1,2,384,384]{4,3,2,1,0:T(8,128)S(1)}, f32[2,1,2,384,384]{4,3,2,1,0:T(8,128)}, u32[]{:S(2)}) copy-start(f32[2,1,2,384,384]{4,3,2,1,0:T(8,128)} %param.10) | copy-start | bytes 7077892
  9.0 0.7 %copy-start.3 = (f32[3,8]{1,0:T(4,128)S(1)}, f32[3,8]{1,0:T(4,128)}, u32[]{:S(2)}) copy-start(f32[3,8]{1,0:T(4,128)} %table.1) | copy-start | bytes 292
  9.0 0.7 %copy-start.4 = (s32[1,2]{1,0:T(1,128)S(1)}, s32[1,2]{1,0:T(1,128)}, u32[]{:S(2)}) copy-start(s32[1,2]{1,0:T(1,128)} %widths.1) | copy-start | bytes 28
  9.6 0.9 %copy-start.1 = (f32[2,2,16,384]{3,2,1,0:T(8,128)S(1)}, f32[2,2,16,384]{3,2,1,0:T(8,128)}, u32[]{:S(2)}) copy-start(f32[2,2,16,384]{3,2,1,0:T(8,128)} %param.11) | copy-start | bytes 294916
  11.1 2.0 %collective-permute-start.4 = (f32[32,384]{1,0:T(8,128)S(1)}, f32[32,384]{1,0:T(8,128)S(1)}, u32[]{:S(2)}, u32[]{:S(2)}) collective-permute-start(f32[32,384]{1,0:T(8,128)S(1)} %get-tuple-element.63.refs_4_), channel_id=1, source_target_pairs={{0,64},{1,65},{2,66},{3,67},{4,68},{5,69},{6,70},{7,71},{8,72},{9,... | collective-permute-start | bytes 147464 | tf_op jit(solution)/shard_map/ppermute | solution.py:523
  11.8 2.1 %collective-permute-start.2 = (f32[32,384]{1,0:T(8,128)S(1)}, f32[32,384]{1,0:T(8,128)S(1)}, u32[]{:S(2)}, u32[]{:S(2)}) collective-permute-start(f32[32,384]{1,0:T(8,128)S(1)} %get-tuple-element.59.refs_4_), channel_id=1, source_target_pairs={{0,64},{1,65},{2,66},{3,67},{4,68},{5,69},{6,70},{7,71},{8,72},{9,... | collective-permute-start | bytes 147464 | tf_op jit(solution)/shard_map/ppermute | solution.py:523
  13.2 9.5 %collective-permute-start.5 = (f32[32,384]{1,0:T(8,128)S(1)}, f32[32,384]{1,0:T(8,128)S(1)}, u32[]{:S(2)}, u32[]{:S(2)}) collective-permute-start(f32[32,384]{1,0:T(8,128)S(1)} %get-tuple-element.66.refs_4_), channel_id=1, source_target_pairs={{64,128},{65,129},{66,130},{67,131},{68,132},{69,133},{70,134},{71... | collective-permute-start | bytes 147464 | tf_op jit(solution)/shard_map/ppermute | solution.py:523
  13.9 1.1 %copy-start.2 = (f32[16,2,3,2,8,128]{5,4,3,2,1,0:T(8,128)S(1)}, f32[16,2,3,2,8,128]{5,4,3,2,1,0:T(8,128)}, u32[]{:S(2)}) copy-start(f32[16,2,3,2,8,128]{5,4,3,2,1,0:T(8,128)} %param.6) | copy-start | bytes 2359300
  13.9 8.8 %collective-permute-start.3 = (f32[32,384]{1,0:T(8,128)S(1)}, f32[32,384]{1,0:T(8,128)S(1)}, u32[]{:S(2)}, u32[]{:S(2)}) collective-permute-start(f32[32,384]{1,0:T(8,128)S(1)} %get-tuple-element.62.refs_4_), channel_id=1, source_target_pairs={{64,128},{65,129},{66,130},{67,131},{68,132},{69,133},{70,134},{71... | collective-permute-start | bytes 147464 | tf_op jit(solution)/shard_map/ppermute | solution.py:523
  15.3 10.2 %collective-permute-start.8 = (f32[960,128]{1,0:T(8,128)S(1)}, f32[960,128]{1,0:T(8,128)S(1)}, u32[]{:S(2)}, u32[]{:S(2)}) collective-permute-start(f32[960,128]{1,0:T(8,128)S(1)} %pack_low.1.low), channel_id=1, source_target_pairs={{0,1},{1,0},{2,3},{3,2},{4,5},{5,4},{6,7},{7,6},{8,9},{9,8},{10,11... | collective-permute-start | bytes 1474568 | tf_op jit(solution)/shard_map/ppermute | solution.py:609
  20.1 11.2 %collective-permute-start.9 = (f32[960,128]{1,0:T(8,128)S(1)}, f32[960,128]{1,0:T(8,128)S(1)}, u32[]{:S(2)}, u32[]{:S(2)}) collective-permute-start(f32[960,128]{1,0:T(8,128)S(1)} %pack_low.1.low), channel_id=1, source_target_pairs={{1,2},{2,1},{3,4},{4,3},{5,6},{6,5},{7,8},{8,7},{9,10},{10,9},{11,... | collective-permute-start | bytes 1474568 | tf_op jit(solution)/shard_map/ppermute | solution.py:609
  22.7 1.4 %collective-permute-start.6 = (f32[32,384]{1,0:T(8,128)S(1)}, f32[32,384]{1,0:T(8,128)S(1)}, u32[]{:S(2)}, u32[]{:S(2)}) collective-permute-start(f32[32,384]{1,0:T(8,128)S(1)} %get-tuple-element.69.refs_4_), channel_id=1, source_target_pairs={{128,192},{129,193},{130,194},{131,195},{132,196},{133,197},{134,1... | collective-permute-start | bytes 147464 | tf_op jit(solution)/shard_map/ppermute | solution.py:523
  23.4 1.4 %collective-permute-start.10 = (f32[32,384]{1,0:T(8,128)S(1)}, f32[32,384]{1,0:T(8,128)S(1)}, u32[]{:S(2)}, u32[]{:S(2)}) collective-permute-start(f32[32,384]{1,0:T(8,128)S(1)} %get-tuple-element.75.refs_4_), channel_id=1, source_target_pairs={{128,192},{129,193},{130,194},{131,195},{132,196},{133,197},{134,1... | collective-permute-start | bytes 147464 | tf_op jit(solution)/shard_map/ppermute | solution.py:523
  24.1 10.7 %collective-permute-start.7 = (f32[32,384]{1,0:T(8,128)S(1)}, f32[32,384]{1,0:T(8,128)S(1)}, u32[]{:S(2)}, u32[]{:S(2)}) collective-permute-start(f32[32,384]{1,0:T(8,128)S(1)} %get-tuple-element.71.refs_4_), channel_id=1, source_target_pairs={{192,256},{193,257},{194,258},{195,259},{196,260},{197,261},{198,2... | collective-permute-start | bytes 147464 | tf_op jit(solution)/shard_map/ppermute | solution.py:523
  24.9 10.7 %collective-permute-start.11 = (f32[32,384]{1,0:T(8,128)S(1)}, f32[32,384]{1,0:T(8,128)S(1)}, u32[]{:S(2)}, u32[]{:S(2)}) collective-permute-start(f32[32,384]{1,0:T(8,128)S(1)} %get-tuple-element.77.refs_4_), channel_id=1, source_target_pairs={{192,256},{193,257},{194,258},{195,259},{196,260},{197,261},{198,2... | collective-permute-start | bytes 147464 | tf_op jit(solution)/shard_map/ppermute | solution.py:523
  34.8 2.1 %collective-permute-start.15 = (f32[32,384]{1,0:T(8,128)S(1)}, f32[32,384]{1,0:T(8,128)S(1)}, u32[]{:S(2)}, u32[]{:S(2)}) collective-permute-start(f32[32,384]{1,0:T(8,128)S(1)} %get-tuple-element.84.refs_4_.refs_1_), channel_id=1, source_target_pairs={{256,320},{257,321},{258,322},{259,323},{260,324},{261,325},{262,3... | collective-permute-start | bytes 147464 | tf_op jit(solution)/shard_map/ppermute | solution.py:523
  35.6 2.1 %collective-permute-start.12 = (f32[32,384]{1,0:T(8,128)S(1)}, f32[32,384]{1,0:T(8,128)S(1)}, u32[]{:S(2)}, u32[]{:S(2)}) collective-permute-start(f32[32,384]{1,0:T(8,128)S(1)} %get-tuple-element.87.refs_4_.refs_0_), channel_id=1, source_target_pairs={{256,320},{257,321},{258,322},{259,323},{260,324},{261,325},{262,3... | collective-permute-start | bytes 147464 | tf_op jit(solution)/shard_map/ppermute | solution.py:523
  36.3 2.8 %collective-permute-start.17 = (f32[64,384]{1,0:T(8,128)S(1)}, f32[64,384]{1,0:T(8,128)S(1)}, u32[]{:S(2)}, u32[]{:S(2)}) collective-permute-start(f32[64,384]{1,0:T(8,128)S(1)} %gather3.1), channel_id=1, source_target_pairs={{257,322},{258,321},{259,324},{260,323},{261,326},{262,325},{263,3... | collective-permute-start | bytes 294920 | tf_op jit(solution)/shard_map/ppermute | solution.py:523
  37.0 2.1 %collective-permute-start.16 = (f32[32,384]{1,0:T(8,128)S(1)}, f32[32,384]{1,0:T(8,128)S(1)}, u32[]{:S(2)}, u32[]{:S(2)}) collective-permute-start(f32[32,384]{1,0:T(8,128)S(1)} %get-tuple-element.93.refs_4_.refs_1_), channel_id=1, source_target_pairs={{320,384},{321,385},{322,386},{323,387},{324,388},{325,389},{326,3... | collective-permute-start | bytes 147464 | tf_op jit(solution)/shard_map/ppermute | solution.py:523
  37.7 2.7 %collective-permute-start.13 = (f32[32,384]{1,0:T(8,128)S(1)}, f32[32,384]{1,0:T(8,128)S(1)}, u32[]{:S(2)}, u32[]{:S(2)}) collective-permute-start(f32[32,384]{1,0:T(8,128)S(1)} %get-tuple-element.89.refs_4_.refs_0_), channel_id=1, source_target_pairs={{320,384},{321,385},{322,386},{323,387},{324,388},{325,389},{326,3... | collective-permute-start | bytes 147464 | tf_op jit(solution)/shard_map/ppermute | solution.py:523
  38.4 20.2 %collective-permute-start.19 = (f32[64,384]{1,0:T(8,128)S(1)}, f32[64,384]{1,0:T(8,128)S(1)}, u32[]{:S(2)}, u32[]{:S(2)}) collective-permute-start(f32[64,384]{1,0:T(8,128)S(1)} %gather4.1), channel_id=1, source_target_pairs={{321,386},{322,385},{323,388},{324,387},{325,390},{326,389},{327,3... | collective-permute-start | bytes 294920 | tf_op jit(solution)/shard_map/ppermute | solution.py:523
  39.1 7.4 %collective-permute-start.18 = (f32[32,384]{1,0:T(8,128)S(1)}, f32[32,384]{1,0:T(8,128)S(1)}, u32[]{:S(2)}, u32[]{:S(2)}) collective-permute-start(f32[32,384]{1,0:T(8,128)S(1)} %get-tuple-element.95.refs_4_.refs_1_), channel_id=1, source_target_pairs={{384,448},{385,449},{386,450},{387,451},{388,452},{389,453},{390,4... | collective-permute-start | bytes 147464 | tf_op jit(solution)/shard_map/ppermute | solution.py:523
  40.5 7.7 %collective-permute-start.14 = (f32[32,384]{1,0:T(8,128)S(1)}, f32[32,384]{1,0:T(8,128)S(1)}, u32[]{:S(2)}, u32[]{:S(2)}) collective-permute-start(f32[32,384]{1,0:T(8,128)S(1)} %get-tuple-element.91.refs_4_.refs_0_), channel_id=1, source_target_pairs={{384,448},{385,449},{386,450},{387,451},{388,452},{389,453},{390,4... | collective-permute-start | bytes 147464 | tf_op jit(solution)/shard_map/ppermute | solution.py:523
  41.8 17.1 %collective-permute-start.20 = (f32[64,384]{1,0:T(8,128)S(1)}, f32[64,384]{1,0:T(8,128)S(1)}, u32[]{:S(2)}, u32[]{:S(2)}) collective-permute-start(f32[64,384]{1,0:T(8,128)S(1)} %gather5.1), channel_id=1, source_target_pairs={{385,450},{386,449},{387,452},{388,451},{389,454},{390,453},{391,4... | collective-permute-start | bytes 294920 | tf_op jit(solution)/shard_map/ppermute | solution.py:523
  48.2 11.1 %collective-permute-start.21 = (f32[64,384]{1,0:T(8,128)S(1)}, f32[64,384]{1,0:T(8,128)S(1)}, u32[]{:S(2)}, u32[]{:S(2)}) collective-permute-start(f32[64,384]{1,0:T(8,128)S(1)} %entered.1), channel_id=1, source_target_pairs={{0,1},{1,0},{2,3},{3,2},{4,5},{5,4},{6,7},{7,6},{8,9},{9,8},{10,11... | collective-permute-start | bytes 294920 | tf_op jit(solution)/shard_map/ppermute | solution.py:599

commit v5 on v4

--- a/solution.py
+++ b/solution.py
@@ -316,7 +316,7 @@
                 bottoms[x - HALO][pl.ds(patch * shots, shots), lanes] = both[patch] + given
 
 
-def full_kernel(shots, depth, coeffs, low, low_on, low_off, high, high_off, high_on, out, v1, v2):
+def full_kernel(shots, depth, coeffs, low, low_off, low_on, high, high_off, high_on, out, v1, v2):
     stride = PC * WIDTH * depth
     lows, highs = (low, low_off, low_on), (high, high_off, high_on)
     plane = COLS * PC * shots
@@ -606,9 +606,9 @@
                 [again],
                 flops=LOW_COST,
             )
-            low_on, low_off = lax.ppermute(low, "tile", on), lax.ppermute(low, "tile", off)
+            low_off, low_on = lax.ppermute(low, "tile", off), lax.ppermute(low, "tile", on)
         if hop == first_far - 1:
-            lows, _ = lax.optimization_barrier(((low, low_on, low_off), traces))
+            lows, _ = lax.optimization_barrier(((low, low_off, low_on), traces))
             (solved,) = call(
                 "full",
                 functools.partial(full_kernel, shots, depth),

time: 61.6 us -> 58.8 us (0.955)
  the two profiles are of different devices: /device:TPU:415 before, /device:TPU:407 now
where the time goes in v5:
time: 58.8 us; the launch traced here: 58.2 us
  starting transfers between devices  27.9 us (47%)
  waiting for transfers between devices  17 us (29%)
  Pallas kernels  9.57 us (16%)
  local copies, waits for them, and re-layouts  2.58 us (4%)
  between operations  1.11 us (2%)
    ppermute x17, starting transfers between devices, both(): return lax.ppermute(x, ('slab', 'tile'), moves)  13.3 us
    pallas_call x27, Pallas kernels, call(): pl.pallas_call(body, name=name, out_shape=[jax.ShapeDtypeStruct(shape, dt...  9.57 us
    ppermute x17, waiting for transfers between devices, both(): return lax.ppermute(x, ('slab', 'tile'), moves)  8.44 us
    ppermute x1, waiting for transfers between devices, per_device(): lax.ppermute(low, 'tile', off)  6.7 us
    ppermute x1, starting transfers between devices, per_device(): lax.ppermute(high, 'tile', off)  3.47 us
    ppermute x1, starting transfers between devices, per_device(): lax.ppermute(low, 'tile', off)  3.47 us
    ppermute x1, starting transfers between devices, per_device(): lax.ppermute(high, 'tile', on)  3.4 us
    unnamed x10, local copies, waits for them, and re-layouts  2.58 us
  transfers between devices with their start and end apart: 22, of which 5 were waited for; matrix products, arithmetic and copies ran while one was open for 0% of the time, Pallas kernels for 11%

profile of v5, /device:TPU:407, one launch (start us, length us, event | category | flops | bytes accessed | tf_op | source)
XLA Modules:
  0.0 58.2 jit_solution(9696436732749275316)
XLA Ops:
  0.6 1.3 %pack_high.1.own.high = f32[592,128]{1,0:T(8,128)S(1)} custom-call(f32[1536,128]{1,0:T(8,128)} %bitcast.10, s32[16,128]{1,0:T(8,128)} %bitcast.12), custom_call_target="tpu_custom_call" | custom-call | flops 500000000 | tf_op jit(solution)/shard_map/pack_high/pallas_call | solution.py:34
  2.0 3.5 %collective-permute-start = (f32[592,128]{1,0:T(8,128)S(1)}, f32[592,128]{1,0:T(8,128)S(1)}, u32[]{:S(2)}, u32[]{:S(2)}) collective-permute-start(f32[592,128]{1,0:T(8,128)S(1)} %pack_high.1.own.high), channel_id=1, source_target_pairs={{1,2},{2,1},{3,4},{4,3},{5,6},{6,5},{7,8},{8,7},{9,10},{10,9},{11,... | collective-permute-start | bytes 909320 | tf_op jit(solution)/shard_map/ppermute | solution.py:538
  5.4 3.4 %collective-permute-start.1 = (f32[592,128]{1,0:T(8,128)S(1)}, f32[592,128]{1,0:T(8,128)S(1)}, u32[]{:S(2)}, u32[]{:S(2)}) collective-permute-start(f32[592,128]{1,0:T(8,128)S(1)} %pack_high.1.own.high), channel_id=1, source_target_pairs={{0,1},{1,0},{2,3},{3,2},{4,5},{5,4},{6,7},{7,6},{8,9},{9,8},{10,11... | collective-permute-start | bytes 909320 | tf_op jit(solution)/shard_map/ppermute | solution.py:538
  8.9 1.7 %copy-done = f32[2,1,2,384,384]{4,3,2,1,0:T(8,128)S(1)} copy-done((f32[2,1,2,384,384]{4,3,2,1,0:T(8,128)S(1)}, f32[2,1,2,384,384]{4,3,2,1,0:T(8,128)}, u32[]{:S(2)}) %copy-start) | copy-done | bytes 2359320
  12.1 1.2 %collective-permute-done.off.high_off = f32[592,128]{1,0:T(8,128)S(1)} collective-permute-done((f32[592,128]{1,0:T(8,128)S(1)}, f32[592,128]{1,0:T(8,128)S(1)}, u32[]{:S(2)}, u32[]{:S(2)}) %collective-permute-start) | collective-permute-done | bytes 303136 | tf_op jit(solution)/shard_map/ppermute | solution.py:538
  13.4 0.7 %collective-permute-start.4 = (f32[32,384]{1,0:T(8,128)S(1)}, f32[32,384]{1,0:T(8,128)S(1)}, u32[]{:S(2)}, u32[]{:S(2)}) collective-permute-start(f32[32,384]{1,0:T(8,128)S(1)} %get-tuple-element.63.refs_4_), channel_id=1, source_target_pairs={{0,64},{1,65},{2,66},{3,67},{4,68},{5,69},{6,70},{7,71},{8,72},{9,... | collective-permute-start | bytes 147464 | tf_op jit(solution)/shard_map/ppermute | solution.py:523
  14.0 0.7 %collective-permute-start.2 = (f32[32,384]{1,0:T(8,128)S(1)}, f32[32,384]{1,0:T(8,128)S(1)}, u32[]{:S(2)}, u32[]{:S(2)}) collective-permute-start(f32[32,384]{1,0:T(8,128)S(1)} %get-tuple-element.59.refs_4_), channel_id=1, source_target_pairs={{0,64},{1,65},{2,66},{3,67},{4,68},{5,69},{6,70},{7,71},{8,72},{9,... | collective-permute-start | bytes 147464 | tf_op jit(solution)/shard_map/ppermute | solution.py:523
  14.7 0.7 %bottom.1 = (f32[32,384]{1,0:T(8,128)S(1)}, f32[32,384]{1,0:T(8,128)S(1)}, f32[528,128]{1,0:T(8,128)S(1)}) custom-call(f32[592,128]{1,0:T(8,128)S(1)} %pack_high.1.own.high, f32[592,128]{1,0:T(8,128)S(1)} %collective-permute-done.off.high_off, f32[592,128]{1,0:T(8,128)S(1)} %collective-permute-done.1.on.high_on, f32[32,128]{1,0:T(8,128)S(1)} %consts.1, ...), custom_call_target="tpu_custom_call" | custom-call | flops 2000000000 | tf_op jit(solution)/shard_map/bottom/pallas_call | solution.py:34
  15.4 0.7 %collective-permute-start.5 = (f32[32,384]{1,0:T(8,128)S(1)}, f32[32,384]{1,0:T(8,128)S(1)}, u32[]{:S(2)}, u32[]{:S(2)}) collective-permute-start(f32[32,384]{1,0:T(8,128)S(1)} %get-tuple-element.66.refs_4_), channel_id=1, source_target_pairs={{64,128},{65,129},{66,130},{67,131},{68,132},{69,133},{70,134},{71... | collective-permute-start | bytes 147464 | tf_op jit(solution)/shard_map/ppermute | solution.py:523
  16.1 0.8 %collective-permute-start.3 = (f32[32,384]{1,0:T(8,128)S(1)}, f32[32,384]{1,0:T(8,128)S(1)}, u32[]{:S(2)}, u32[]{:S(2)}) collective-permute-start(f32[32,384]{1,0:T(8,128)S(1)} %get-tuple-element.62.refs_4_), channel_id=1, source_target_pairs={{64,128},{65,129},{66,130},{67,131},{68,132},{69,133},{70,134},{71... | collective-permute-start | bytes 147464 | tf_op jit(solution)/shard_map/ppermute | solution.py:523
  17.5 3.5 %collective-permute-start.8 = (f32[960,128]{1,0:T(8,128)S(1)}, f32[960,128]{1,0:T(8,128)S(1)}, u32[]{:S(2)}, u32[]{:S(2)}) collective-permute-start(f32[960,128]{1,0:T(8,128)S(1)} %pack_low.1.low), channel_id=1, source_target_pairs={{1,2},{2,1},{3,4},{4,3},{5,6},{6,5},{7,8},{8,7},{9,10},{10,9},{11,... | collective-permute-start | bytes 1474568 | tf_op jit(solution)/shard_map/ppermute | solution.py:609
  21.0 2.4 %collective-permute-start.9 = (f32[960,128]{1,0:T(8,128)S(1)}, f32[960,128]{1,0:T(8,128)S(1)}, u32[]{:S(2)}, u32[]{:S(2)}) collective-permute-start(f32[960,128]{1,0:T(8,128)S(1)} %pack_low.1.low), channel_id=1, source_target_pairs={{0,1},{1,0},{2,3},{3,2},{4,5},{5,4},{6,7},{7,6},{8,9},{9,8},{10,11... | collective-permute-start | bytes 1474568 | tf_op jit(solution)/shard_map/ppermute | solution.py:609
  23.4 0.7 %collective-permute-start.6 = (f32[32,384]{1,0:T(8,128)S(1)}, f32[32,384]{1,0:T(8,128)S(1)}, u32[]{:S(2)}, u32[]{:S(2)}) collective-permute-start(f32[32,384]{1,0:T(8,128)S(1)} %get-tuple-element.69.refs_4_), channel_id=1, source_target_pairs={{128,192},{129,193},{130,194},{131,195},{132,196},{133,197},{134,1... | collective-permute-start | bytes 147464 | tf_op jit(solution)/shard_map/ppermute | solution.py:523
  24.1 0.7 %collective-permute-start.10 = (f32[32,384]{1,0:T(8,128)S(1)}, f32[32,384]{1,0:T(8,128)S(1)}, u32[]{:S(2)}, u32[]{:S(2)}) collective-permute-start(f32[32,384]{1,0:T(8,128)S(1)} %get-tuple-element.75.refs_4_), channel_id=1, source_target_pairs={{128,192},{129,193},{130,194},{131,195},{132,196},{133,197},{134,1... | collective-permute-start | bytes 147464 | tf_op jit(solution)/shard_map/ppermute | solution.py:523
  24.9 0.7 %collective-permute-start.7 = (f32[32,384]{1,0:T(8,128)S(1)}, f32[32,384]{1,0:T(8,128)S(1)}, u32[]{:S(2)}, u32[]{:S(2)}) collective-permute-start(f32[32,384]{1,0:T(8,128)S(1)} %get-tuple-element.71.refs_4_), channel_id=1, source_target_pairs={{192,256},{193,257},{194,258},{195,259},{196,260},{197,261},{198,2... | collective-permute-start | bytes 147464 | tf_op jit(solution)/shard_map/ppermute | solution.py:523
  25.6 0.7 %collective-permute-start.11 = (f32[32,384]{1,0:T(8,128)S(1)}, f32[32,384]{1,0:T(8,128)S(1)}, u32[]{:S(2)}, u32[]{:S(2)}) collective-permute-start(f32[32,384]{1,0:T(8,128)S(1)} %get-tuple-element.77.refs_4_), channel_id=1, source_target_pairs={{192,256},{193,257},{194,258},{195,259},{196,260},{197,261},{198,2... | collective-permute-start | bytes 147464 | tf_op jit(solution)/shard_map/ppermute | solution.py:523
  26.2 6.7 %collective-permute-done.8.low_off = f32[960,128]{1,0:T(8,128)S(1)} collective-permute-done((f32[960,128]{1,0:T(8,128)S(1)}, f32[960,128]{1,0:T(8,128)S(1)}, u32[]{:S(2)}, u32[]{:S(2)}) %collective-permute-start.8) | collective-permute-done | bytes 491552 | tf_op jit(solution)/shard_map/ppermute | solution.py:609
  33.0 3.5 %full.1.base = f32[1536,128]{1,0:T(8,128)S(1)} custom-call(f32[528,128]{1,0:T(8,128)S(1)} %get-tuple-element.58.coeffs, f32[960,128]{1,0:T(8,128)S(1)} %pack_low.1.low, f32[960,128]{1,0:T(8,128)S(1)} %collective-permute-done.8.low_off, f32[960,128]{1,0:T(8,128)S(1)} %collective-permute-done.9.low_on, f32[592,128]{1,0:T(8,128)S(1)} %pack_high.1.own.high, ...), custom_call_target="tpu_custom_call" | custom-call | flops 5000000000 | tf_op jit(solution)/shard_map/full/pallas_call | solution.py:34
  36.5 0.7 %collective-permute-start.15 = (f32[32,384]{1,0:T(8,128)S(1)}, f32[32,384]{1,0:T(8,128)S(1)}, u32[]{:S(2)}, u32[]{:S(2)}) collective-permute-start(f32[32,384]{1,0:T(8,128)S(1)} %get-tuple-element.84.refs_4_.refs_1_), channel_id=1, source_target_pairs={{256,320},{257,321},{258,322},{259,323},{260,324},{261,325},{262,3... | collective-permute-start | bytes 147464 | tf_op jit(solution)/shard_map/ppermute | solution.py:523
  37.2 0.7 %collective-permute-start.12 = (f32[32,384]{1,0:T(8,128)S(1)}, f32[32,384]{1,0:T(8,128)S(1)}, u32[]{:S(2)}, u32[]{:S(2)}) collective-permute-start(f32[32,384]{1,0:T(8,128)S(1)} %get-tuple-element.87.refs_4_.refs_0_), channel_id=1, source_target_pairs={{256,320},{257,321},{258,322},{259,323},{260,324},{261,325},{262,3... | collective-permute-start | bytes 147464 | tf_op jit(solution)/shard_map/ppermute | solution.py:523
  37.9 0.7 %collective-permute-start.17 = (f32[64,384]{1,0:T(8,128)S(1)}, f32[64,384]{1,0:T(8,128)S(1)}, u32[]{:S(2)}, u32[]{:S(2)}) collective-permute-start(f32[64,384]{1,0:T(8,128)S(1)} %gather3.1), channel_id=1, source_target_pairs={{257,322},{258,321},{259,324},{260,323},{261,326},{262,325},{263,3... | collective-permute-start | bytes 294920 | tf_op jit(solution)/shard_map/ppermute | solution.py:523
  38.7 0.7 %collective-permute-start.16 = (f32[32,384]{1,0:T(8,128)S(1)}, f32[32,384]{1,0:T(8,128)S(1)}, u32[]{:S(2)}, u32[]{:S(2)}) collective-permute-start(f32[32,384]{1,0:T(8,128)S(1)} %get-tuple-element.93.refs_4_.refs_1_), channel_id=1, source_target_pairs={{320,384},{321,385},{322,386},{323,387},{324,388},{325,389},{326,3... | collective-permute-start | bytes 147464 | tf_op jit(solution)/shard_map/ppermute | solution.py:523
  39.4 0.7 %collective-permute-start.13 = (f32[32,384]{1,0:T(8,128)S(1)}, f32[32,384]{1,0:T(8,128)S(1)}, u32[]{:S(2)}, u32[]{:S(2)}) collective-permute-start(f32[32,384]{1,0:T(8,128)S(1)} %get-tuple-element.89.refs_4_.refs_0_), channel_id=1, source_target_pairs={{320,384},{321,385},{322,386},{323,387},{324,388},{325,389},{326,3... | collective-permute-start | bytes 147464 | tf_op jit(solution)/shard_map/ppermute | solution.py:523
  40.1 0.7 %collective-permute-start.19 = (f32[64,384]{1,0:T(8,128)S(1)}, f32[64,384]{1,0:T(8,128)S(1)}, u32[]{:S(2)}, u32[]{:S(2)}) collective-permute-start(f32[64,384]{1,0:T(8,128)S(1)} %gather4.1), channel_id=1, source_target_pairs={{321,386},{322,385},{323,388},{324,387},{325,390},{326,389},{327,3... | collective-permute-start | bytes 294920 | tf_op jit(solution)/shard_map/ppermute | solution.py:523
  40.8 1.3 %collective-permute-start.18 = (f32[32,384]{1,0:T(8,128)S(1)}, f32[32,384]{1,0:T(8,128)S(1)}, u32[]{:S(2)}, u32[]{:S(2)}) collective-permute-start(f32[32,384]{1,0:T(8,128)S(1)} %get-tuple-element.95.refs_4_.refs_1_), channel_id=1, source_target_pairs={{384,448},{385,449},{386,450},{387,451},{388,452},{389,453},{390,4... | collective-permute-start | bytes 147464 | tf_op jit(solution)/shard_map/ppermute | solution.py:523
  42.2 1.3 %collective-permute-start.14 = (f32[32,384]{1,0:T(8,128)S(1)}, f32[32,384]{1,0:T(8,128)S(1)}, u32[]{:S(2)}, u32[]{:S(2)}) collective-permute-start(f32[32,384]{1,0:T(8,128)S(1)} %get-tuple-element.91.refs_4_.refs_0_), channel_id=1, source_target_pairs={{384,448},{385,449},{386,450},{387,451},{388,452},{389,453},{390,4... | collective-permute-start | bytes 147464 | tf_op jit(solution)/shard_map/ppermute | solution.py:523
  43.5 1.3 %collective-permute-start.20 = (f32[64,384]{1,0:T(8,128)S(1)}, f32[64,384]{1,0:T(8,128)S(1)}, u32[]{:S(2)}, u32[]{:S(2)}) collective-permute-start(f32[64,384]{1,0:T(8,128)S(1)} %gather5.1), channel_id=1, source_target_pairs={{385,450},{386,449},{387,452},{388,451},{389,454},{390,453},{391,4... | collective-permute-start | bytes 294920 | tf_op jit(solution)/shard_map/ppermute | solution.py:523
  44.8 4.1 %collective-permute-done.18.refs_0_.refs_1_ = f32[32,384]{1,0:T(8,128)S(1)} collective-permute-done((f32[32,384]{1,0:T(8,128)S(1)}, f32[32,384]{1,0:T(8,128)S(1)}, u32[]{:S(2)}, u32[]{:S(2)}) %collective-permute-start.18) | collective-permute-done | bytes 49184 | tf_op jit(solution)/shard_map/ppermute | solution.py:523
  48.9 4.3 %collective-permute-done.14.refs_0_ = f32[32,384]{1,0:T(8,128)S(1)} collective-permute-done((f32[32,384]{1,0:T(8,128)S(1)}, f32[32,384]{1,0:T(8,128)S(1)}, u32[]{:S(2)}, u32[]{:S(2)}) %collective-permute-start.14) | collective-permute-done | bytes 49184 | tf_op jit(solution)/shard_map/ppermute | solution.py:523
  53.2 1.9 %collective-permute-start.21 = (f32[64,384]{1,0:T(8,128)S(1)}, f32[64,384]{1,0:T(8,128)S(1)}, u32[]{:S(2)}, u32[]{:S(2)}) collective-permute-start(f32[64,384]{1,0:T(8,128)S(1)} %entered.1), channel_id=1, source_target_pairs={{0,1},{1,0},{2,3},{3,2},{4,5},{5,4},{6,7},{7,6},{8,9},{9,8},{10,11... | collective-permute-start | bytes 294920 | tf_op jit(solution)/shard_map/ppermute | solution.py:599
  55.7 0.6 %collective-permute-done.21.refs_6_ = f32[64,384]{1,0:T(8,128)S(1)} collective-permute-done((f32[64,384]{1,0:T(8,128)S(1)}, f32[64,384]{1,0:T(8,128)S(1)}, u32[]{:S(2)}, u32[]{:S(2)}) %collective-permute-start.21) | collective-permute-done | bytes 98336 | tf_op jit(solution)/shard_map/ppermute | solution.py:599
  56.4 1.8 %inject.1 = (f32[1536,128]{1,0:T(8,128)}, f32[64,384]{1,0:T(8,128)}) custom-call(f32[528,128]{1,0:T(8,128)S(1)} %get-tuple-element.58.coeffs, f32[1536,128]{1,0:T(8,128)S(1)} %full.1.base, f32[32,384]{1,0:T(8,128)S(1)} %get-tuple-element.98.refs_0_, f32[32,384]{1,0:T(8,128)S(1)} %get-tuple-element.102.refs_1_, f32[32,384]{1,0:T(8,128)S(1)} %get-tuple-element.103.refs_2_, ...), custom_call_target="tpu_custom_call" | custom-call | flops 500000000 | tf_op jit(solution)/shard_map/inject/pallas_call | solution.py:34
  (49 shorter events, 3.2 us)
Async XLA Ops:
  2.0 11.4 %collective-permute-start = (f32[592,128]{1,0:T(8,128)S(1)}, f32[592,128]{1,0:T(8,128)S(1)}, u32[]{:S(2)}, u32[]{:S(2)}) collective-permute-start(f32[592,128]{1,0:T(8,128)S(1)} %pack_high.1.own.high), channel_id=1, source_target_pairs={{1,2},{2,1},{3,4},{4,3},{5,6},{6,5},{7,8},{8,7},{9,10},{10,9},{11,... | collective-permute-start | bytes 909320 | tf_op jit(solution)/shard_map/ppermute | solution.py:538
  5.4 7.9 %collective-permute-start.1 = (f32[592,128]{1,0:T(8,128)S(1)}, f32[592,128]{1,0:T(8,128)S(1)}, u32[]{:S(2)}, u32[]{:S(2)}) collective-permute-start(f32[592,128]{1,0:T(8,128)S(1)} %pack_high.1.own.high), channel_id=1, source_target_pairs={{0,1},{1,0},{2,3},{3,2},{4,5},{5,4},{6,7},{7,6},{8,9},{9,8},{10,11... | collective-permute-start | bytes 909320 | tf_op jit(solution)/shard_map/ppermute | solution.py:538
  8.8 1.7 %copy-start = (f32[2,1,2,384,384]{4,3,2,1,0:T(8,128)S(1)}, f32[2,1,2,384,384]{4,3,2,1,0:T(8,128)}, u32[]{:S(2)}) copy-start(f32[2,1,2,384,384]{4,3,2,1,0:T(8,128)} %param.10) | copy-start | bytes 7077892
  10.5 0.7 %copy-start.3 = (f32[3,8]{1,0:T(4,128)S(1)}, f32[3,8]{1,0:T(4,128)}, u32[]{:S(2)}) copy-start(f32[3,8]{1,0:T(4,128)} %table.1) | copy-start | bytes 292
  10.5 0.7 %copy-start.4 = (s32[1,2]{1,0:T(1,128)S(1)}, s32[1,2]{1,0:T(1,128)}, u32[]{:S(2)}) copy-start(s32[1,2]{1,0:T(1,128)} %widths.1) | copy-start | bytes 28
  11.2 0.9 %copy-start.1 = (f32[2,2,16,384]{3,2,1,0:T(8,128)S(1)}, f32[2,2,16,384]{3,2,1,0:T(8,128)}, u32[]{:S(2)}) copy-start(f32[2,2,16,384]{3,2,1,0:T(8,128)} %param.11) | copy-start | bytes 294916
  13.4 2.0 %collective-permute-start.4 = (f32[32,384]{1,0:T(8,128)S(1)}, f32[32,384]{1,0:T(8,128)S(1)}, u32[]{:S(2)}, u32[]{:S(2)}) collective-permute-start(f32[32,384]{1,0:T(8,128)S(1)} %get-tuple-element.63.refs_4_), channel_id=1, source_target_pairs={{0,64},{1,65},{2,66},{3,67},{4,68},{5,69},{6,70},{7,71},{8,72},{9,... | collective-permute-start | bytes 147464 | tf_op jit(solution)/shard_map/ppermute | solution.py:523
  14.0 2.1 %collective-permute-start.2 = (f32[32,384]{1,0:T(8,128)S(1)}, f32[32,384]{1,0:T(8,128)S(1)}, u32[]{:S(2)}, u32[]{:S(2)}) collective-permute-start(f32[32,384]{1,0:T(8,128)S(1)} %get-tuple-element.59.refs_4_), channel_id=1, source_target_pairs={{0,64},{1,65},{2,66},{3,67},{4,68},{5,69},{6,70},{7,71},{8,72},{9,... | collective-permute-start | bytes 147464 | tf_op jit(solution)/shard_map/ppermute | solution.py:523
  15.4 8.0 %collective-permute-start.5 = (f32[32,384]{1,0:T(8,128)S(1)}, f32[32,384]{1,0:T(8,128)S(1)}, u32[]{:S(2)}, u32[]{:S(2)}) collective-permute-start(f32[32,384]{1,0:T(8,128)S(1)} %get-tuple-element.66.refs_4_), channel_id=1, source_target_pairs={{64,128},{65,129},{66,130},{67,131},{68,132},{69,133},{70,134},{71... | collective-permute-start | bytes 147464 | tf_op jit(solution)/shard_map/ppermute | solution.py:523
  16.1 1.1 %copy-start.2 = (f32[16,2,3,2,8,128]{5,4,3,2,1,0:T(8,128)S(1)}, f32[16,2,3,2,8,128]{5,4,3,2,1,0:T(8,128)}, u32[]{:S(2)}) copy-start(f32[16,2,3,2,8,128]{5,4,3,2,1,0:T(8,128)} %param.6) | copy-start | bytes 2359300
  16.1 7.3 %collective-permute-start.3 = (f32[32,384]{1,0:T(8,128)S(1)}, f32[32,384]{1,0:T(8,128)S(1)}, u32[]{:S(2)}, u32[]{:S(2)}) collective-permute-start(f32[32,384]{1,0:T(8,128)S(1)} %get-tuple-element.62.refs_4_), channel_id=1, source_target_pairs={{64,128},{65,129},{66,130},{67,131},{68,132},{69,133},{70,134},{71... | collective-permute-start | bytes 147464 | tf_op jit(solution)/shard_map/ppermute | solution.py:523
  17.5 15.4 %collective-permute-start.8 = (f32[960,128]{1,0:T(8,128)S(1)}, f32[960,128]{1,0:T(8,128)S(1)}, u32[]{:S(2)}, u32[]{:S(2)}) collective-permute-start(f32[960,128]{1,0:T(8,128)S(1)} %pack_low.1.low), channel_id=1, source_target_pairs={{1,2},{2,1},{3,4},{4,3},{5,6},{6,5},{7,8},{8,7},{9,10},{10,9},{11,... | collective-permute-start | bytes 1474568 | tf_op jit(solution)/shard_map/ppermute | solution.py:609
  21.0 11.9 %collective-permute-start.9 = (f32[960,128]{1,0:T(8,128)S(1)}, f32[960,128]{1,0:T(8,128)S(1)}, u32[]{:S(2)}, u32[]{:S(2)}) collective-permute-start(f32[960,128]{1,0:T(8,128)S(1)} %pack_low.1.low), channel_id=1, source_target_pairs={{0,1},{1,0},{2,3},{3,2},{4,5},{5,4},{6,7},{7,6},{8,9},{9,8},{10,11... | collective-permute-start | bytes 1474568 | tf_op jit(solution)/shard_map/ppermute | solution.py:609
  23.4 1.4 %collective-permute-start.6 = (f32[32,384]{1,0:T(8,128)S(1)}, f32[32,384]{1,0:T(8,128)S(1)}, u32[]{:S(2)}, u32[]{:S(2)}) collective-permute-start(f32[32,384]{1,0:T(8,128)S(1)} %get-tuple-element.69.refs_4_), channel_id=1, source_target_pairs={{128,192},{129,193},{130,194},{131,195},{132,196},{133,197},{134,1... | collective-permute-start | bytes 147464 | tf_op jit(solution)/shard_map/ppermute | solution.py:523
  24.1 1.4 %collective-permute-start.10 = (f32[32,384]{1,0:T(8,128)S(1)}, f32[32,384]{1,0:T(8,128)S(1)}, u32[]{:S(2)}, u32[]{:S(2)}) collective-permute-start(f32[32,384]{1,0:T(8,128)S(1)} %get-tuple-element.75.refs_4_), channel_id=1, source_target_pairs={{128,192},{129,193},{130,194},{131,195},{132,196},{133,197},{134,1... | collective-permute-start | bytes 147464 | tf_op jit(solution)/shard_map/ppermute | solution.py:523
  24.9 11.6 %collective-permute-start.7 = (f32[32,384]{1,0:T(8,128)S(1)}, f32[32,384]{1,0:T(8,128)S(1)}, u32[]{:S(2)}, u32[]{:S(2)}) collective-permute-start(f32[32,384]{1,0:T(8,128)S(1)} %get-tuple-element.71.refs_4_), channel_id=1, source_target_pairs={{192,256},{193,257},{194,258},{195,259},{196,260},{197,261},{198,2... | collective-permute-start | bytes 147464 | tf_op jit(solution)/shard_map/ppermute | solution.py:523
  25.6 11.6 %collective-permute-start.11 = (f32[32,384]{1,0:T(8,128)S(1)}, f32[32,384]{1,0:T(8,128)S(1)}, u32[]{:S(2)}, u32[]{:S(2)}) collective-permute-start(f32[32,384]{1,0:T(8,128)S(1)} %get-tuple-element.77.refs_4_), channel_id=1, source_target_pairs={{192,256},{193,257},{194,258},{195,259},{196,260},{197,261},{198,2... | collective-permute-start | bytes 147464 | tf_op jit(solution)/shard_map/ppermute | solution.py:523
  36.5 2.1 %collective-permute-start.15 = (f32[32,384]{1,0:T(8,128)S(1)}, f32[32,384]{1,0:T(8,128)S(1)}, u32[]{:S(2)}, u32[]{:S(2)}) collective-permute-start(f32[32,384]{1,0:T(8,128)S(1)} %get-tuple-element.84.refs_4_.refs_1_), channel_id=1, source_target_pairs={{256,320},{257,321},{258,322},{259,323},{260,324},{261,325},{262,3... | collective-permute-start | bytes 147464 | tf_op jit(solution)/shard_map/ppermute | solution.py:523
  37.2 2.1 %collective-permute-start.12 = (f32[32,384]{1,0:T(8,128)S(1)}, f32[32,384]{1,0:T(8,128)S(1)}, u32[]{:S(2)}, u32[]{:S(2)}) collective-permute-start(f32[32,384]{1,0:T(8,128)S(1)} %get-tuple-element.87.refs_4_.refs_0_), channel_id=1, source_target_pairs={{256,320},{257,321},{258,322},{259,323},{260,324},{261,325},{262,3... | collective-permute-start | bytes 147464 | tf_op jit(solution)/shard_map/ppermute | solution.py:523
  37.9 2.8 %collective-permute-start.17 = (f32[64,384]{1,0:T(8,128)S(1)}, f32[64,384]{1,0:T(8,128)S(1)}, u32[]{:S(2)}, u32[]{:S(2)}) collective-permute-start(f32[64,384]{1,0:T(8,128)S(1)} %gather3.1), channel_id=1, source_target_pairs={{257,322},{258,321},{259,324},{260,323},{261,326},{262,325},{263,3... | collective-permute-start | bytes 294920 | tf_op jit(solution)/shard_map/ppermute | solution.py:523
  38.7 2.1 %collective-permute-start.16 = (f32[32,384]{1,0:T(8,128)S(1)}, f32[32,384]{1,0:T(8,128)S(1)}, u32[]{:S(2)}, u32[]{:S(2)}) collective-permute-start(f32[32,384]{1,0:T(8,128)S(1)} %get-tuple-element.93.refs_4_.refs_1_), channel_id=1, source_target_pairs={{320,384},{321,385},{322,386},{323,387},{324,388},{325,389},{326,3... | collective-permute-start | bytes 147464 | tf_op jit(solution)/shard_map/ppermute | solution.py:523
  39.4 2.7 %collective-permute-start.13 = (f32[32,384]{1,0:T(8,128)S(1)}, f32[32,384]{1,0:T(8,128)S(1)}, u32[]{:S(2)}, u32[]{:S(2)}) collective-permute-start(f32[32,384]{1,0:T(8,128)S(1)} %get-tuple-element.89.refs_4_.refs_0_), channel_id=1, source_target_pairs={{320,384},{321,385},{322,386},{323,387},{324,388},{325,389},{326,3... | collective-permute-start | bytes 147464 | tf_op jit(solution)/shard_map/ppermute | solution.py:523
  40.1 15.3 %collective-permute-start.19 = (f32[64,384]{1,0:T(8,128)S(1)}, f32[64,384]{1,0:T(8,128)S(1)}, u32[]{:S(2)}, u32[]{:S(2)}) collective-permute-start(f32[64,384]{1,0:T(8,128)S(1)} %gather4.1), channel_id=1, source_target_pairs={{321,386},{322,385},{323,388},{324,387},{325,390},{326,389},{327,3... | collective-permute-start | bytes 294920 | tf_op jit(solution)/shard_map/ppermute | solution.py:523
  40.8 8.1 %collective-permute-start.18 = (f32[32,384]{1,0:T(8,128)S(1)}, f32[32,384]{1,0:T(8,128)S(1)}, u32[]{:S(2)}, u32[]{:S(2)}) collective-permute-start(f32[32,384]{1,0:T(8,128)S(1)} %get-tuple-element.95.refs_4_.refs_1_), channel_id=1, source_target_pairs={{384,448},{385,449},{386,450},{387,451},{388,452},{389,453},{390,4... | collective-permute-start | bytes 147464 | tf_op jit(solution)/shard_map/ppermute | solution.py:523
  42.2 11.0 %collective-permute-start.14 = (f32[32,384]{1,0:T(8,128)S(1)}, f32[32,384]{1,0:T(8,128)S(1)}, u32[]{:S(2)}, u32[]{:S(2)}) collective-permute-start(f32[32,384]{1,0:T(8,128)S(1)} %get-tuple-element.91.refs_4_.refs_0_), channel_id=1, source_target_pairs={{384,448},{385,449},{386,450},{387,451},{388,452},{389,453},{390,4... | collective-permute-start | bytes 147464 | tf_op jit(solution)/shard_map/ppermute | solution.py:523
  43.5 12.3 %collective-permute-start.20 = (f32[64,384]{1,0:T(8,128)S(1)}, f32[64,384]{1,0:T(8,128)S(1)}, u32[]{:S(2)}, u32[]{:S(2)}) collective-permute-start(f32[64,384]{1,0:T(8,128)S(1)} %gather5.1), channel_id=1, source_target_pairs={{385,450},{386,449},{387,452},{388,451},{389,454},{390,453},{391,4... | collective-permute-start | bytes 294920 | tf_op jit(solution)/shard_map/ppermute | solution.py:523
  53.2 3.2 %collective-permute-start.21 = (f32[64,384]{1,0:T(8,128)S(1)}, f32[64,384]{1,0:T(8,128)S(1)}, u32[]{:S(2)}, u32[]{:S(2)}) collective-permute-start(f32[64,384]{1,0:T(8,128)S(1)} %entered.1), channel_id=1, source_target_pairs={{0,1},{1,0},{2,3},{3,2},{4,5},{5,4},{6,7},{7,6},{8,9},{9,8},{10,11... | collective-permute-start | bytes 294920 | tf_op jit(solution)/shard_map/ppermute | solution.py:599

commit v6 on v4

--- a/solution.py
+++ b/solution.py
@@ -25,7 +25,7 @@
 LIMIT = 6 * MIB
 HOP_COST = 2e9
 LOW_COST = 2e9
-HOP_COSTS = (2e9, 2e9, 2e9, 2e9, 1e6, 1e6, 2e9)
+HOP_COSTS = (2e9, 4e9, 4e9, 2e9, 1e6, 1e6, 2e9)
 GATHER_COST = 2e9
 FULL_COST = 5e9
 
@@ -582,7 +582,7 @@
         arrived = [both(trace, step) for trace in traces]
         groups = (len(offs), len(ons))
         sides = [*offs, *ons]
-        if hop in (1, slabs - 2):
+        if hop in (2, slabs - 2):
             arrived = lax.optimization_barrier(arrived)
         from_off, from_on = [], []
         if hop >= first_far:
@@ -597,7 +597,7 @@
                 flops=GATHER_COST,
             )
             from_on = [lax.ppermute(entered, "tile", on)]
-        if hop == 1:
+        if hop == 2:
             again, _ = lax.optimization_barrier((src, traces))
             (low,) = call(
                 "pack_low",
@@ -606,8 +606,8 @@
                 [again],
                 flops=LOW_COST,
             )
-            low_on, low_off = lax.ppermute(low, "tile", on), lax.ppermute(low, "tile", off)
-        if hop == first_far - 1:
+            low_off, low_on = lax.ppermute(low, "tile", off), lax.ppermute(low, "tile", on)
+        if hop == first_far:
             lows, _ = lax.optimization_barrier(((low, low_on, low_off), traces))
             (solved,) = call(
                 "full",
@@ -623,7 +623,7 @@
         sums = []
         new_traces, new_helds = [None] * width, [None] * width
         for col in reversed(range(width)):
-            if hop == first_far - 1 and col < width - 1:
+            if hop == first_far and col < width - 1:
                 arrived[col], _ = lax.optimization_barrier((arrived[col], new_traces[-1]))
             counts = groups if col == width - 1 else (0, 0)
             new_traces[col], new_helds[col], *more = call(

time: 61.6 us -> 60.6 us (0.984)
  the two profiles are of different devices: /device:TPU:415 before, /device:TPU:471 now
where the time goes in v6:
time: 60.6 us; the launch traced here: 60.1 us
  starting transfers between devices  26.9 us (44%)
  waiting for transfers between devices  19.9 us (33%)
  Pallas kernels  9.5 us (16%)
  local copies, waits for them, and re-layouts  2.58 us (4%)
  between operations  1.12 us (2%)
    ppermute x17, starting transfers between devices, both(): return lax.ppermute(x, ('slab', 'tile'), moves)  13.3 us
    pallas_call x27, Pallas kernels, call(): pl.pallas_call(body, name=name, out_shape=[jax.ShapeDtypeStruct(shape, dt...  9.5 us
    ppermute x17, waiting for transfers between devices, both(): return lax.ppermute(x, ('slab', 'tile'), moves)  8.82 us
    ppermute x1, waiting for transfers between devices, per_device(): lax.ppermute(low, 'tile', off)  8.36 us
    ppermute x1, starting transfers between devices, per_device(): lax.ppermute(high, 'tile', off)  3.47 us
    ppermute x1, starting transfers between devices, per_device(): lax.ppermute(low, 'tile', off)  3.47 us
    ppermute x1, starting transfers between devices, per_device(): from_on = [lax.ppermute(entered, 'tile', on)]  2.59 us
    unnamed x10, local copies, waits for them, and re-layouts  2.58 us
  transfers between devices with their start and end apart: 22, of which 5 were waited for; matrix products, arithmetic and copies ran while one was open for 0% of the time, Pallas kernels for 11%

profile of v6, /device:TPU:471, one launch (start us, length us, event | category | flops | bytes accessed | tf_op | source)
XLA Modules:
  0.0 60.1 jit_solution(16532452977267770964)
XLA Ops:
  0.6 1.3 %pack_high.1.own.high = f32[592,128]{1,0:T(8,128)S(1)} custom-call(f32[1536,128]{1,0:T(8,128)} %bitcast.10, s32[16,128]{1,0:T(8,128)} %bitcast.12), custom_call_target="tpu_custom_call" | custom-call | flops 500000000 | tf_op jit(solution)/shard_map/pack_high/pallas_call | solution.py:34
  2.0 3.5 %collective-permute-start = (f32[592,128]{1,0:T(8,128)S(1)}, f32[592,128]{1,0:T(8,128)S(1)}, u32[]{:S(2)}, u32[]{:S(2)}) collective-permute-start(f32[592,128]{1,0:T(8,128)S(1)} %pack_high.1.own.high), channel_id=1, source_target_pairs={{1,2},{2,1},{3,4},{4,3},{5,6},{6,5},{7,8},{8,7},{9,10},{10,9},{11,... | collective-permute-start | bytes 909320 | tf_op jit(solution)/shard_map/ppermute | solution.py:538
  5.4 2.2 %collective-permute-start.1 = (f32[592,128]{1,0:T(8,128)S(1)}, f32[592,128]{1,0:T(8,128)S(1)}, u32[]{:S(2)}, u32[]{:S(2)}) collective-permute-start(f32[592,128]{1,0:T(8,128)S(1)} %pack_high.1.own.high), channel_id=1, source_target_pairs={{0,1},{1,0},{2,3},{3,2},{4,5},{5,4},{6,7},{7,6},{8,9},{9,8},{10,11... | collective-permute-start | bytes 909320 | tf_op jit(solution)/shard_map/ppermute | solution.py:538
  7.7 1.7 %copy-done = f32[2,1,2,384,384]{4,3,2,1,0:T(8,128)S(1)} copy-done((f32[2,1,2,384,384]{4,3,2,1,0:T(8,128)S(1)}, f32[2,1,2,384,384]{4,3,2,1,0:T(8,128)}, u32[]{:S(2)}) %copy-start) | copy-done | bytes 2359320
  10.0 0.6 consts.1
  10.9 2.4 %collective-permute-done.off.high_off = f32[592,128]{1,0:T(8,128)S(1)} collective-permute-done((f32[592,128]{1,0:T(8,128)S(1)}, f32[592,128]{1,0:T(8,128)S(1)}, u32[]{:S(2)}, u32[]{:S(2)}) %collective-permute-start) | collective-permute-done | bytes 303136 | tf_op jit(solution)/shard_map/ppermute | solution.py:538
  13.4 0.7 %collective-permute-start.2 = (f32[32,384]{1,0:T(8,128)S(1)}, f32[32,384]{1,0:T(8,128)S(1)}, u32[]{:S(2)}, u32[]{:S(2)}) collective-permute-start(f32[32,384]{1,0:T(8,128)S(1)} %get-tuple-element.59.refs_4_), channel_id=1, source_target_pairs={{0,64},{1,65},{2,66},{3,67},{4,68},{5,69},{6,70},{7,71},{8,72},{9,... | collective-permute-start | bytes 147464 | tf_op jit(solution)/shard_map/ppermute | solution.py:523
  14.0 0.7 %collective-permute-start.5 = (f32[32,384]{1,0:T(8,128)S(1)}, f32[32,384]{1,0:T(8,128)S(1)}, u32[]{:S(2)}, u32[]{:S(2)}) collective-permute-start(f32[32,384]{1,0:T(8,128)S(1)} %get-tuple-element.65.refs_4_), channel_id=1, source_target_pairs={{0,64},{1,65},{2,66},{3,67},{4,68},{5,69},{6,70},{7,71},{8,72},{9,... | collective-permute-start | bytes 147464 | tf_op jit(solution)/shard_map/ppermute | solution.py:523
  14.7 0.7 %bottom.1 = (f32[32,384]{1,0:T(8,128)S(1)}, f32[32,384]{1,0:T(8,128)S(1)}, f32[528,128]{1,0:T(8,128)S(1)}) custom-call(f32[592,128]{1,0:T(8,128)S(1)} %pack_high.1.own.high, f32[592,128]{1,0:T(8,128)S(1)} %collective-permute-done.off.high_off, f32[592,128]{1,0:T(8,128)S(1)} %collective-permute-done.1.on.high_on, f32[32,128]{1,0:T(8,128)S(1)} %consts.1, ...), custom_call_target="tpu_custom_call" | custom-call | flops 2000000000 | tf_op jit(solution)/shard_map/bottom/pallas_call | solution.py:34
  15.4 0.7 %collective-permute-start.3 = (f32[32,384]{1,0:T(8,128)S(1)}, f32[32,384]{1,0:T(8,128)S(1)}, u32[]{:S(2)}, u32[]{:S(2)}) collective-permute-start(f32[32,384]{1,0:T(8,128)S(1)} %get-tuple-element.62.refs_4_), channel_id=1, source_target_pairs={{64,128},{65,129},{66,130},{67,131},{68,132},{69,133},{70,134},{71... | collective-permute-start | bytes 147464 | tf_op jit(solution)/shard_map/ppermute | solution.py:523
  16.1 0.7 %collective-permute-start.6 = (f32[32,384]{1,0:T(8,128)S(1)}, f32[32,384]{1,0:T(8,128)S(1)}, u32[]{:S(2)}, u32[]{:S(2)}) collective-permute-start(f32[32,384]{1,0:T(8,128)S(1)} %get-tuple-element.68.refs_4_), channel_id=1, source_target_pairs={{64,128},{65,129},{66,130},{67,131},{68,132},{69,133},{70,134},{71... | collective-permute-start | bytes 147464 | tf_op jit(solution)/shard_map/ppermute | solution.py:523
  16.9 0.7 %collective-permute-start.4 = (f32[32,384]{1,0:T(8,128)S(1)}, f32[32,384]{1,0:T(8,128)S(1)}, u32[]{:S(2)}, u32[]{:S(2)}) collective-permute-start(f32[32,384]{1,0:T(8,128)S(1)} %get-tuple-element.64.refs_4_), channel_id=1, source_target_pairs={{128,192},{129,193},{130,194},{131,195},{132,196},{133,197},{134,1... | collective-permute-start | bytes 147464 | tf_op jit(solution)/shard_map/ppermute | solution.py:523
  17.6 0.8 %collective-permute-start.7 = (f32[32,384]{1,0:T(8,128)S(1)}, f32[32,384]{1,0:T(8,128)S(1)}, u32[]{:S(2)}, u32[]{:S(2)}) collective-permute-start(f32[32,384]{1,0:T(8,128)S(1)} %get-tuple-element.70.refs_4_), channel_id=1, source_target_pairs={{128,192},{129,193},{130,194},{131,195},{132,196},{133,197},{134,1... | collective-permute-start | bytes 147464 | tf_op jit(solution)/shard_map/ppermute | solution.py:523
  19.0 1.9 %collective-permute-start.10 = (f32[960,128]{1,0:T(8,128)S(1)}, f32[960,128]{1,0:T(8,128)S(1)}, u32[]{:S(2)}, u32[]{:S(2)}) collective-permute-start(f32[960,128]{1,0:T(8,128)S(1)} %pack_low.1.low), channel_id=1, source_target_pairs={{0,1},{1,0},{2,3},{3,2},{4,5},{5,4},{6,7},{7,6},{8,9},{9,8},{10,11... | collective-permute-start | bytes 1474568 | tf_op jit(solution)/shard_map/ppermute | solution.py:609
  20.9 3.5 %collective-permute-start.11 = (f32[960,128]{1,0:T(8,128)S(1)}, f32[960,128]{1,0:T(8,128)S(1)}, u32[]{:S(2)}, u32[]{:S(2)}) collective-permute-start(f32[960,128]{1,0:T(8,128)S(1)} %pack_low.1.low), channel_id=1, source_target_pairs={{1,2},{2,1},{3,4},{4,3},{5,6},{6,5},{7,8},{8,7},{9,10},{10,9},{11,... | collective-permute-start | bytes 1474568 | tf_op jit(solution)/shard_map/ppermute | solution.py:609
  24.4 0.7 %collective-permute-start.8 = (f32[32,384]{1,0:T(8,128)S(1)}, f32[32,384]{1,0:T(8,128)S(1)}, u32[]{:S(2)}, u32[]{:S(2)}) collective-permute-start(f32[32,384]{1,0:T(8,128)S(1)} %get-tuple-element.73.refs_4_), channel_id=1, source_target_pairs={{192,256},{193,257},{194,258},{195,259},{196,260},{197,261},{198,2... | collective-permute-start | bytes 147464 | tf_op jit(solution)/shard_map/ppermute | solution.py:523
  25.1 0.7 %collective-permute-start.12 = (f32[32,384]{1,0:T(8,128)S(1)}, f32[32,384]{1,0:T(8,128)S(1)}, u32[]{:S(2)}, u32[]{:S(2)}) collective-permute-start(f32[32,384]{1,0:T(8,128)S(1)} %get-tuple-element.79.refs_4_), channel_id=1, source_target_pairs={{192,256},{193,257},{194,258},{195,259},{196,260},{197,261},{198,2... | collective-permute-start | bytes 147464 | tf_op jit(solution)/shard_map/ppermute | solution.py:523
  25.8 0.7 %collective-permute-start.9 = (f32[32,384]{1,0:T(8,128)S(1)}, f32[32,384]{1,0:T(8,128)S(1)}, u32[]{:S(2)}, u32[]{:S(2)}) collective-permute-start(f32[32,384]{1,0:T(8,128)S(1)} %get-tuple-element.75.refs_4_.refs_1_), channel_id=1, source_target_pairs={{256,320},{257,321},{258,322},{259,323},{260,324},{261,325},{262,3... | collective-permute-start | bytes 147464 | tf_op jit(solution)/shard_map/ppermute | solution.py:523
  26.6 0.7 %collective-permute-start.13 = (f32[32,384]{1,0:T(8,128)S(1)}, f32[32,384]{1,0:T(8,128)S(1)}, u32[]{:S(2)}, u32[]{:S(2)}) collective-permute-start(f32[32,384]{1,0:T(8,128)S(1)} %get-tuple-element.81.refs_4_.refs_0_), channel_id=1, source_target_pairs={{256,320},{257,321},{258,322},{259,323},{260,324},{261,325},{262,3... | collective-permute-start | bytes 147464 | tf_op jit(solution)/shard_map/ppermute | solution.py:523
  27.3 0.7 %collective-permute-start.17 = (f32[64,384]{1,0:T(8,128)S(1)}, f32[64,384]{1,0:T(8,128)S(1)}, u32[]{:S(2)}, u32[]{:S(2)}) collective-permute-start(f32[64,384]{1,0:T(8,128)S(1)} %gather3.1), channel_id=1, source_target_pairs={{257,322},{258,321},{259,324},{260,323},{261,326},{262,325},{263,3... | collective-permute-start | bytes 294920 | tf_op jit(solution)/shard_map/ppermute | solution.py:523
  27.9 8.4 %collective-permute-done.11.low_off = f32[960,128]{1,0:T(8,128)S(1)} collective-permute-done((f32[960,128]{1,0:T(8,128)S(1)}, f32[960,128]{1,0:T(8,128)S(1)}, u32[]{:S(2)}, u32[]{:S(2)}) %collective-permute-start.11) | collective-permute-done | bytes 491552 | tf_op jit(solution)/shard_map/ppermute | solution.py:609
  36.3 3.5 %full.1.base = f32[1536,128]{1,0:T(8,128)S(1)} custom-call(f32[528,128]{1,0:T(8,128)S(1)} %get-tuple-element.58.coeffs, f32[960,128]{1,0:T(8,128)S(1)} %pack_low.1.low, f32[960,128]{1,0:T(8,128)S(1)} %collective-permute-done.10.low_on, f32[960,128]{1,0:T(8,128)S(1)} %collective-permute-done.11.low_off, f32[592,128]{1,0:T(8,128)S(1)} %pack_high.1.own.high, ...), custom_call_target="tpu_custom_call" | custom-call | flops 5000000000 | tf_op jit(solution)/shard_map/full/pallas_call | solution.py:34
  39.9 0.7 %collective-permute-start.16 = (f32[32,384]{1,0:T(8,128)S(1)}, f32[32,384]{1,0:T(8,128)S(1)}, u32[]{:S(2)}, u32[]{:S(2)}) collective-permute-start(f32[32,384]{1,0:T(8,128)S(1)} %get-tuple-element.88.refs_4_.refs_1_), channel_id=1, source_target_pairs={{320,384},{321,385},{322,386},{323,387},{324,388},{325,389},{326,3... | collective-permute-start | bytes 147464 | tf_op jit(solution)/shard_map/ppermute | solution.py:523
  40.6 0.7 %collective-permute-start.14 = (f32[32,384]{1,0:T(8,128)S(1)}, f32[32,384]{1,0:T(8,128)S(1)}, u32[]{:S(2)}, u32[]{:S(2)}) collective-permute-start(f32[32,384]{1,0:T(8,128)S(1)} %get-tuple-element.91.refs_4_.refs_0_), channel_id=1, source_target_pairs={{320,384},{321,385},{322,386},{323,387},{324,388},{325,389},{326,3... | collective-permute-start | bytes 147464 | tf_op jit(solution)/shard_map/ppermute | solution.py:523
  41.3 0.7 %collective-permute-start.19 = (f32[64,384]{1,0:T(8,128)S(1)}, f32[64,384]{1,0:T(8,128)S(1)}, u32[]{:S(2)}, u32[]{:S(2)}) collective-permute-start(f32[64,384]{1,0:T(8,128)S(1)} %gather4.1), channel_id=1, source_target_pairs={{321,386},{322,385},{323,388},{324,387},{325,390},{326,389},{327,3... | collective-permute-start | bytes 294920 | tf_op jit(solution)/shard_map/ppermute | solution.py:523
  42.0 1.3 %collective-permute-start.15 = (f32[32,384]{1,0:T(8,128)S(1)}, f32[32,384]{1,0:T(8,128)S(1)}, u32[]{:S(2)}, u32[]{:S(2)}) collective-permute-start(f32[32,384]{1,0:T(8,128)S(1)} %get-tuple-element.93.refs_4_.refs_0_), channel_id=1, source_target_pairs={{384,448},{385,449},{386,450},{387,451},{388,452},{389,453},{390,4... | collective-permute-start | bytes 147464 | tf_op jit(solution)/shard_map/ppermute | solution.py:523
  43.4 1.3 %collective-permute-start.18 = (f32[32,384]{1,0:T(8,128)S(1)}, f32[32,384]{1,0:T(8,128)S(1)}, u32[]{:S(2)}, u32[]{:S(2)}) collective-permute-start(f32[32,384]{1,0:T(8,128)S(1)} %get-tuple-element.95.refs_4_.refs_1_), channel_id=1, source_target_pairs={{384,448},{385,449},{386,450},{387,451},{388,452},{389,453},{390,4... | collective-permute-start | bytes 147464 | tf_op jit(solution)/shard_map/ppermute | solution.py:523
  44.7 1.3 %collective-permute-start.20 = (f32[64,384]{1,0:T(8,128)S(1)}, f32[64,384]{1,0:T(8,128)S(1)}, u32[]{:S(2)}, u32[]{:S(2)}) collective-permute-start(f32[64,384]{1,0:T(8,128)S(1)} %gather5.1), channel_id=1, source_target_pairs={{385,450},{386,449},{387,452},{388,451},{389,454},{390,453},{391,4... | collective-permute-start | bytes 294920 | tf_op jit(solution)/shard_map/ppermute | solution.py:523
  46.0 5.4 %collective-permute-done.15.refs_0_ = f32[32,384]{1,0:T(8,128)S(1)} collective-permute-done((f32[32,384]{1,0:T(8,128)S(1)}, f32[32,384]{1,0:T(8,128)S(1)}, u32[]{:S(2)}, u32[]{:S(2)}) %collective-permute-start.15) | collective-permute-done | bytes 49184 | tf_op jit(solution)/shard_map/ppermute | solution.py:523
  51.4 3.4 %collective-permute-done.18.refs_0_.refs_1_ = f32[32,384]{1,0:T(8,128)S(1)} collective-permute-done((f32[32,384]{1,0:T(8,128)S(1)}, f32[32,384]{1,0:T(8,128)S(1)}, u32[]{:S(2)}, u32[]{:S(2)}) %collective-permute-start.18) | collective-permute-done | bytes 49184 | tf_op jit(solution)/shard_map/ppermute | solution.py:523
  54.8 2.6 %collective-permute-start.21 = (f32[64,384]{1,0:T(8,128)S(1)}, f32[64,384]{1,0:T(8,128)S(1)}, u32[]{:S(2)}, u32[]{:S(2)}) collective-permute-start(f32[64,384]{1,0:T(8,128)S(1)} %entered.1), channel_id=1, source_target_pairs={{0,1},{1,0},{2,3},{3,2},{4,5},{5,4},{6,7},{7,6},{8,9},{9,8},{10,11... | collective-permute-start | bytes 294920 | tf_op jit(solution)/shard_map/ppermute | solution.py:599
  58.3 1.7 %inject.1 = (f32[1536,128]{1,0:T(8,128)}, f32[64,384]{1,0:T(8,128)}) custom-call(f32[528,128]{1,0:T(8,128)S(1)} %get-tuple-element.58.coeffs, f32[1536,128]{1,0:T(8,128)S(1)} %full.1.base, f32[32,384]{1,0:T(8,128)S(1)} %get-tuple-element.98.refs_0_, f32[32,384]{1,0:T(8,128)S(1)} %get-tuple-element.102.refs_1_, f32[32,384]{1,0:T(8,128)S(1)} %get-tuple-element.103.refs_2_, ...), custom_call_target="tpu_custom_call" | custom-call | flops 500000000 | tf_op jit(solution)/shard_map/inject/pallas_call | solution.py:34
  (49 shorter events, 2.9 us)
Async XLA Ops:
  2.0 11.4 %collective-permute-start = (f32[592,128]{1,0:T(8,128)S(1)}, f32[592,128]{1,0:T(8,128)S(1)}, u32[]{:S(2)}, u32[]{:S(2)}) collective-permute-start(f32[592,128]{1,0:T(8,128)S(1)} %pack_high.1.own.high), channel_id=1, source_target_pairs={{1,2},{2,1},{3,4},{4,3},{5,6},{6,5},{7,8},{8,7},{9,10},{10,9},{11,... | collective-permute-start | bytes 909320 | tf_op jit(solution)/shard_map/ppermute | solution.py:538
  5.4 7.9 %collective-permute-start.1 = (f32[592,128]{1,0:T(8,128)S(1)}, f32[592,128]{1,0:T(8,128)S(1)}, u32[]{:S(2)}, u32[]{:S(2)}) collective-permute-start(f32[592,128]{1,0:T(8,128)S(1)} %pack_high.1.own.high), channel_id=1, source_target_pairs={{0,1},{1,0},{2,3},{3,2},{4,5},{5,4},{6,7},{7,6},{8,9},{9,8},{10,11... | collective-permute-start | bytes 909320 | tf_op jit(solution)/shard_map/ppermute | solution.py:538
  7.6 1.7 %copy-start = (f32[2,1,2,384,384]{4,3,2,1,0:T(8,128)S(1)}, f32[2,1,2,384,384]{4,3,2,1,0:T(8,128)}, u32[]{:S(2)}) copy-start(f32[2,1,2,384,384]{4,3,2,1,0:T(8,128)} %param.10) | copy-start | bytes 7077892
  9.3 0.7 %copy-start.3 = (f32[3,8]{1,0:T(4,128)S(1)}, f32[3,8]{1,0:T(4,128)}, u32[]{:S(2)}) copy-start(f32[3,8]{1,0:T(4,128)} %table.1) | copy-start | bytes 292
  9.3 0.7 %copy-start.4 = (s32[1,2]{1,0:T(1,128)S(1)}, s32[1,2]{1,0:T(1,128)}, u32[]{:S(2)}) copy-start(s32[1,2]{1,0:T(1,128)} %widths.1) | copy-start | bytes 28
  10.0 0.9 %copy-start.1 = (f32[2,2,16,384]{3,2,1,0:T(8,128)S(1)}, f32[2,2,16,384]{3,2,1,0:T(8,128)}, u32[]{:S(2)}) copy-start(f32[2,2,16,384]{3,2,1,0:T(8,128)} %param.11) | copy-start | bytes 294916
  13.4 2.0 %collective-permute-start.2 = (f32[32,384]{1,0:T(8,128)S(1)}, f32[32,384]{1,0:T(8,128)S(1)}, u32[]{:S(2)}, u32[]{:S(2)}) collective-permute-start(f32[32,384]{1,0:T(8,128)S(1)} %get-tuple-element.59.refs_4_), channel_id=1, source_target_pairs={{0,64},{1,65},{2,66},{3,67},{4,68},{5,69},{6,70},{7,71},{8,72},{9,... | collective-permute-start | bytes 147464 | tf_op jit(solution)/shard_map/ppermute | solution.py:523
  14.0 2.1 %collective-permute-start.5 = (f32[32,384]{1,0:T(8,128)S(1)}, f32[32,384]{1,0:T(8,128)S(1)}, u32[]{:S(2)}, u32[]{:S(2)}) collective-permute-start(f32[32,384]{1,0:T(8,128)S(1)} %get-tuple-element.65.refs_4_), channel_id=1, source_target_pairs={{0,64},{1,65},{2,66},{3,67},{4,68},{5,69},{6,70},{7,71},{8,72},{9,... | collective-permute-start | bytes 147464 | tf_op jit(solution)/shard_map/ppermute | solution.py:523
  15.4 1.4 %collective-permute-start.3 = (f32[32,384]{1,0:T(8,128)S(1)}, f32[32,384]{1,0:T(8,128)S(1)}, u32[]{:S(2)}, u32[]{:S(2)}) collective-permute-start(f32[32,384]{1,0:T(8,128)S(1)} %get-tuple-element.62.refs_4_), channel_id=1, source_target_pairs={{64,128},{65,129},{66,130},{67,131},{68,132},{69,133},{70,134},{71... | collective-permute-start | bytes 147464 | tf_op jit(solution)/shard_map/ppermute | solution.py:523
  16.1 1.4 %collective-permute-start.6 = (f32[32,384]{1,0:T(8,128)S(1)}, f32[32,384]{1,0:T(8,128)S(1)}, u32[]{:S(2)}, u32[]{:S(2)}) collective-permute-start(f32[32,384]{1,0:T(8,128)S(1)} %get-tuple-element.68.refs_4_), channel_id=1, source_target_pairs={{64,128},{65,129},{66,130},{67,131},{68,132},{69,133},{70,134},{71... | collective-permute-start | bytes 147464 | tf_op jit(solution)/shard_map/ppermute | solution.py:523
  16.9 7.5 %collective-permute-start.4 = (f32[32,384]{1,0:T(8,128)S(1)}, f32[32,384]{1,0:T(8,128)S(1)}, u32[]{:S(2)}, u32[]{:S(2)}) collective-permute-start(f32[32,384]{1,0:T(8,128)S(1)} %get-tuple-element.64.refs_4_), channel_id=1, source_target_pairs={{128,192},{129,193},{130,194},{131,195},{132,196},{133,197},{134,1... | collective-permute-start | bytes 147464 | tf_op jit(solution)/shard_map/ppermute | solution.py:523
  17.5 1.1 %copy-start.2 = (f32[16,2,3,2,8,128]{5,4,3,2,1,0:T(8,128)S(1)}, f32[16,2,3,2,8,128]{5,4,3,2,1,0:T(8,128)}, u32[]{:S(2)}) copy-start(f32[16,2,3,2,8,128]{5,4,3,2,1,0:T(8,128)} %param.6) | copy-start | bytes 2359300
  17.6 6.8 %collective-permute-start.7 = (f32[32,384]{1,0:T(8,128)S(1)}, f32[32,384]{1,0:T(8,128)S(1)}, u32[]{:S(2)}, u32[]{:S(2)}) collective-permute-start(f32[32,384]{1,0:T(8,128)S(1)} %get-tuple-element.70.refs_4_), channel_id=1, source_target_pairs={{128,192},{129,193},{130,194},{131,195},{132,196},{133,197},{134,1... | collective-permute-start | bytes 147464 | tf_op jit(solution)/shard_map/ppermute | solution.py:523
  19.0 9.0 %collective-permute-start.10 = (f32[960,128]{1,0:T(8,128)S(1)}, f32[960,128]{1,0:T(8,128)S(1)}, u32[]{:S(2)}, u32[]{:S(2)}) collective-permute-start(f32[960,128]{1,0:T(8,128)S(1)} %pack_low.1.low), channel_id=1, source_target_pairs={{0,1},{1,0},{2,3},{3,2},{4,5},{5,4},{6,7},{7,6},{8,9},{9,8},{10,11... | collective-permute-start | bytes 1474568 | tf_op jit(solution)/shard_map/ppermute | solution.py:609
  20.9 15.4 %collective-permute-start.11 = (f32[960,128]{1,0:T(8,128)S(1)}, f32[960,128]{1,0:T(8,128)S(1)}, u32[]{:S(2)}, u32[]{:S(2)}) collective-permute-start(f32[960,128]{1,0:T(8,128)S(1)} %pack_low.1.low), channel_id=1, source_target_pairs={{1,2},{2,1},{3,4},{4,3},{5,6},{6,5},{7,8},{8,7},{9,10},{10,9},{11,... | collective-permute-start | bytes 1474568 | tf_op jit(solution)/shard_map/ppermute | solution.py:609
  24.4 1.4 %collective-permute-start.8 = (f32[32,384]{1,0:T(8,128)S(1)}, f32[32,384]{1,0:T(8,128)S(1)}, u32[]{:S(2)}, u32[]{:S(2)}) collective-permute-start(f32[32,384]{1,0:T(8,128)S(1)} %get-tuple-element.73.refs_4_), channel_id=1, source_target_pairs={{192,256},{193,257},{194,258},{195,259},{196,260},{197,261},{198,2... | collective-permute-start | bytes 147464 | tf_op jit(solution)/shard_map/ppermute | solution.py:523
  25.1 1.4 %collective-permute-start.12 = (f32[32,384]{1,0:T(8,128)S(1)}, f32[32,384]{1,0:T(8,128)S(1)}, u32[]{:S(2)}, u32[]{:S(2)}) collective-permute-start(f32[32,384]{1,0:T(8,128)S(1)} %get-tuple-element.79.refs_4_), channel_id=1, source_target_pairs={{192,256},{193,257},{194,258},{195,259},{196,260},{197,261},{198,2... | collective-permute-start | bytes 147464 | tf_op jit(solution)/shard_map/ppermute | solution.py:523
  25.8 14.0 %collective-permute-start.9 = (f32[32,384]{1,0:T(8,128)S(1)}, f32[32,384]{1,0:T(8,128)S(1)}, u32[]{:S(2)}, u32[]{:S(2)}) collective-permute-start(f32[32,384]{1,0:T(8,128)S(1)} %get-tuple-element.75.refs_4_.refs_1_), channel_id=1, source_target_pairs={{256,320},{257,321},{258,322},{259,323},{260,324},{261,325},{262,3... | collective-permute-start | bytes 147464 | tf_op jit(solution)/shard_map/ppermute | solution.py:523
  26.6 14.0 %collective-permute-start.13 = (f32[32,384]{1,0:T(8,128)S(1)}, f32[32,384]{1,0:T(8,128)S(1)}, u32[]{:S(2)}, u32[]{:S(2)}) collective-permute-start(f32[32,384]{1,0:T(8,128)S(1)} %get-tuple-element.81.refs_4_.refs_0_), channel_id=1, source_target_pairs={{256,320},{257,321},{258,322},{259,323},{260,324},{261,325},{262,3... | collective-permute-start | bytes 147464 | tf_op jit(solution)/shard_map/ppermute | solution.py:523
  27.3 16.1 %collective-permute-start.17 = (f32[64,384]{1,0:T(8,128)S(1)}, f32[64,384]{1,0:T(8,128)S(1)}, u32[]{:S(2)}, u32[]{:S(2)}) collective-permute-start(f32[64,384]{1,0:T(8,128)S(1)} %gather3.1), channel_id=1, source_target_pairs={{257,322},{258,321},{259,324},{260,323},{261,326},{262,325},{263,3... | collective-permute-start | bytes 294920 | tf_op jit(solution)/shard_map/ppermute | solution.py:523
  39.9 3.4 %collective-permute-start.16 = (f32[32,384]{1,0:T(8,128)S(1)}, f32[32,384]{1,0:T(8,128)S(1)}, u32[]{:S(2)}, u32[]{:S(2)}) collective-permute-start(f32[32,384]{1,0:T(8,128)S(1)} %get-tuple-element.88.refs_4_.refs_1_), channel_id=1, source_target_pairs={{320,384},{321,385},{322,386},{323,387},{324,388},{325,389},{326,3... | collective-permute-start | bytes 147464 | tf_op jit(solution)/shard_map/ppermute | solution.py:523
  40.6 1.4 %collective-permute-start.14 = (f32[32,384]{1,0:T(8,128)S(1)}, f32[32,384]{1,0:T(8,128)S(1)}, u32[]{:S(2)}, u32[]{:S(2)}) collective-permute-start(f32[32,384]{1,0:T(8,128)S(1)} %get-tuple-element.91.refs_4_.refs_0_), channel_id=1, source_target_pairs={{320,384},{321,385},{322,386},{323,387},{324,388},{325,389},{326,3... | collective-permute-start | bytes 147464 | tf_op jit(solution)/shard_map/ppermute | solution.py:523
  41.3 16.4 %collective-permute-start.19 = (f32[64,384]{1,0:T(8,128)S(1)}, f32[64,384]{1,0:T(8,128)S(1)}, u32[]{:S(2)}, u32[]{:S(2)}) collective-permute-start(f32[64,384]{1,0:T(8,128)S(1)} %gather4.1), channel_id=1, source_target_pairs={{321,386},{322,385},{323,388},{324,387},{325,390},{326,389},{327,3... | collective-permute-start | bytes 294920 | tf_op jit(solution)/shard_map/ppermute | solution.py:523
  42.0 9.4 %collective-permute-start.15 = (f32[32,384]{1,0:T(8,128)S(1)}, f32[32,384]{1,0:T(8,128)S(1)}, u32[]{:S(2)}, u32[]{:S(2)}) collective-permute-start(f32[32,384]{1,0:T(8,128)S(1)} %get-tuple-element.93.refs_4_.refs_0_), channel_id=1, source_target_pairs={{384,448},{385,449},{386,450},{387,451},{388,452},{389,453},{390,4... | collective-permute-start | bytes 147464 | tf_op jit(solution)/shard_map/ppermute | solution.py:523
  43.4 11.4 %collective-permute-start.18 = (f32[32,384]{1,0:T(8,128)S(1)}, f32[32,384]{1,0:T(8,128)S(1)}, u32[]{:S(2)}, u32[]{:S(2)}) collective-permute-start(f32[32,384]{1,0:T(8,128)S(1)} %get-tuple-element.95.refs_4_.refs_1_), channel_id=1, source_target_pairs={{384,448},{385,449},{386,450},{387,451},{388,452},{389,453},{390,4... | collective-permute-start | bytes 147464 | tf_op jit(solution)/shard_map/ppermute | solution.py:523
  44.7 13.3 %collective-permute-start.20 = (f32[64,384]{1,0:T(8,128)S(1)}, f32[64,384]{1,0:T(8,128)S(1)}, u32[]{:S(2)}, u32[]{:S(2)}) collective-permute-start(f32[64,384]{1,0:T(8,128)S(1)} %gather5.1), channel_id=1, source_target_pairs={{385,450},{386,449},{387,452},{388,451},{389,454},{390,453},{391,4... | collective-permute-start | bytes 294920 | tf_op jit(solution)/shard_map/ppermute | solution.py:523
  54.8 3.5 %collective-permute-start.21 = (f32[64,384]{1,0:T(8,128)S(1)}, f32[64,384]{1,0:T(8,128)S(1)}, u32[]{:S(2)}, u32[]{:S(2)}) collective-permute-start(f32[64,384]{1,0:T(8,128)S(1)} %entered.1), channel_id=1, source_target_pairs={{0,1},{1,0},{2,3},{3,2},{4,5},{5,4},{6,7},{7,6},{8,9},{9,8},{10,11... | collective-permute-start | bytes 294920 | tf_op jit(solution)/shard_map/ppermute | solution.py:599
